TPU v7x, 128 devices: a whole 4x4x4 slice. The times are simulated.
128 devices in a mesh: replica: 4 (over x_lo, core), shard: 32 (over z, y, x_hi).
Axes of the slice: x: 4 (x_hi: 2, x_lo: 2; x = x_hi * 2 + x_lo), y: 4, z: 4, core: 2. Of those that a mesh axis runs over, the one named last changes fastest.
Arguments:
- hidden_in: bfloat16 [4, 3, 2048, 1536], P('replica', None, 'shard'), may hold values from -6 to 6
- doc_ids: int32 [4, 3, 2048], P('replica', None, 'shard'), may hold values from 0 to 7, as said below
- out_grad: bfloat16 [4, 3, 2048, 1536], P('replica', None, 'shard'), may hold values from -6 to 6
- norm_attn: bfloat16 [1536], P('shard'), may hold values from 0.5 to 1.5
- w_query: bfloat16 [1536, 1536], P('shard'), may hold values from -0.15625 to 0.15625
- w_key: bfloat16 [1536, 512], P('shard'), may hold values from -0.15625 to 0.15625
- w_value: bfloat16 [1536, 512], P('shard'), may hold values from -0.15625 to 0.15625
- w_out: bfloat16 [1536, 1536], P('shard'), may hold values from -6 to 6
- norm_ffn: bfloat16 [1536], P('shard'), may hold values from 0.5 to 1.5
- w_gate: bfloat16 [1536, 3840], P('shard'), may hold values from -0.15625 to 0.15625
- w_up: bfloat16 [1536, 3840], P('shard'), may hold values from -0.15625 to 0.15625
- w_down: bfloat16 [3840, 1536], P('shard'), may hold values from -0.5 to 0.5
Outputs:
- output: bfloat16 [4, 3, 2048, 1536], P('replica', None, 'shard')
- grad_in: bfloat16 [4, 3, 2048, 1536], P('replica', None, 'shard')
- grad_norm_attn: float32 [1536], P('shard')
- grad_query: float32 [1536, 1536], P('shard')
- grad_key: float32 [1536, 512], P('shard')
- grad_value: float32 [1536, 512], P('shard')
- grad_out: float32 [1536, 1536], P('shard')
- grad_norm_ffn: float32 [1536], P('shard')
- grad_gate: float32 [1536, 3840], P('shard')
- grad_up: float32 [1536, 3840], P('shard')
- grad_down: float32 [3840, 1536], P('shard')
Inputs may be any that keep to these rules, and one draw needn't show every extreme that they name: `doc_ids`: within each sequence the document numbers start at 0 and never fall; a sequence holds at most 8 documents; in each replica group one of its 3 sequences is a single document.
All inputs are finite; a program needn't handle non-finite values.
Results may differ from a plain program's by a relative error of at most 0.028.
Values may be sent and summed in bfloat16 or wider, within the bound.
No kernel may reach another device: no remote copies, remote signals or barrier semaphores. Data moves between devices by JAX's collectives and lax.ppermute only.
A program may use at most 320 MiB of HBM per device.

v0:
```python
from functools import partial
import math

import jax
import jax.numpy as jnp
from jax import lax
from jax.sharding import PartitionSpec as P

HEADS = 24
KVH = 8
HD = 64


branch_scale = 1.4 / math.sqrt(52.0)
eps_norm = 1e-05


def product(left, right):
    return jnp.dot(left, right, preferred_element_type=jnp.float32)


def angle_tables(places):
    half_size = HD // 2
    inverse = jnp.exp(-jnp.arange(half_size, dtype=jnp.float32) * (math.log(10000.0) / half_size))
    angles = places.astype(jnp.float32)[:, None] * inverse[None, :]
    return (jnp.cos(angles)[:, None, :], jnp.sin(angles)[:, None, :])


def rotate(values, cosine, sine, sign):
    row_count = values.shape[0]
    split_heads = values.reshape(row_count, -1, HD)
    half_size = HD // 2
    front_half = split_heads[..., :half_size]
    back_half = split_heads[..., half_size:]
    turned_sine = sine * sign
    turned = jnp.concatenate(
        [
            front_half * cosine - back_half * turned_sine,
            back_half * cosine + front_half * turned_sine,
        ],
        axis=-1,
    )
    return turned.reshape(row_count, -1)


def attend_fwd(pieces, allowed):
    q_part, k_part, v_part = pieces
    scores = jnp.einsum("gcd,kd->gck", q_part, k_part, preferred_element_type=jnp.float32) * 0.125
    scores = jnp.where(allowed[None], scores, -1e30)
    highest = jnp.max(scores, axis=-1, keepdims=True)
    expo = jnp.exp(scores - highest)
    total = jnp.sum(expo, axis=-1, keepdims=True)
    probs = (expo / total).astype(jnp.bfloat16)
    mixed = jnp.einsum("gck,kd->gcd", probs, v_part, preferred_element_type=jnp.float32)
    return (mixed, highest + jnp.log(total))


def attend_bwd(pieces, allowed):
    q_part, k_part, v_part, log_total, d_part = pieces
    scores = jnp.einsum("gcd,kd->gck", q_part, k_part, preferred_element_type=jnp.float32) * 0.125
    scores = jnp.where(allowed[None], scores, -1e30)
    probs = jnp.exp(scores - log_total)
    d_probs = jnp.einsum("gcd,kd->gck", d_part, v_part, preferred_element_type=jnp.float32)
    offset = jnp.sum(d_probs * probs, axis=-1, keepdims=True)
    d_scores = (probs * (d_probs - offset)).astype(jnp.bfloat16)
    d_query = (
        jnp.einsum("gck,kd->gcd", d_scores, k_part, preferred_element_type=jnp.float32) * 0.125
    )
    d_key = jnp.einsum("gck,gcd->kd", d_scores, q_part, preferred_element_type=jnp.float32) * 0.125
    d_value = jnp.einsum(
        "gck,gcd->kd", probs.astype(jnp.bfloat16), d_part, preferred_element_type=jnp.float32
    )
    return (d_query, d_key, d_value)


def forward_pass(resid_low, documents, weights, cosine, sine, places, key_places):
    gain_attn, w_query, w_key, w_value, w_out, gain_ffn, w_gate, w_up, w_down = weights
    resid = resid_low.astype(jnp.float32)
    span = resid.shape[0]
    groups = HEADS // KVH
    scale_one = lax.rsqrt(jnp.mean(resid * resid, axis=-1, keepdims=True) + eps_norm)
    normed = (resid * scale_one * gain_attn.astype(jnp.float32)).astype(jnp.bfloat16)
    queries = rotate(product(normed, w_query), cosine, sine, 1.0).astype(jnp.bfloat16)
    keys_local = rotate(product(normed, w_key), cosine, sine, 1.0).astype(jnp.bfloat16)
    values_local = product(normed, w_value).astype(jnp.bfloat16)
    keys_all, values_all, docs_all = (
        lax.all_gather(keys_local, "shard", axis=0, tiled=True),
        lax.all_gather(values_local, "shard", axis=0, tiled=True),
        lax.all_gather(documents.astype(jnp.bfloat16), "shard", axis=0, tiled=True),
    )
    length = keys_all.shape[0]
    allowed = (documents.astype(jnp.float32)[:, None] == docs_all.astype(jnp.float32)[None, :]) & (
        key_places[None, :] <= places[:, None]
    )
    q_heads = queries.reshape(span, KVH, groups, HD).transpose(1, 2, 0, 3)
    k_heads = keys_all.reshape(length, KVH, HD).transpose(1, 0, 2)
    v_heads = values_all.reshape(length, KVH, HD).transpose(1, 0, 2)
    mixed, log_total = lax.map(partial(attend_fwd, allowed=allowed), (q_heads, k_heads, v_heads))
    attn = mixed.transpose(2, 0, 1, 3).reshape(span, HEADS * HD).astype(jnp.bfloat16)
    middle = resid + branch_scale * product(attn, w_out)
    scale_two = lax.rsqrt(jnp.mean(middle * middle, axis=-1, keepdims=True) + eps_norm)
    normed_two = (middle * scale_two * gain_ffn.astype(jnp.float32)).astype(jnp.bfloat16)
    gate_pre = product(normed_two, w_gate)
    up_pre = product(normed_two, w_up)
    hidden_act = (jax.nn.silu(gate_pre) * up_pre).astype(jnp.bfloat16)
    result = (middle + branch_scale * product(hidden_act, w_down)).astype(jnp.bfloat16)
    record = (
        resid,
        scale_one,
        normed,
        allowed,
        q_heads,
        k_heads,
        v_heads,
        log_total,
        attn,
        middle,
        scale_two,
        normed_two,
        gate_pre,
        up_pre,
        hidden_act,
    )
    return (record, result)


def backward_pass(record, cot_low, weights, cosine, sine):
    gain_attn, w_query, w_key, w_value, w_out, gain_ffn, w_gate, w_up, w_down = weights
    (
        resid,
        scale_one,
        normed,
        allowed,
        q_heads,
        k_heads,
        v_heads,
        log_total,
        attn,
        middle,
        scale_two,
        normed_two,
        gate_pre,
        up_pre,
        hidden_act,
    ) = record
    span = resid.shape[0]
    length = k_heads.shape[1]
    groups = HEADS // KVH
    d_out = cot_low.astype(jnp.float32)
    d_branch = (branch_scale * d_out).astype(jnp.bfloat16)
    grad_down = product(hidden_act.T, d_branch)
    d_hidden = product(d_branch, w_down.T)
    sigmoid_gate = jax.nn.sigmoid(gate_pre)
    silu_gate = gate_pre * sigmoid_gate
    d_gate = (d_hidden * up_pre * sigmoid_gate * (1.0 + gate_pre * (1.0 - sigmoid_gate))).astype(
        jnp.bfloat16
    )
    d_up = (d_hidden * silu_gate).astype(jnp.bfloat16)
    d_norm_two = product(d_gate, w_gate.T) + product(d_up, w_up.T)
    grad_gate = product(normed_two.T, d_gate)
    grad_up = product(normed_two.T, d_up)
    unit_two = middle * scale_two
    d_unit_two = d_norm_two * gain_ffn.astype(jnp.float32)
    grad_gain_ffn = jnp.sum(d_norm_two * unit_two, axis=0)
    d_middle = d_out + scale_two * (
        d_unit_two - unit_two * jnp.mean(d_unit_two * unit_two, axis=-1, keepdims=True)
    )
    d_attn_branch = (branch_scale * d_middle).astype(jnp.bfloat16)
    grad_out = product(attn.T, d_attn_branch)
    d_attn = product(d_attn_branch, w_out.T).astype(jnp.bfloat16)
    d_heads = d_attn.reshape(span, KVH, groups, HD).transpose(1, 2, 0, 3)
    d_query, d_key, d_value = lax.map(
        partial(attend_bwd, allowed=allowed), (q_heads, k_heads, v_heads, log_total, d_heads)
    )
    d_query_rows = d_query.transpose(2, 0, 1, 3).reshape(span, HEADS * HD)
    d_key_rows = d_key.transpose(1, 0, 2).reshape(length, KVH * HD)
    d_value_rows = d_value.transpose(1, 0, 2).reshape(length, KVH * HD)
    d_key_local, d_value_local = (
        lax.psum_scatter(
            d_key_rows.astype(jnp.bfloat16), "shard", scatter_dimension=0, tiled=True
        ).astype(jnp.float32),
        lax.psum_scatter(
            d_value_rows.astype(jnp.bfloat16), "shard", scatter_dimension=0, tiled=True
        ).astype(jnp.float32),
    )
    d_query_pre = rotate(d_query_rows, cosine, sine, -1.0).astype(jnp.bfloat16)
    d_key_pre = rotate(d_key_local, cosine, sine, -1.0).astype(jnp.bfloat16)
    d_value_pre = d_value_local.astype(jnp.bfloat16)
    d_normed = (
        product(d_query_pre, w_query.T)
        + product(d_key_pre, w_key.T)
        + product(d_value_pre, w_value.T)
    )
    grad_query = product(normed.T, d_query_pre)
    grad_key = product(normed.T, d_key_pre)
    grad_value = product(normed.T, d_value_pre)
    unit_one = resid * scale_one
    d_unit_one = d_normed * gain_attn.astype(jnp.float32)
    grad_gain_attn = jnp.sum(d_normed * unit_one, axis=0)
    grad_resid = d_middle + scale_one * (
        d_unit_one - unit_one * jnp.mean(d_unit_one * unit_one, axis=-1, keepdims=True)
    )
    terms = (
        grad_gain_attn,
        grad_query,
        grad_key,
        grad_value,
        grad_out,
        grad_gain_ffn,
        grad_gate,
        grad_up,
        grad_down,
    )
    return (terms, grad_resid.astype(jnp.bfloat16))


def on_device(
    hidden_in,
    doc_ids,
    out_grad,
    norm_attn,
    w_query,
    w_key,
    w_value,
    w_out,
    norm_ffn,
    w_gate,
    w_up,
    w_down,
):
    weights = (
        lax.all_gather(norm_attn, "shard", axis=0, tiled=True),
        lax.all_gather(w_query, "shard", axis=0, tiled=True),
        lax.all_gather(w_key, "shard", axis=0, tiled=True),
        lax.all_gather(w_value, "shard", axis=0, tiled=True),
        lax.all_gather(w_out, "shard", axis=0, tiled=True),
        lax.all_gather(norm_ffn, "shard", axis=0, tiled=True),
        lax.all_gather(w_gate, "shard", axis=0, tiled=True),
        lax.all_gather(w_up, "shard", axis=0, tiled=True),
        lax.all_gather(w_down, "shard", axis=0, tiled=True),
    )
    span = hidden_in.shape[2]
    shards = lax.axis_size("shard")
    length = span * shards
    places = lax.axis_index("shard") * span + jnp.arange(span, dtype=jnp.int32)
    key_places = jnp.arange(length, dtype=jnp.int32)
    cosine, sine = angle_tables(places)
    micro_count = hidden_in.shape[1]
    records = []
    results = []
    for micro in range(micro_count):
        record, result = forward_pass(
            hidden_in[0, micro], doc_ids[0, micro], weights, cosine, sine, places, key_places
        )
        records.append(record)
        results.append(result)
    back_weights = (
        lax.all_gather(norm_attn, "shard", axis=0, tiled=True),
        lax.all_gather(w_query, "shard", axis=0, tiled=True),
        lax.all_gather(w_key, "shard", axis=0, tiled=True),
        lax.all_gather(w_value, "shard", axis=0, tiled=True),
        lax.all_gather(w_out, "shard", axis=0, tiled=True),
        lax.all_gather(norm_ffn, "shard", axis=0, tiled=True),
        lax.all_gather(w_gate, "shard", axis=0, tiled=True),
        lax.all_gather(w_up, "shard", axis=0, tiled=True),
        lax.all_gather(w_down, "shard", axis=0, tiled=True),
    )
    totals = None
    grad_rows = []
    for micro in range(micro_count):
        terms, grad_resid = backward_pass(
            records[micro], out_grad[0, micro], back_weights, cosine, sine
        )
        grad_rows.append(grad_resid)
        if micro == 0:
            totals = terms
        else:
            totals = tuple((acc + term for acc, term in zip(totals, terms)))
    owned = (
        lax.psum_scatter(
            totals[0].astype(jnp.bfloat16), "shard", scatter_dimension=0, tiled=True
        ).astype(jnp.float32),
        lax.psum_scatter(
            totals[1].astype(jnp.bfloat16), "shard", scatter_dimension=0, tiled=True
        ).astype(jnp.float32),
        lax.psum_scatter(
            totals[2].astype(jnp.bfloat16), "shard", scatter_dimension=0, tiled=True
        ).astype(jnp.float32),
        lax.psum_scatter(
            totals[3].astype(jnp.bfloat16), "shard", scatter_dimension=0, tiled=True
        ).astype(jnp.float32),
        lax.psum_scatter(
            totals[4].astype(jnp.bfloat16), "shard", scatter_dimension=0, tiled=True
        ).astype(jnp.float32),
        lax.psum_scatter(
            totals[5].astype(jnp.bfloat16), "shard", scatter_dimension=0, tiled=True
        ).astype(jnp.float32),
        lax.psum_scatter(
            totals[6].astype(jnp.bfloat16), "shard", scatter_dimension=0, tiled=True
        ).astype(jnp.float32),
        lax.psum_scatter(
            totals[7].astype(jnp.bfloat16), "shard", scatter_dimension=0, tiled=True
        ).astype(jnp.float32),
        lax.psum_scatter(
            totals[8].astype(jnp.bfloat16), "shard", scatter_dimension=0, tiled=True
        ).astype(jnp.float32),
    )
    summed = (
        lax.psum(owned[0].astype(jnp.bfloat16), "replica").astype(jnp.float32),
        lax.psum(owned[1].astype(jnp.bfloat16), "replica").astype(jnp.float32),
        lax.psum(owned[2].astype(jnp.bfloat16), "replica").astype(jnp.float32),
        lax.psum(owned[3].astype(jnp.bfloat16), "replica").astype(jnp.float32),
        lax.psum(owned[4].astype(jnp.bfloat16), "replica").astype(jnp.float32),
        lax.psum(owned[5].astype(jnp.bfloat16), "replica").astype(jnp.float32),
        lax.psum(owned[6].astype(jnp.bfloat16), "replica").astype(jnp.float32),
        lax.psum(owned[7].astype(jnp.bfloat16), "replica").astype(jnp.float32),
        lax.psum(owned[8].astype(jnp.bfloat16), "replica").astype(jnp.float32),
    )
    output = jnp.stack(results)[None]
    grad_in = jnp.stack(grad_rows)[None]
    return (
        output,
        grad_in,
        summed[0],
        summed[1],
        summed[2],
        summed[3],
        summed[4],
        summed[5],
        summed[6],
        summed[7],
        summed[8],
    )


def solution(mesh):
    placed = (
        P("replica", None, "shard", None),
        P("replica", None, "shard"),
        P("replica", None, "shard", None),
        P("shard"),
        P("shard", None),
        P("shard", None),
        P("shard", None),
        P("shard", None),
        P("shard"),
        P("shard", None),
        P("shard", None),
        P("shard", None),
    )
    return jax.shard_map(
        on_device,
        mesh=mesh,
        in_specs=placed,
        out_specs=(
            P("replica", None, "shard", None),
            P("replica", None, "shard", None),
            P("shard"),
            P("shard", None),
            P("shard", None),
            P("shard", None),
            P("shard", None),
            P("shard"),
            P("shard", None),
            P("shard", None),
            P("shard", None),
        ),
        check_vma=False,
    )
```

profile of v0, /device:TPU:49, one launch (start us, length us, event | category | flops | bytes accessed | tf_op | source)
XLA Modules:
  0.0 4225.2 jit_solution(2277071362777677466)
XLA Ops:
  14.4 135.0 %all-reduce.8 = (bf16[1536]{0:T(1024)(128)(2,1)S(1)}, bf16[2048]{0:T(1024)(128)(2,1)S(1)}, bf16[1536]{0:T(1024)(128)(2,1)S(1)}, bf16[2048]{0:T(1024)(128)(2,1)S(1)}, bf16[2048]{0:T(1024)(128)(2,1)S(1)}) all-reduce(bf16[1536]{0:T(1024)(128)(2,1)S(1)} %dynamic-update-slice.1, ...), channel_id=1, replica_groups=mesh['replica'=4,'shard'=32] {'shard'}, use_global_device_ids=true, to_apply=%add.1 | all-reduce | flops 9216 | bytes 36864
  166.7 101.5 %all-gather.39.cloned.1.call-done = bf16[2048,512]{1,0:T(8,128)(2,1)} async-done(((bf16[64,512]{1,0:T(8,128)(2,1)}), bf16[2048,512]{1,0:T(8,128)(2,1)}) %all-gather.39.cloned.1.call-update) | async-done | bytes 2097168 | tf_op jit(solution)/shard_map/all_gather | solution.py:87
  272.2 68.5 %all-gather.41.cloned.1.call-done = bf16[2048,512]{1,0:T(8,128)(2,1)} async-done(((bf16[64,512]{1,0:T(8,128)(2,1)}), bf16[2048,512]{1,0:T(8,128)(2,1)}) %all-gather.41.cloned.1.call-update) | async-done | bytes 2097168 | tf_op jit(solution)/shard_map/all_gather | solution.py:88
  344.6 68.5 %all-gather.21.cloned.1.call-done = bf16[2048,512]{1,0:T(8,128)(2,1)} async-done(((bf16[64,512]{1,0:T(8,128)(2,1)}), bf16[2048,512]{1,0:T(8,128)(2,1)}) %all-gather.21.cloned.1.call-update) | async-done | bytes 2097168 | tf_op jit(solution)/shard_map/all_gather | solution.py:87
  417.1 68.5 %all-gather.25.cloned.1.call-done = bf16[2048,512]{1,0:T(8,128)(2,1)} async-done(((bf16[64,512]{1,0:T(8,128)(2,1)}), bf16[2048,512]{1,0:T(8,128)(2,1)}) %all-gather.25.cloned.1.call-update) | async-done | bytes 2097168 | tf_op jit(solution)/shard_map/all_gather | solution.py:88
  489.6 68.7 %all-gather.35.cloned.1.call-done = bf16[2048,512]{1,0:T(8,128)(2,1)} async-done(((bf16[64,512]{1,0:T(8,128)(2,1)}), bf16[2048,512]{1,0:T(8,128)(2,1)}) %all-gather.35.cloned.1.call-update) | async-done | bytes 2097168 | tf_op jit(solution)/shard_map/all_gather | solution.py:87
  562.2 68.7 %all-gather.37.cloned.1.call-done = bf16[2048,512]{1,0:T(8,128)(2,1)} async-done(((bf16[64,512]{1,0:T(8,128)(2,1)}), bf16[2048,512]{1,0:T(8,128)(2,1)}) %all-gather.37.cloned.1.call-update) | async-done | bytes 2097168 | tf_op jit(solution)/shard_map/all_gather | solution.py:88
  634.9 82.4 %all-gather.17.cloned.1.call-done = bf16[1536,1536]{1,0:T(8,128)(2,1)} async-done(((bf16[48,1536]{1,0:T(8,128)(2,1)}), bf16[1536,1536]{1,0:T(8,128)(2,1)}) %all-gather.17.cloned.1.call-update) | async-done | bytes 4718608 | tf_op jit(solution)/shard_map/all_gather | solution.py:233
  732.3 27.8 while.86
  763.2 27.8 while.84
  792.8 28.2 while.85
  828.9 100.3 %all-gather.29.cloned.1.call-done = bf16[1536,3840]{1,0:T(8,128)(2,1)} async-done(((bf16[48,3840]{1,0:T(8,128)(2,1)}), bf16[1536,3840]{1,0:T(8,128)(2,1)}) %all-gather.29.cloned.1.call-update) | async-done | bytes 11796496 | tf_op jit(solution)/shard_map/all_gather | solution.py:238
  936.6 118.8 %all-gather.31.cloned.1.call-done = bf16[1536,3840]{1,0:T(8,128)(2,1)} async-done(((bf16[48,3840]{1,0:T(8,128)(2,1)}), bf16[1536,3840]{1,0:T(8,128)(2,1)}) %all-gather.31.cloned.1.call-update) | async-done | bytes 11796496 | tf_op jit(solution)/shard_map/all_gather | solution.py:239
  1062.8 118.9 %all-gather.33.cloned.1.call-done = bf16[3840,1536]{1,0:T(8,128)(2,1)} async-done(((bf16[120,1536]{1,0:T(8,128)(2,1)}), bf16[3840,1536]{1,0:T(8,128)(2,1)}) %all-gather.33.cloned.1.call-update) | async-done | bytes 11796496 | tf_op jit(solution)/shard_map/all_gather | solution.py:240
  1278.6 58.9 %while.87 = (s32[]{:T(128)}, f32[8,3,64,64]{3,2,1,0:T(8,128)}, bf16[8,2048,64]{1,2,0:T(8,128)(2,1)S(1)}, bf16[8,2048,64]{1,2,0:T(8,128)(2,1)}, bf16[8,3,64,64]{3...) while((s32[]{:T(128)}, f32[8,3,64,64]{3,2,1,0:T(8,128)}, ...), condition=%wide.region_21.22_spmd.clone, body=%wide.region_19.21_spmd.clone.sunk | while | flops 255733568 | bytes 14206345 | solution.py:172
  1348.2 66.0 %while.88 = (s32[]{:T(128)}, f32[8,3,64,64]{3,2,1,0:T(8,128)}, bf16[8,2048,64]{1,2,0:T(8,128)(2,1)S(1)}, bf16[8,2048,64]{1,2,0:T(8,128)(2,1)}, bf16[8,3,64,64]{3...) while((s32[]{:T(128)}, f32[8,3,64,64]{3,2,1,0:T(8,128)}, ...), condition=%wide.region_28.29_spmd.clone, body=%wide.region_26.28_spmd.clone.sunk | while | flops 255733568 | bytes 14206345 | solution.py:172
  1426.8 71.1 %while.89 = (s32[]{:T(128)}, f32[8,3,64,64]{3,2,1,0:T(8,128)}, bf16[8,2048,64]{1,2,0:T(8,128)(2,1)S(1)}, bf16[8,2048,64]{1,2,0:T(8,128)(2,1)}, bf16[8,3,64,64]{3...) while((s32[]{:T(128)}, f32[8,3,64,64]{3,2,1,0:T(8,128)}, ...), condition=%wide.region_35.36_spmd.clone, body=%wide.region_33.35_spmd.clone.sunk | while | flops 255733568 | bytes 14206345 | solution.py:172
  1513.8 159.5 %reduce-scatter.44.cloned.1.call-done = bf16[64,512]{1,0:T(8,128)(2,1)} async-done(((bf16[2048,512]{1,0:T(8,128)(2,1)}), bf16[64,512]{1,0:T(8,128)(2,1)}) %reduce-scatter.44.cloned.1.call-update) | async-done | bytes 65552
  1674.3 184.2 %reduce-scatter.48.cloned.1.call-done = bf16[64,512]{1,0:T(8,128)(2,1)} async-done(((bf16[2048,512]{1,0:T(8,128)(2,1)}), bf16[64,512]{1,0:T(8,128)(2,1)}) %reduce-scatter.48.cloned.1.call-update) | async-done | bytes 65552
  1863.1 181.3 %reduce-scatter.42.cloned.1.call-done = bf16[64,512]{1,0:T(8,128)(2,1)} async-done(((bf16[2048,512]{1,0:T(8,128)(2,1)}), bf16[64,512]{1,0:T(8,128)(2,1)}) %reduce-scatter.42.cloned.1.call-update) | async-done | bytes 65552
  2047.6 182.6 %reduce-scatter.46.cloned.1.call-done = bf16[64,512]{1,0:T(8,128)(2,1)} async-done(((bf16[2048,512]{1,0:T(8,128)(2,1)}), bf16[64,512]{1,0:T(8,128)(2,1)}) %reduce-scatter.46.cloned.1.call-update) | async-done | bytes 65552
  2234.5 181.5 %reduce-scatter.50.cloned.1.call-done = bf16[64,512]{1,0:T(8,128)(2,1)} async-done(((bf16[2048,512]{1,0:T(8,128)(2,1)}), bf16[64,512]{1,0:T(8,128)(2,1)}) %reduce-scatter.50.cloned.1.call-update) | async-done | bytes 65552
  2504.1 21.1 add_convert_fusion.1
  2597.8 78.4 %all-reduce.7 = (bf16[1536]{0:T(1024)(128)(2,1)}, bf16[1536]{0:T(1024)(128)(2,1)}) all-reduce(bf16[1536]{0:T(1024)(128)(2,1)} %add_convert_fusion.10, bf16[1536]{0:T(1024)(128)(2,1)} %add_convert_fusion.9), channel_id=11, replica_groups=mesh['replica'=4,'shard'=32] {'shard'}, use_global_device_ids=true, to_apply=%region_42.43.clone | all-reduce | flops 3072 | bytes 12288
  2679.5 224.2 %reduce-scatter.30.cloned.1.call-done = bf16[48,512]{1,0:T(8,128)(2,1)} async-done(((bf16[1536,512]{1,0:T(8,128)(2,1)}), bf16[48,512]{1,0:T(8,128)(2,1)}) %reduce-scatter.30.cloned.1.call-update) | async-done | bytes 49168 | tf_op jit(solution)/shard_map/reduce_scatter | solution.py:289
  2904.6 230.0 %reduce-scatter.26.cloned.1.call-done = bf16[48,1536]{1,0:T(8,128)(2,1)} async-done(((bf16[1536,1536]{1,0:T(8,128)(2,1)}), bf16[48,1536]{1,0:T(8,128)(2,1)}) %reduce-scatter.26.cloned.1.call-update) | async-done | bytes 147472 | tf_op jit(solution)/shard_map/reduce_scatter | solution.py:283
  3134.7 231.2 %reduce-scatter.32.cloned.1.call-done = bf16[48,1536]{1,0:T(8,128)(2,1)} async-done(((bf16[1536,1536]{1,0:T(8,128)(2,1)}), bf16[48,1536]{1,0:T(8,128)(2,1)}) %reduce-scatter.32.cloned.1.call-update) | async-done | bytes 147472 | tf_op jit(solution)/shard_map/reduce_scatter | solution.py:292
  3365.8 251.4 %reduce-scatter.34.cloned.1.call-done = bf16[48,3840]{1,0:T(8,128)(2,1)} async-done(((bf16[1536,3840]{1,0:T(8,128)(2,1)}), bf16[48,3840]{1,0:T(8,128)(2,1)}) %reduce-scatter.34.cloned.1.call-update) | async-done | bytes 368656 | tf_op jit(solution)/shard_map/reduce_scatter | solution.py:298
  3617.2 251.8 %reduce-scatter.36.cloned.1.call-done = bf16[48,3840]{1,0:T(8,128)(2,1)} async-done(((bf16[1536,3840]{1,0:T(8,128)(2,1)}), bf16[48,3840]{1,0:T(8,128)(2,1)}) %reduce-scatter.36.cloned.1.call-update) | async-done | bytes 368656 | tf_op jit(solution)/shard_map/reduce_scatter | solution.py:301
  3869.0 250.8 %reduce-scatter.38.cloned.1.call-done = bf16[120,1536]{1,0:T(8,128)(2,1)} async-done(((bf16[3840,1536]{1,0:T(8,128)(2,1)}), bf16[120,1536]{1,0:T(8,128)(2,1)}) %reduce-scatter.38.cloned.1.call-update) | async-done | bytes 368656 | tf_op jit(solution)/shard_map/reduce_scatter | solution.py:304
  4123.8 36.3 all-reduce.14.cloned.1.call-done
  4165.3 45.4 %all-reduce.16.cloned.1.call-done = (bf16[48,1536]{1,0:T(8,128)(2,1)}, bf16[48,1536]{1,0:T(8,128)(2,1)}, bf16[48,3840]{1,0:T(8,128)(2,1)}, bf16[48,3840]{1,0:T(8,128)(2,1)}, bf16[120,1536]{1,0:T(8,128)(2,1)}) async-done(((bf16[48,1536]{1,0:T(8,128)(2,1)}, bf16[48,1536]{1,0:T(8,128)(2,1)}, bf16[48,3840]{1,0:T(8,128)(2,1)}, bf16[48,3840]{1,0:T(8,128)(2,1)}, bf16[120,1536]{1,0:T(8,128)(2,1)}), ...) | async-done | bytes 1400848 | tf_op jit(solution)/shard_map/psum | solution.py:310
  (787 shorter events, 694.8 us)
Async XLA Ops:
  7.2 144.5 %all-gather.19.cloned.1.call-start = ((), (), s32[]{:S(2)}) async-start(), calls=%async_computation.14 | async-start | bytes 1622016 | tf_op jit(solution)/shard_map/all_gather | solution.py:234
  7.9 148.4 %all-gather.23.cloned.1.call-start = ((), (), s32[]{:S(2)}) async-start(), calls=%async_computation.16 | async-start | bytes 1622016 | tf_op jit(solution)/shard_map/all_gather | solution.py:235
  8.7 259.5 %all-gather.39.cloned.1.call-start = ((), (), s32[]{:S(2)}) async-start(), calls=%async_computation.24 | async-start | bytes 2162688 | tf_op jit(solution)/shard_map/all_gather | solution.py:87
  149.5 579.9 %copy-start.46 = (f32[1536]{0:T(1024)}, f32[1536]{0:T(1024)S(1)}, u32[]{:S(2)}) copy-start(f32[1536]{0:T(1024)S(1)} %convert_element_type.559) | copy-start | bytes 18436
  156.2 184.5 %all-gather.41.cloned.1.call-start = ((), (), s32[]{:S(2)}) async-start(), calls=%async_computation.25 | async-start | bytes 2162688 | tf_op jit(solution)/shard_map/all_gather | solution.py:88
  158.9 254.3 %all-gather.21.cloned.1.call-start = ((), (), s32[]{:S(2)}) async-start(), calls=%async_computation.15 | async-start | bytes 2162688 | tf_op jit(solution)/shard_map/all_gather | solution.py:87
  159.8 325.9 %all-gather.25.cloned.1.call-start = ((), (), s32[]{:S(2)}) async-start(), calls=%async_computation.17 | async-start | bytes 2162688 | tf_op jit(solution)/shard_map/all_gather | solution.py:88
  160.9 397.4 %all-gather.35.cloned.1.call-start = ((), (), s32[]{:S(2)}) async-start(), calls=%async_computation.22 | async-start | bytes 2162688 | tf_op jit(solution)/shard_map/all_gather | solution.py:87
  161.7 469.2 %all-gather.37.cloned.1.call-start = ((), (), s32[]{:S(2)}) async-start(), calls=%async_computation.23 | async-start | bytes 2162688 | tf_op jit(solution)/shard_map/all_gather | solution.py:88
  162.9 554.4 %all-gather.17.cloned.1.call-start = ((), (), s32[]{:S(2)}) async-start(), calls=%async_computation.13 | async-start | bytes 4866048 | tf_op jit(solution)/shard_map/all_gather | solution.py:233
  163.6 659.0 %all-gather.27.cloned.1.call-start = ((), (), s32[]{:S(2)}) async-start(), calls=%async_computation.18 | async-start | bytes 4866048 | tf_op jit(solution)/shard_map/all_gather | solution.py:236
  164.2 764.9 %all-gather.29.cloned.1.call-start = ((), (), s32[]{:S(2)}) async-start(), calls=%async_computation.19 | async-start | bytes 12165120 | tf_op jit(solution)/shard_map/all_gather | solution.py:238
  164.9 890.4 %all-gather.31.cloned.1.call-start = ((), (), s32[]{:S(2)}) async-start(), calls=%async_computation.20 | async-start | bytes 12165120 | tf_op jit(solution)/shard_map/all_gather | solution.py:239
  165.5 1016.2 %all-gather.33.cloned.1.call-start = ((), (), s32[]{:S(2)}) async-start(), calls=%async_computation.21 | async-start | bytes 12165120 | tf_op jit(solution)/shard_map/all_gather | solution.py:240
  166.3 1346.5 %reduce-scatter.40.cloned.1.call-start = ((), (), s32[]{:S(2)}) async-start(), calls=%async_computation.33 | async-start | bytes 2162688
  1345.3 328.0 %reduce-scatter.44.cloned.1.call-start = ((), (), s32[]{:S(2)}) async-start(), calls=%async_computation.35 | async-start | bytes 2162688
  1423.8 434.6 %reduce-scatter.48.cloned.1.call-start = ((), (), s32[]{:S(2)}) async-start(), calls=%async_computation.37 | async-start | bytes 2162688
  1500.4 544.0 %reduce-scatter.42.cloned.1.call-start = ((), (), s32[]{:S(2)}) async-start(), calls=%async_computation.34 | async-start | bytes 2162688
  1504.5 725.7 %reduce-scatter.46.cloned.1.call-start = ((), (), s32[]{:S(2)}) async-start(), calls=%async_computation.36 | async-start | bytes 2162688
  1508.5 907.5 %reduce-scatter.50.cloned.1.call-start = ((), (), s32[]{:S(2)}) async-start(), calls=%async_computation.38 | async-start | bytes 2162688
  1512.6 1166.8 %reduce-scatter.28.cloned.1.call-start = ((), (), s32[]{:S(2)}) async-start(), calls=%async_computation.27 | async-start | bytes 1622016 | tf_op jit(solution)/shard_map/reduce_scatter | solution.py:286
  1863.1 1040.6 %reduce-scatter.30.cloned.1.call-start = ((), (), s32[]{:S(2)}) async-start(), calls=%async_computation.28 | async-start | bytes 1622016 | tf_op jit(solution)/shard_map/reduce_scatter | solution.py:289
  2419.8 714.9 %reduce-scatter.26.cloned.1.call-start = ((), (), s32[]{:S(2)}) async-start(), calls=%async_computation.26 | async-start | bytes 4866048 | tf_op jit(solution)/shard_map/reduce_scatter | solution.py:283
  2434.9 930.9 %reduce-scatter.32.cloned.1.call-start = ((), (), s32[]{:S(2)}) async-start(), calls=%async_computation.29 | async-start | bytes 4866048 | tf_op jit(solution)/shard_map/reduce_scatter | solution.py:292
  2442.5 1174.8 %reduce-scatter.34.cloned.1.call-start = ((), (), s32[]{:S(2)}) async-start(), calls=%async_computation.30 | async-start | bytes 12165120 | tf_op jit(solution)/shard_map/reduce_scatter | solution.py:298
  2483.7 1385.3 %reduce-scatter.36.cloned.1.call-start = ((), (), s32[]{:S(2)}) async-start(), calls=%async_computation.31 | async-start | bytes 12165120 | tf_op jit(solution)/shard_map/reduce_scatter | solution.py:301
  2525.2 1594.6 %reduce-scatter.38.cloned.1.call-start = ((), (), s32[]{:S(2)}) async-start(), calls=%async_computation.32 | async-start | bytes 12165120 | tf_op jit(solution)/shard_map/reduce_scatter | solution.py:304
  2567.1 1593.1 %all-reduce.14.cloned.1.call-start = ((), (), s32[]{:S(2)}) async-start(), calls=%async_computation.39 | async-start | bytes 198656 | tf_op jit(solution)/shard_map/psum | solution.py:309
  2597.2 1524.7 %copy-start.28 = (f32[64,1536]{1,0:T(8,128)S(1)}, f32[64,1536]{1,0:T(8,128)}, u32[]{:S(2)}) copy-start(f32[64,1536]{1,0:T(8,128)} %copy-done.26) | copy-start | bytes 1179652
  2597.2 1524.7 %copy-start.30 = (f32[64,1536]{1,0:T(8,128)S(1)}, f32[64,1536]{1,0:T(8,128)}, u32[]{:S(2)}) copy-start(f32[64,1536]{1,0:T(8,128)} %get-tuple-element.767) | copy-start | bytes 1179652
  2597.2 1524.7 %copy-start.32 = (f32[64,1536]{1,0:T(8,128)S(1)}, f32[64,1536]{1,0:T(8,128)}, u32[]{:S(2)}) copy-start(f32[64,1536]{1,0:T(8,128)} %get-tuple-element.768) | copy-start | bytes 1179652
  2903.7 1307.1 %all-reduce.16.cloned.1.call-start = ((), (), s32[]{:S(2)}) async-start(), calls=%async_computation.40 | async-start | bytes 2801664 | tf_op jit(solution)/shard_map/psum | solution.py:310
  (108 other events, 6674.6 us)
Sparse Core Ops, SparseCore 0:
  11.0 67.0 all-gather.18
  81.1 66.6 all-gather.22
  156.3 111.8 all-gather.38
  271.7 68.9 all-gather.40
  344.2 68.9 all-gather.20
  416.7 68.9 all-gather.24
  489.3 68.9 all-gather.34
  561.9 68.9 all-gather.36
  634.0 83.2 all-gather.16
  720.1 81.9 all-gather.26
  805.2 123.9 all-gather.28
  932.0 123.3 all-gather.30
  1058.4 123.3 all-gather.32
  1345.4 142.4 reduce-scatter.39
  1490.2 183.0 reduce-scatter.43
  1675.5 182.8 reduce-scatter.47
  1860.8 183.5 reduce-scatter.41
  2046.6 183.5 reduce-scatter.45
  2232.7 183.2 reduce-scatter.49
  2420.7 258.7 reduce-scatter.27
  2685.1 218.5 reduce-scatter.29
  2908.7 225.8 reduce-scatter.25
  3139.8 226.0 reduce-scatter.31
  3371.1 246.1 reduce-scatter.33
  3623.5 245.4 reduce-scatter.35
  3874.3 245.4 reduce-scatter.37
  4123.2 36.9 all-reduce.13
  4163.0 47.6 all-reduce.15
where the time goes:
time: 4240 us; the launch traced here: 4230 us
  waiting for transfers between devices  3280 us (77%)
  matrix products  556 us (13%)
  blocking collectives  213 us (5%)
  local copies, waits for them, and re-layouts  98.8 us (2%)
  other arithmetic  53 us (1%)
    unnamed x34, waiting for transfers between devices  894 us
    dot_general x63, matrix products, product(): return jnp.dot(left, right, preferred_element_type=jnp.float32)  308 us
    reduce_scatter x1, waiting for transfers between devices, on_device(): lax.psum_scatter(totals[7].astype(jnp.bfloat16), 'shard', scatter_dimensi...  252 us
    reduce_scatter x1, waiting for transfers between devices, on_device(): lax.psum_scatter(totals[6].astype(jnp.bfloat16), 'shard', scatter_dimensi...  251 us
    reduce_scatter x1, waiting for transfers between devices, on_device(): lax.psum_scatter(totals[8].astype(jnp.bfloat16), 'shard', scatter_dimensi...  251 us
    all_gather x3, waiting for transfers between devices, forward_pass(): lax.all_gather(keys_local, 'shard', axis=0, tiled=True)  239 us
    reduce_scatter x1, waiting for transfers between devices, on_device(): lax.psum_scatter(totals[4].astype(jnp.bfloat16), 'shard', scatter_dimensi...  231 us
    reduce_scatter x1, waiting for transfers between devices, on_device(): lax.psum_scatter(totals[1].astype(jnp.bfloat16), 'shard', scatter_dimensi...  230 us
  transfers between devices with their start and end apart: 28, of which 24 were waited for; matrix products, arithmetic and copies ran while one was open for 12% of the time, Pallas kernels for 0%

commit v1 on v0

v1 whole, which is shorter than its diff:
```python
from functools import partial
import math

import jax
import jax.numpy as jnp
from jax import lax
from jax.experimental import pallas as pl
from jax.experimental.pallas import tpu as pltpu
from jax.sharding import Mesh
from jax.sharding import PartitionSpec as P

HEADS = 24
KVH = 8
HD = 64
D = 1536
FF = 3840
MB = 3
SPAN = 64
SHARDS = 32
SEQ = 2048
PARTS = 4
ROWS = MB * SPAN
BOTH = 2 * ROWS
GROUP = HEADS // KVH
HALF_KV = KVH // 2
HQ = HALF_KV * GROUP * HD
HK = HALF_KV * HD
HF = FF // 2
CHUNK = SPAN // PARTS
TILE = 4
TILES = SHARDS // TILE
BLOCK = TILE * SPAN
TROWS = GROUP * TILE * CHUNK

SHARD = ("z", "y", "xh")
branch_scale = 1.4 / math.sqrt(52.0)
eps_norm = 1e-05
NEG = -1e30
VMEM_LIMIT = 48 * 1024 * 1024


def product(left, right):
    return jnp.dot(left, right, preferred_element_type=jnp.float32)


def product_t(left, right):
    return lax.dot_general(left, right, (((1,), (1,)), ((), ())), preferred_element_type=jnp.float32)


def t_product(left, right):
    return lax.dot_general(left, right, (((0,), (0,)), ((), ())), preferred_element_type=jnp.float32)


def swap(values):
    return lax.ppermute(values, "c", [(0, 1), (1, 0)])


def exchange(values):
    return lax.all_to_all(values, SHARD, 0, 0, tiled=True)


def stack_heads(rows):
    return jnp.concatenate([rows[:, g * HD : (g + 1) * HD] for g in range(GROUP)], axis=0)


def lay_heads(rows):
    size = TILE * CHUNK
    return jnp.concatenate([rows[g * size : (g + 1) * size] for g in range(GROUP)], axis=1)


def tile_mask(part, start_rows, tile, blocks):
    wide = blocks * BLOCK
    row = lax.broadcasted_iota(jnp.int32, (TROWS, 1), 0)
    inside = lax.rem(row, TILE * CHUNK)
    q_pos = tile * BLOCK + (inside // CHUNK) * SPAN + part * CHUNK + lax.rem(inside, CHUNK)
    k_pos = (tile + 1 - blocks) * BLOCK + lax.broadcasted_iota(jnp.int32, (TROWS, wide), 1)
    return (k_pos >= start_rows) & (k_pos <= q_pos)


def fwd_kernel(part_ref, first_ref, q_ref, kv_ref, start_ref, o_ref, lse_ref):
    micro = pl.program_id(0)
    part = part_ref[0]

    def tile_body(tile, carry):
        first = first_ref[micro * TILES + tile]

        def work(blocks):
            wide = blocks * BLOCK
            begin = tile + 1 - blocks
            q_rows = stack_heads(
                q_ref[pl.ds(tile * TILE, TILE), 0].reshape(TILE * CHUNK, GROUP * HD)
            ) * jnp.bfloat16(0.125)
            keys = kv_ref[pl.ds(begin * TILE, blocks * TILE), 0].reshape(wide, 2 * HD)
            scores = product_t(q_rows, keys[:, :HD])
            start_rows = start_ref[0, tile][:, :1]
            allowed = tile_mask(part, start_rows, tile, blocks)
            scores = jnp.where(allowed, scores, NEG)
            highest = jnp.max(scores, axis=-1, keepdims=True)
            expo = jnp.exp(scores - highest)
            total = jnp.sum(expo, axis=-1, keepdims=True)
            mixed = product(expo.astype(jnp.bfloat16), keys[:, HD:]) / total
            o_ref[pl.ds(tile * TILE, TILE), 0] = (
                lay_heads(mixed).astype(jnp.bfloat16).reshape(TILE, CHUNK, GROUP * HD)
            )
            lse_ref[0, tile] = jnp.broadcast_to(highest + jnp.log(total), (TROWS, 128))

        for blocks in range(1, TILES + 1):
            pl.when(tile + 1 - first == blocks)(partial(work, blocks))
        return carry

    lax.fori_loop(0, TILES, tile_body, 0)


def bwd_kernel(part_ref, first_ref, q_ref, kv_ref, start_ref, do_ref, lse_ref, dq_ref, dkv_ref, acc):
    micro = pl.program_id(0)
    part = part_ref[0]
    acc[...] = jnp.zeros_like(acc)

    def tile_body(tile, carry):
        first = first_ref[micro * TILES + tile]

        def work(blocks):
            wide = blocks * BLOCK
            begin = tile + 1 - blocks
            q_rows = stack_heads(
                q_ref[pl.ds(tile * TILE, TILE), 0].reshape(TILE * CHUNK, GROUP * HD)
            ) * jnp.bfloat16(0.125)
            d_rows = stack_heads(
                do_ref[pl.ds(tile * TILE, TILE), 0].reshape(TILE * CHUNK, GROUP * HD)
            )
            keys = kv_ref[pl.ds(begin * TILE, blocks * TILE), 0].reshape(wide, 2 * HD)
            scores = product_t(q_rows, keys[:, :HD])
            start_rows = start_ref[0, tile][:, :1]
            allowed = tile_mask(part, start_rows, tile, blocks)
            probs = jnp.where(allowed, jnp.exp(scores - lse_ref[0, tile][:, :1]), 0.0)
            d_probs = product_t(d_rows, keys[:, HD:])
            offset = jnp.sum(d_probs * probs, axis=-1, keepdims=True)
            d_scores = (probs * (d_probs - offset)).astype(jnp.bfloat16)
            d_query = product(d_scores, keys[:, :HD]) * 0.125
            dq_ref[pl.ds(tile * TILE, TILE), 0] = (
                lay_heads(d_query).astype(jnp.bfloat16).reshape(TILE, CHUNK, GROUP * HD)
            )
            d_key = t_product(d_scores, q_rows)
            d_value = t_product(probs.astype(jnp.bfloat16), d_rows)
            where = pl.ds(begin * BLOCK, wide)
            acc[where, :] += jnp.concatenate([d_key, d_value], axis=1)

        for blocks in range(1, TILES + 1):
            pl.when(tile + 1 - first == blocks)(partial(work, blocks))
        return carry

    lax.fori_loop(0, TILES, tile_body, 0)
    dkv_ref[:, 0] = acc[...].astype(jnp.bfloat16).reshape(SHARDS, SPAN, 2 * HD)


SMEM = pl.BlockSpec(memory_space=pltpu.SMEM)
Q_SPEC = pl.BlockSpec((SHARDS, 1, CHUNK, GROUP * HD), lambda m: (0, m, 0, 0))
KV_SPEC = pl.BlockSpec((SHARDS, 1, SPAN, 2 * HD), lambda m: (0, m, 0, 0))
COL_SPEC = pl.BlockSpec((1, TILES, TROWS, 128), lambda m: (m, 0, 0, 0))
Q_SHAPE = jax.ShapeDtypeStruct((SHARDS, MB, CHUNK, GROUP * HD), jnp.bfloat16)
KV_SHAPE = jax.ShapeDtypeStruct((SHARDS, MB, SPAN, 2 * HD), jnp.bfloat16)
COL_SHAPE = jax.ShapeDtypeStruct((MB, TILES, TROWS, 128), jnp.float32)


def attend_fwd(part, first, queries, keys, starts):
    return pl.pallas_call(
        fwd_kernel,
        grid=(MB,),
        in_specs=[SMEM, SMEM, Q_SPEC, KV_SPEC, COL_SPEC],
        out_specs=[Q_SPEC, COL_SPEC],
        out_shape=[Q_SHAPE, COL_SHAPE],
        compiler_params=pltpu.CompilerParams(vmem_limit_bytes=VMEM_LIMIT),
        name="attend_forward",
    )(part, first, queries, keys, starts)


def attend_bwd(part, first, queries, keys, starts, d_mixed, lse):
    return pl.pallas_call(
        bwd_kernel,
        grid=(MB,),
        in_specs=[SMEM, SMEM, Q_SPEC, KV_SPEC, COL_SPEC, Q_SPEC, COL_SPEC],
        out_specs=[Q_SPEC, KV_SPEC],
        out_shape=[Q_SHAPE, KV_SHAPE],
        scratch_shapes=[pltpu.VMEM((SEQ, 2 * HD), jnp.float32)],
        compiler_params=pltpu.CompilerParams(vmem_limit_bytes=VMEM_LIMIT),
        name="attend_backward",
    )(part, first, queries, keys, starts, d_mixed, lse)


def rotate(values, cosine, sine, sign):
    half = HD // 2
    front, back = values[..., :half], values[..., half:]
    turned = sine * sign
    return jnp.concatenate([front * cosine - back * turned, back * cosine + front * turned], axis=-1)


def to_units_q(rows):
    split = rows.reshape(2, MB, PARTS, CHUNK, HALF_KV, GROUP * HD)
    return split.transpose(4, 0, 2, 1, 3, 5).reshape(SHARDS, MB, CHUNK, GROUP * HD)


def from_units_q(units):
    split = units.reshape(HALF_KV, 2, PARTS, MB, CHUNK, GROUP * HD)
    return split.transpose(1, 3, 2, 4, 0, 5).reshape(BOTH, HQ)


def to_units_kv(keys, values):
    both = jnp.concatenate([keys, values], axis=-1).transpose(3, 0, 1, 2, 4)
    wide = jnp.broadcast_to(both[:, :, None], (HALF_KV, 2, PARTS, MB, SPAN, 2 * HD))
    return wide.reshape(SHARDS, MB, SPAN, 2 * HD)


def piece_perm():
    return [(k * SHARDS + s, (s // 16) * SHARDS + 2 * (s % 16) + k) for k in range(2) for s in range(SHARDS)]


def row_pieces(core, local):
    half = lax.dynamic_slice_in_dim(local, core * (D // 2), D // 2, axis=1)
    return lax.ppermute(half, ("c",) + SHARD, piece_perm())


def row_half(piece):
    rows = piece.shape[0]
    whole = lax.all_gather(piece, SHARD, axis=0, tiled=True)
    return whole.reshape(16, 2, rows, D // 2).transpose(0, 2, 1, 3).reshape(16 * rows, D)


def col_half(core, local):
    half = local.shape[1] // 2
    return lax.dynamic_slice_in_dim(local, core * half, half, axis=1)


def add_x(values):
    return values.astype(jnp.float32) + lax.ppermute(values, "xl", [(0, 1), (1, 0)]).astype(jnp.float32)


def join_cores(core, mine):
    other = swap(mine)
    first = jnp.where(core == 0, mine, other)
    second = jnp.where(core == 0, other, mine)
    return jnp.concatenate([first, second], axis=1).astype(jnp.float32)


def scatter_sum(values):
    return jnp.sum(exchange(values).astype(jnp.float32), axis=0).astype(jnp.bfloat16)


def own_rows(core, piece):
    back = lax.ppermute(piece, ("c",) + SHARD, [(b, a) for a, b in piece_perm()])
    return join_cores(core, back)


def to_pieces(grad):
    rows = grad.shape[0] // 16
    return grad.reshape(16, rows, 2, D // 2).transpose(0, 2, 1, 3).reshape(SHARDS, rows, D // 2)


def on_device(
    hidden_in,
    doc_ids,
    out_grad,
    norm_attn,
    w_query,
    w_key,
    w_value,
    w_out,
    norm_ffn,
    w_gate,
    w_up,
    w_down,
):
    core = lax.axis_index("c")
    shard = lax.axis_index(SHARD)
    low = jnp.bfloat16

    packed = jnp.concatenate([doc_ids.reshape(-1).astype(low), norm_attn, norm_ffn])
    small = exchange(jnp.broadcast_to(packed[None, None], (SHARDS, 1, packed.shape[0])))[:, 0]
    docs_mine = small[:, :ROWS].reshape(SHARDS, MB, SPAN).transpose(1, 0, 2).reshape(MB, SEQ)
    gain_attn = small[:, ROWS : ROWS + 48].reshape(D).astype(jnp.float32)
    gain_ffn = small[:, ROWS + 48 :].reshape(D).astype(jnp.float32)
    docs_other = swap(docs_mine)

    w_qkv = lax.all_gather(
        jnp.concatenate([col_half(core, w_query), col_half(core, w_key), col_half(core, w_value)], axis=1),
        SHARD,
        axis=0,
        tiled=True,
    )
    w_o = row_half(row_pieces(core, w_out))
    w_gu = lax.all_gather(
        jnp.concatenate([col_half(core, w_gate), col_half(core, w_up)], axis=1), SHARD, axis=0, tiled=True
    )
    w_d = row_half(row_pieces(core, w_down))

    x_low = hidden_in.reshape(ROWS, D)
    x = x_low.astype(jnp.float32)
    x_both = jnp.concatenate([x_low, swap(x_low)], axis=0).astype(jnp.float32)
    dy_low = out_grad.reshape(ROWS, D)
    dy = dy_low.astype(jnp.float32)
    df = (branch_scale * jnp.concatenate([dy_low, swap(dy_low)], axis=0).astype(jnp.float32)).astype(low)

    which = lax.rem(shard // PARTS, 2)
    part = lax.rem(shard, PARTS)
    docs = jnp.where(which == 0, docs_mine, docs_other).astype(jnp.float32)
    counted = jnp.sum((docs[:, None, :] < docs[:, :, None]).astype(jnp.int32), axis=-1)
    q_start = lax.dynamic_slice_in_dim(counted.reshape(MB, SHARDS, SPAN), part * CHUNK, CHUNK, axis=2)
    q_start = q_start.reshape(MB, TILES, 1, TILE * CHUNK)
    first = (q_start[:, :, 0, 0] // BLOCK).reshape(-1)
    starts = jnp.broadcast_to(q_start, (MB, TILES, GROUP, TILE * CHUNK)).reshape(MB, TILES, TROWS, 1)
    starts = jnp.broadcast_to(starts, (MB, TILES, TROWS, 128))
    part_arr = part.reshape(1).astype(jnp.int32)

    places = (shard * SPAN + jnp.arange(SPAN, dtype=jnp.int32)).astype(jnp.float32)
    half_size = HD // 2
    inverse = jnp.exp(-jnp.arange(half_size, dtype=jnp.float32) * (math.log(10000.0) / half_size))
    angles = places[:, None] * inverse[None, :]
    cosine, sine = jnp.cos(angles)[:, None, :], jnp.sin(angles)[:, None, :]

    r1_both = lax.rsqrt(jnp.mean(x_both * x_both, axis=-1, keepdims=True) + eps_norm)
    r1 = r1_both[:ROWS]
    n1 = (x_both * r1_both * gain_attn).astype(low)
    qkv = product(n1, w_qkv)
    q5 = qkv[:, :HQ].reshape(2, MB, SPAN, HALF_KV * GROUP, HD)
    k5 = qkv[:, HQ : HQ + HK].reshape(2, MB, SPAN, HALF_KV, HD)
    v5 = qkv[:, HQ + HK :].reshape(2, MB, SPAN, HALF_KV, HD).astype(low)
    q_rot = rotate(q5, cosine, sine, 1.0).astype(low).reshape(BOTH, HQ)
    k_rot = rotate(k5, cosine, sine, 1.0).astype(low)
    unit_q = exchange(to_units_q(q_rot))
    unit_kv = exchange(to_units_kv(k_rot, v5))
    unit_o, lse = attend_fwd(part_arr, first, unit_q, unit_kv, starts)
    attn = from_units_q(exchange(unit_o))
    y1 = product(attn, w_o)
    hmid = x + branch_scale * (y1[:ROWS] + swap(y1[ROWS:].astype(low)).astype(jnp.float32))

    r2 = lax.rsqrt(jnp.mean(hmid * hmid, axis=-1, keepdims=True) + eps_norm)
    z2 = hmid * r2
    n2_mine = (z2 * gain_ffn).astype(low)
    n2 = jnp.concatenate([n2_mine, swap(n2_mine)], axis=0)
    gu = product(n2, w_gu)
    gate, up = gu[:, :HF], gu[:, HF:]
    sigma = jax.nn.sigmoid(gate)
    silu = gate * sigma
    act = (silu * up).astype(low)
    y2 = product(act, w_d)
    result = hmid + branch_scale * (y2[:ROWS] + swap(y2[ROWS:].astype(low)).astype(jnp.float32))

    g_down = t_product(act, df).astype(low)
    d_act = product_t(df, w_d)
    d_gate = (d_act * up * sigma * (1.0 + gate * (1.0 - sigma))).astype(low)
    d_up = (d_act * silu).astype(low)
    d_gu = jnp.concatenate([d_gate, d_up], axis=1)
    g_gu = t_product(n2, d_gu).astype(low)
    dn2_both = product_t(d_gu, w_gu)
    dn2 = dn2_both[:ROWS] + swap(dn2_both[ROWS:].astype(low)).astype(jnp.float32)
    e2 = dn2 * gain_ffn
    g_gain_ffn = jnp.sum(dn2 * z2, axis=0)
    dh = dy + r2 * (e2 - z2 * jnp.mean(e2 * z2, axis=-1, keepdims=True))

    da_mine = (branch_scale * dh).astype(low)
    da = jnp.concatenate([da_mine, swap(da_mine)], axis=0)
    g_o = t_product(attn, da).astype(low)
    do = product_t(da, w_o).astype(low)
    unit_do = exchange(to_units_q(do))
    unit_dq, unit_dkv = attend_bwd(part_arr, first, unit_q, unit_kv, starts, unit_do, lse)
    dq = from_units_q(exchange(unit_dq)).astype(jnp.float32)
    dkv = exchange(unit_dkv).reshape(HALF_KV, 2, PARTS, MB, SPAN, 2 * HD).astype(jnp.float32)
    dkv = jnp.sum(dkv, axis=2).transpose(1, 2, 3, 0, 4)
    dq = rotate(dq.reshape(2, MB, SPAN, HALF_KV * GROUP, HD), cosine, sine, -1.0).reshape(BOTH, HQ)
    dk = rotate(dkv[..., :HD], cosine, sine, -1.0).reshape(BOTH, HK)
    dv = dkv[..., HD:].reshape(BOTH, HK)
    d_qkv = jnp.concatenate([dq, dk, dv], axis=1).astype(low)
    g_qkv = t_product(n1, d_qkv).astype(low)
    dn1_both = product_t(d_qkv, w_qkv)
    dn1 = dn1_both[:ROWS] + swap(dn1_both[ROWS:].astype(low)).astype(jnp.float32)
    z1 = x * r1
    e1 = dn1 * gain_attn
    g_gain_attn = jnp.sum(dn1 * z1, axis=0)
    grad_in = (dh + r1 * (e1 - z1 * jnp.mean(e1 * z1, axis=-1, keepdims=True))).astype(low)

    s_gu = add_x(lax.psum_scatter(g_gu, SHARD, scatter_dimension=0, tiled=True)).astype(low)
    s_d = add_x(
        lax.psum_scatter(to_pieces(g_down), SHARD, scatter_dimension=0, tiled=True)[0]
    ).astype(low)
    s_qkv = add_x(scatter_sum(g_qkv.reshape(SHARDS, 48, HQ + 2 * HK))).astype(low)
    s_o = add_x(scatter_sum(to_pieces(g_o))).astype(low)
    gains = jnp.stack([g_gain_attn.reshape(SHARDS, 48), g_gain_ffn.reshape(SHARDS, 48)], axis=1)
    s_gain = add_x(jnp.sum(exchange(gains), axis=0))
    s_gain = s_gain + swap(s_gain)

    return (
        result.reshape(1, MB, SPAN, D).astype(low),
        grad_in.reshape(1, MB, SPAN, D),
        s_gain[0],
        join_cores(core, s_qkv[:, :HQ]),
        join_cores(core, s_qkv[:, HQ : HQ + HK]),
        join_cores(core, s_qkv[:, HQ + HK :]),
        own_rows(core, s_o),
        s_gain[1],
        join_cores(core, s_gu[:, :HF]),
        join_cores(core, s_gu[:, HF:]),
        own_rows(core, s_d),
    )


def solution(mesh):
    fine = Mesh(mesh.devices.reshape(2, 2, 4, 4, 2), ("xl", "c", "z", "y", "xh"))
    replica = ("xl", "c")
    tokens = P(replica, None, SHARD, None)
    matrix = P(SHARD, None)
    vector = P(SHARD)
    return jax.shard_map(
        on_device,
        mesh=fine,
        in_specs=(
            tokens,
            P(replica, None, SHARD),
            tokens,
            vector,
            matrix,
            matrix,
            matrix,
            matrix,
            vector,
            matrix,
            matrix,
            matrix,
        ),
        out_specs=(
            tokens,
            tokens,
            vector,
            matrix,
            matrix,
            matrix,
            matrix,
            vector,
            matrix,
            matrix,
            matrix,
        ),
        check_vma=False,
    )
```

time: 4240 us -> 1010 us (0.24)
  waiting for transfers between devices: 3280 us -> 540 us
  matrix products: 556 us -> 67.3 us
  blocking collectives: 213 us -> 41.9 us
  starting transfers between devices: 1.98 us -> 144 us
  Pallas kernels: 0 us -> 46 us
    reduce_scatter x7 -> x2, waiting for transfers between devices: 1440 us -> 227 us  [the longest x1 227 us: on_device(): lax.psum_scatter(g_gu, SHARD, scatter_dimension=0, tiled=True)]
    unnamed x34 -> x6, waiting for transfers between devices: 894 us -> 0.1 us
    all_gather x13 -> x4, waiting for transfers between devices: 865 us -> 194 us  [the longest x1 104 us: on_device(): lax.all_gather(jnp.concatenate([col_half(core, w_gate), col_half(core, w_...]
    dot_general x63 -> x4, matrix products: 308 us -> 20 us  [product(): return jnp.dot(left, right, preferred_element_type=jnp.float32)]
    unnamed x2 -> x0, blocking collectives: 213 us -> none
    dot_general x168 -> x8, matrix products: 248 us -> 47.4 us  [the longest x4 26.4 us: t_product(): lax.dot_general(left, right, (((0,), (0,)), ((), ())), preferred_element_...]
    ppermute x0 -> x26, waiting for transfers between devices: none -> 83.6 us  [the longest x5 56.8 us: add_x(): lax.ppermute(values, 'xl', [(0, 1), (1, 0)]).astype(jnp.float32)]
    psum x2 -> x0, waiting for transfers between devices: 81.8 us -> none  [the longest x1 45.4 us: on_device(): lax.psum(owned[1].astype(jnp.bfloat16), 'replica').astype(jnp.float32)]
  transfers between devices with their start and end apart: 28 -> 40, of which waited for: 24 -> 27; matrix products, arithmetic and copies ran while one was open for 12% -> 16% of each run, Pallas kernels for 0% -> 5%
where the time goes in v1:
time: 1010 us; the launch traced here: 994 us
  waiting for transfers between devices  540 us (53%)
  starting transfers between devices  144 us (14%)
  local copies, waits for them, and re-layouts  103 us (10%)
  matrix products  67.3 us (7%)
  Pallas kernels  46 us (5%)
  blocking collectives  41.9 us (4%)
  other arithmetic  38.1 us (4%)
  between operations  15.4 us (2%)
    reduce_scatter x1, waiting for transfers between devices, on_device(): lax.psum_scatter(g_gu, SHARD, scatter_dimension=0, tiled=True)  227 us
    all_gather x1, waiting for transfers between devices, on_device(): lax.all_gather(jnp.concatenate([col_half(core, w_gate), col_half(core, w_...  104 us
    all_to_all x8, starting transfers between devices, exchange(): return lax.all_to_all(values, SHARD, 0, 0, tiled=True)  64.5 us
    all_gather x2, waiting for transfers between devices, row_half(): whole = lax.all_gather(piece, SHARD, axis=0, tiled=True)  56.9 us
    ppermute x5, waiting for transfers between devices, add_x(): lax.ppermute(values, 'xl', [(0, 1), (1, 0)]).astype(jnp.float32)  56.8 us
    all_to_all x2, blocking collectives, exchange(): return lax.all_to_all(values, SHARD, 0, 0, tiled=True)  41.9 us
    all_to_all x8, waiting for transfers between devices, exchange(): return lax.all_to_all(values, SHARD, 0, 0, tiled=True)  34.8 us
    all_gather x1, waiting for transfers between devices, on_device(): lax.all_gather(jnp.concatenate([col_half(core, w_query), col_half(core, w...  33.5 us
  transfers between devices with their start and end apart: 40, of which 27 were waited for; matrix products, arithmetic and copies ran while one was open for 16% of the time, Pallas kernels for 5%

profile of v1, /device:TPU:49, one launch (start us, length us, event | category | flops | bytes accessed | tf_op | source)
XLA Modules:
  0.0 994.5 jit_solution(2789397420260831391)
XLA Ops:
  10.7 7.4 collective-permute-start.2
  20.2 10.6 %collective-permute-start.5 = (bf16[120,768]{1,0:T(8,128)(2,1)S(1)}, bf16[120,768]{1,0:T(8,128)(2,1)S(1)}, u32[]{:S(2)}, u32[]{:S(2)}) collective-permute-start(bf16[120,768]{1,0:T(8,128)(2,1)S(1)} %constant_dynamic-slice_fusion), channel_id=1, source_target_pairs={{0,0},{1,2},{2,4},{3,6},{4,8},{5,10},{6,12},{7,14},{8,16},{9,18},{... | collective-permute-start | bytes 552968 | tf_op jit(solution)/shard_map/ppermute | solution.py:219
  38.1 8.0 all-to-all-start
  58.0 33.5 %all-gather.5.cloned.1.call-done = bf16[1536,1280]{1,0:T(8,128)(2,1)} async-done(((bf16[48,1280]{1,0:T(8,128)(2,1)}), bf16[1536,1280]{1,0:T(8,128)(2,1)}) %all-gather.5.cloned.1.call-update) | async-done | bytes 3932176 | tf_op jit(solution)/shard_map/all_gather | solution.py:283
  104.9 6.9 all-to-all-start.1
  114.3 8.4 all-to-all-done.1.q_ref
  124.2 9.0 all-to-all-start.2
  139.8 14.4 %all-to-all-done.2.kv_ref = bf16[32,3,64,128]{3,2,1,0:T(8,128)(2,1)S(1)} async-done(((bf16[32,3,64,128]{3,2,1,0:T(8,128)(2,1)}), bf16[32,3,64,128]{3,2,1,0:T(8,128)(2,1)S(1)}, u32[]{:S(2)}, u32[]{:S(2)}) %all-to-all-start.2) | async-done | bytes 1572896 | tf_op jit(solution)/shard_map/all_to_all | solution.py:59
  156.6 19.1 %attend_forward.1 = (bf16[32,3,16,192]{3,2,1,0:T(8,128)(2,1)}, f32[3,8,192,128]{3,2,1,0:T(8,128)S(1)}) custom-call(s32[1]{0:T(128)} %bitcast.1.part_ref, s32[24]{0:T(128)S(1)} %and_select_fusion.first_ref, bf16[32,3,16,192]{3,2,1,0:T(8,128)(2,1)S(1)} %all-to-all-done.1.q_ref, bf16[32,3,64,128]{3,2,1,0:T(8,128)(2,1)S(1)} %all-to-all-done.2.kv_ref, ...), custom_call_target="tpu_custom_call" | custom-call | tf_op jit(solution)/shard_map/attend_forward/pallas_call | solution.py:166
  177.1 8.0 all-to-all-start.3
  185.1 12.5 %reduce-scatter.5.cloned.1.call-start = ((), (), s32[]{:S(2)}) async-start(), calls=%async_computation.17 | async-start | bytes 6082560 | tf_op jit(solution)/shard_map/reduce_scatter | solution.py:382
  220.4 56.9 %all-gather.11.cloned.1.call-done = bf16[3840,768]{1,0:T(8,128)(2,1)} async-done(((bf16[120,768]{1,0:T(8,128)(2,1)}), bf16[3840,768]{1,0:T(8,128)(2,1)}) %all-gather.11.cloned.1.call-update) | async-done | bytes 5898256 | tf_op jit(solution)/shard_map/all_gather | solution.py:224
  277.3 19.2 %copy.100 = bf16[16,2,120,768]{3,1,2,0:T(2,128)(2,1)S(1)} copy(bf16[16,2,120,768]{3,2,1,0:T(8,128)(2,1)} %bitcast.85) | data formatting | bytes 11796480 | tf_op jit(solution)/shard_map/reshape | solution.py:225
  300.1 104.0 %all-gather.9.cloned.1.call-done = bf16[1536,3840]{1,0:T(8,128)(2,1)} async-done(((bf16[48,3840]{1,0:T(8,128)(2,1)}), bf16[1536,3840]{1,0:T(8,128)(2,1)}) %all-gather.9.cloned.1.call-update) | async-done | bytes 11796496 | tf_op jit(solution)/shard_map/all_gather | solution.py:290
  404.1 8.3 fusion.18
  419.7 6.9 convolution_convert_fusion.1
  426.7 13.3 %reshape.324 = bf16[16,120,2,768]{3,2,1,0:T(2,128)(2,1)} reshape(bf16[1920,1536]{1,0:T(8,128)(2,1)} %convolution_convert_fusion.1) | data formatting | bytes 11796480 | tf_op jit(solution)/shard_map/reshape | solution.py:255
  446.1 11.1 %convolution_convert_fusion = bf16[1536,3840]{1,0:T(8,128)(2,1)} fusion(bf16[384,1920]{1,0:T(8,128)(2,1)} %get-tuple-element.26, bf16[384,1920]{1,0:T(8,128)(2,1)} %get-tuple-element.25, bf16[192,1536]{1,0:T(8,128)(2,1)} %collective-permute-done.4, bf16[192,1536]{1,0:T(8,128)(2,1)} %multiply_convert_fusion.5), kind=kOutput, calls=%fused_computation.1 | convolution fusion | flops 4544004096 | bytes 15925248 | tf_op jit(solution)/shard_map/dot_general | solution.py:51
  457.2 8.7 fusion.4
  483.2 20.1 %all_to_all.50.do_ref = bf16[32,3,16,192]{3,2,1,0:T(8,128)(2,1)S(1)} all-to-all(bf16[32,3,16,192]{3,2,1,0:T(8,128)(2,1)S(1)} %bitcast.90), channel_id=1, replica_groups=mesh['xl'=2,'c'=2,'z'=4,'y'=4,'xh'=2] {'z','y','xh'}, dimensions={0} | all-to-all | bytes 1179648 | tf_op jit(solution)/shard_map/all_to_all | solution.py:59
  503.3 26.9 %attend_backward.1 = (bf16[32,3,16,192]{3,2,1,0:T(8,128)(2,1)S(1)}, bf16[32,3,64,128]{3,2,1,0:T(8,128)(2,1)S(1)}) custom-call(s32[1]{0:T(128)} %bitcast.1.part_ref, s32[24]{0:T(128)S(1)} %and_select_fusion.first_ref, bf16[32,3,16,192]{3,2,1,0:T(8,128)(2,1)S(1)} %all-to-all-done.1.q_ref, bf16[32,3,64,128]{3,2,1,0:T(8,128)(2,1)S(1)} %all-to-all-done.2.kv_ref, ...), custom_call_target="tpu_custom_call" | custom-call | tf_op jit(solution)/shard_map/attend_backward/pallas_call | solution.py:178
  530.2 21.7 %all_to_all.51 = bf16[32,3,16,192]{3,2,1,0:T(8,128)(2,1)S(1)} all-to-all(bf16[32,3,16,192]{3,2,1,0:T(8,128)(2,1)S(1)} %get-tuple-element.17), channel_id=1, replica_groups=mesh['xl'=2,'c'=2,'z'=4,'y'=4,'xh'=2] {'z','y','xh'}, dimensions={0} | all-to-all | bytes 1179648 | tf_op jit(solution)/shard_map/all_to_all | solution.py:59
  551.9 8.3 all-to-all-start.6
  581.3 8.2 all-to-all-start.9
  618.9 7.4 all-to-all-start.7
  632.4 8.8 all-to-all-start.8
  641.7 45.3 %collective-permute-done.17 = bf16[48,768]{1,0:T(8,128)(2,1)S(1)} collective-permute-done((bf16[48,768]{1,0:T(8,128)(2,1)S(1)}, bf16[48,768]{1,0:T(8,128)(2,1)S(1)}, u32[]{:S(2)}, u32[]{:S(2)}) %collective-permute-start.17) | collective-permute-done | bytes 73760 | tf_op jit(solution)/shard_map/ppermute | solution.py:234
  687.0 8.4 collective-permute-start.18
  725.5 6.6 collective-permute-start.24
  732.2 8.9 collective-permute-done.24
  744.3 226.9 %reduce-scatter.3.cloned.1.call-done = bf16[48,3840]{1,0:T(8,128)(2,1)} async-done(((bf16[1536,3840]{1,0:T(8,128)(2,1)}), bf16[48,3840]{1,0:T(8,128)(2,1)}) %reduce-scatter.3.cloned.1.call-update) | async-done | bytes 368656 | tf_op jit(solution)/shard_map/reduce_scatter | solution.py:380
  972.3 6.9 collective-permute-done.20
  (262 shorter events, 208.7 us)
Async XLA Ops:
  7.2 84.2 %all-gather.5.cloned.1.call-start = ((), (), s32[]{:S(2)}) async-start(), calls=%async_computation.12 | async-start | bytes 4055040 | tf_op jit(solution)/shard_map/all_gather | solution.py:283
  9.7 187.8 %all-gather.7.cloned.1.call-start = ((), (), s32[]{:S(2)}) async-start(), calls=%async_computation.13 | async-start | bytes 2433024 | tf_op jit(solution)/shard_map/all_gather | solution.py:224
  10.7 8.8 collective-permute-start.2
  20.1 257.2 %all-gather.11.cloned.1.call-start = ((), (), s32[]{:S(2)}) async-start(), calls=%async_computation.15 | async-start | bytes 6082560 | tf_op jit(solution)/shard_map/all_gather | solution.py:224
  20.2 13.1 %collective-permute-start.5 = (bf16[120,768]{1,0:T(8,128)(2,1)S(1)}, bf16[120,768]{1,0:T(8,128)(2,1)S(1)}, u32[]{:S(2)}, u32[]{:S(2)}) collective-permute-start(bf16[120,768]{1,0:T(8,128)(2,1)S(1)} %constant_dynamic-slice_fusion), channel_id=1, source_target_pairs={{0,0},{1,2},{2,4},{3,6},{4,8},{5,10},{6,12},{7,14},{8,16},{9,18},{... | collective-permute-start | bytes 552968 | tf_op jit(solution)/shard_map/ppermute | solution.py:219
  34.0 370.1 %all-gather.9.cloned.1.call-start = ((), (), s32[]{:S(2)}) async-start(), calls=%async_computation.14 | async-start | bytes 12165120 | tf_op jit(solution)/shard_map/all_gather | solution.py:290
  38.1 14.1 %all-to-all-start = ((bf16[32,2,144]{2,1,0:T(2,128)(2,1)}), bf16[32,2,144]{2,1,0:T(2,128)(2,1)S(1)}, u32[]{:S(2)}, u32[]{:S(2)}) async-start(bf16[32,2,144]{2,1,0:T(2,128)(2,1)} %reshape.333), calls=%async_computation | async-start | bytes 65536 | tf_op jit(solution)/shard_map/all_to_all | solution.py:59
  46.1 11.6 %collective-permute-start.1 = (bf16[192,1536]{1,0:T(8,128)(2,1)S(1)}, bf16[192,1536]{1,0:T(8,128)(2,1)S(1)}, u32[]{:S(2)}, u32[]{:S(2)}) collective-permute-start(bf16[192,1536]{1,0:T(8,128)(2,1)S(1)} %bitcast.74), channel_id=1, source_target_pairs={{0,32},{32,0},{1,33},{33,1},{2,34},{34,2},{3,35},{35,3},{4,36},{36... | collective-permute-start | bytes 1769480 | tf_op jit(solution)/shard_map/ppermute | solution.py:55
  52.6 80.6 %collective-permute-start = (bf16[3,2048]{1,0:T(4,128)(2,1)S(1)}, bf16[3,2048]{1,0:T(4,128)(2,1)S(1)}, u32[]{:S(2)}, u32[]{:S(2)}) collective-permute-start(bf16[3,2048]{1,0:T(4,128)(2,1)S(1)} %reshape.301), channel_id=1, source_target_pairs={{0,32},{32,0},{1,33},{33,1},{2,34},{34,2},{3,35},{35,3},{4,36},{36... | collective-permute-start | bytes 36872 | tf_op jit(solution)/shard_map/ppermute | solution.py:55
  104.9 17.8 %all-to-all-start.1 = ((bf16[32,3,16,192]{3,2,1,0:T(8,128)(2,1)}), bf16[32,3,16,192]{3,2,1,0:T(8,128)(2,1)S(1)}, u32[]{:S(2)}, u32[]{:S(2)}) async-start(bf16[32,3,16,192]{3,2,1,0:T(8,128)(2,1)} %bitcast.4), calls=%async_computation.1 | async-start | bytes 1572864 | tf_op jit(solution)/shard_map/all_to_all | solution.py:59
  124.2 30.0 %all-to-all-start.2 = ((bf16[32,3,64,128]{3,2,1,0:T(8,128)(2,1)}), bf16[32,3,64,128]{3,2,1,0:T(8,128)(2,1)S(1)}, u32[]{:S(2)}, u32[]{:S(2)}) async-start(bf16[32,3,64,128]{3,2,1,0:T(8,128)(2,1)} %bitcast.83), calls=%async_computation.2 | async-start | bytes 3145728 | tf_op jit(solution)/shard_map/all_to_all | solution.py:59
  177.1 26.3 %all-to-all-start.3 = ((bf16[32,3,16,192]{3,2,1,0:T(8,128)(2,1)}), bf16[32,3,16,192]{3,2,1,0:T(8,128)(2,1)S(1)}, u32[]{:S(2)}, u32[]{:S(2)}) async-start(bf16[32,3,16,192]{3,2,1,0:T(8,128)(2,1)} %get-tuple-element.15), calls=%async_computation.3 | async-start | bytes 1572864 | tf_op jit(solution)/shard_map/all_to_all | solution.py:59
  185.1 534.7 %reduce-scatter.5.cloned.1.call-start = ((), (), s32[]{:S(2)}) async-start(), calls=%async_computation.17 | async-start | bytes 6082560 | tf_op jit(solution)/shard_map/reduce_scatter | solution.py:382
  219.9 80.2 %collective-permute-start.4 = (bf16[192,1536]{1,0:T(8,128)(2,1)}, bf16[192,1536]{1,0:T(8,128)(2,1)}, u32[]{:S(2)}, u32[]{:S(2)}) collective-permute-start(bf16[192,1536]{1,0:T(8,128)(2,1)} %multiply_convert_fusion.5), channel_id=1, source_target_pairs={{0,32},{32,0},{1,33},{33,1},{2,34},{34,2},{3,35},{35,3},{4,36},{36... | collective-permute-start | bytes 1769480 | tf_op jit(solution)/shard_map/ppermute | solution.py:55
  220.3 192.2 %collective-permute-start.7 = (bf16[192,1536]{1,0:T(8,128)(2,1)S(1)}, bf16[192,1536]{1,0:T(8,128)(2,1)}, u32[]{:S(2)}, u32[]{:S(2)}) collective-permute-start(bf16[192,1536]{1,0:T(8,128)(2,1)S(1)} %bitcast.97), channel_id=1, source_target_pairs={{0,32},{32,0},{1,33},{33,1},{2,34},{34,2},{3,35},{35,3},{4,36},{36... | collective-permute-start | bytes 1769480 | tf_op jit(solution)/shard_map/ppermute | solution.py:55
  446.0 525.2 %reduce-scatter.3.cloned.1.call-start = ((), (), s32[]{:S(2)}) async-start(), calls=%async_computation.16 | async-start | bytes 12165120 | tf_op jit(solution)/shard_map/reduce_scatter | solution.py:380
  465.9 6.1 collective-permute-start.8
  551.9 29.3 %all-to-all-start.6 = ((bf16[32,3,64,128]{3,2,1,0:T(8,128)(2,1)}), bf16[32,3,64,128]{3,2,1,0:T(8,128)(2,1)}, u32[]{:S(2)}, u32[]{:S(2)}) async-start(bf16[32,3,64,128]{3,2,1,0:T(8,128)(2,1)} %copy-done.3), calls=%async_computation.6 | async-start | bytes 3145728 | tf_op jit(solution)/shard_map/all_to_all | solution.py:59
  581.3 37.7 %all-to-all-start.9 = ((bf16[32,48,768]{2,1,0:T(8,128)(2,1)}), bf16[32,48,768]{2,1,0:T(8,128)(2,1)S(1)}, u32[]{:S(2)}, u32[]{:S(2)}) async-start(bf16[32,48,768]{2,1,0:T(8,128)(2,1)} %bitcast.81), calls=%async_computation.9 | async-start | bytes 4718592 | tf_op jit(solution)/shard_map/all_to_all | solution.py:59
  603.8 5.8 collective-permute-start.10
  618.9 13.5 %all-to-all-start.7 = ((f32[32,2,48]{2,1,0:T(2,128)}), f32[32,2,48]{2,1,0:T(2,128)S(1)}, u32[]{:S(2)}, u32[]{:S(2)}) async-start(f32[32,2,48]{2,1,0:T(2,128)} %pad_maximum_fusion.15), calls=%async_computation.7 | async-start | bytes 65536 | tf_op jit(solution)/shard_map/all_to_all | solution.py:59
  632.4 76.4 %all-to-all-start.8 = ((bf16[32,48,1280]{2,1,0:T(8,128)(2,1)}), bf16[32,48,1280]{2,1,0:T(8,128)(2,1)}, u32[]{:S(2)}, u32[]{:S(2)}) async-start(bf16[32,48,1280]{2,1,0:T(8,128)(2,1)} %bitcast.88), calls=%async_computation.8 | async-start | bytes 7864320 | tf_op jit(solution)/shard_map/all_to_all | solution.py:59
  641.6 45.4 %collective-permute-start.17 = (bf16[48,768]{1,0:T(8,128)(2,1)S(1)}, bf16[48,768]{1,0:T(8,128)(2,1)S(1)}, u32[]{:S(2)}, u32[]{:S(2)}) collective-permute-start(bf16[48,768]{1,0:T(8,128)(2,1)S(1)} %reduce_sum.115), channel_id=1, source_target_pairs={{0,64},{64,0},{1,65},{65,1},{2,66},{66,2},{3,67},{67,3},{4,68},{68... | collective-permute-start | bytes 221192 | tf_op jit(solution)/shard_map/ppermute | solution.py:234
  687.0 13.9 %collective-permute-start.18 = (bf16[48,768]{1,0:T(8,128)(2,1)S(1)}, bf16[48,768]{1,0:T(8,128)(2,1)S(1)}, u32[]{:S(2)}, u32[]{:S(2)}) collective-permute-start(bf16[48,768]{1,0:T(8,128)(2,1)S(1)} %add_convert_fusion.7), channel_id=1, source_target_pairs={{0,0},{2,1},{4,2},{6,3},{8,4},{10,5},{12,6},{14,7},{16,8},{18,9},{... | collective-permute-start | bytes 221192 | tf_op jit(solution)/shard_map/ppermute | solution.py:249
  707.6 8.5 collective-permute-start.12
  711.6 5.5 collective-permute-start.13
  718.3 13.8 %collective-permute-start.14 = (bf16[48,768]{1,0:T(8,128)(2,1)S(1)}, bf16[48,768]{1,0:T(8,128)(2,1)S(1)}, u32[]{:S(2)}, u32[]{:S(2)}) collective-permute-start(bf16[48,768]{1,0:T(8,128)(2,1)S(1)} %slice.172), channel_id=1, source_target_pairs={{0,32},{32,0},{1,33},{33,1},{2,34},{34,2},{3,35},{35,3},{4,36},{36... | collective-permute-start | bytes 221192 | tf_op jit(solution)/shard_map/ppermute | solution.py:55
  719.7 4.8 collective-permute-start.23
  725.5 15.5 %collective-permute-start.24 = (bf16[120,768]{1,0:T(8,128)(2,1)S(1)}, bf16[120,768]{1,0:T(8,128)(2,1)S(1)}, u32[]{:S(2)}, u32[]{:S(2)}) collective-permute-start(bf16[120,768]{1,0:T(8,128)(2,1)S(1)} %add_convert_fusion.5), channel_id=1, source_target_pairs={{0,0},{2,1},{4,2},{6,3},{8,4},{10,5},{12,6},{14,7},{16,8},{18,9},{... | collective-permute-start | bytes 552968 | tf_op jit(solution)/shard_map/ppermute | solution.py:249
  741.0 231.2 %collective-permute-start.25 = (bf16[120,768]{1,0:T(8,128)(2,1)S(1)}, bf16[120,768]{1,0:T(8,128)(2,1)S(1)}, u32[]{:S(2)}, u32[]{:S(2)}) collective-permute-start(bf16[120,768]{1,0:T(8,128)(2,1)S(1)} %collective-permute-done.24), channel_id=1, source_target_pairs={{0,32},{32,0},{1,33},{33,1},{2,34},{34,2},{3,35},{35,3},{4,36},{36... | collective-permute-start | bytes 552968 | tf_op jit(solution)/shard_map/ppermute | solution.py:55
  971.2 8.0 collective-permute-start.20
  980.4 4.3 collective-permute-start.22
  (39 other events, 403.8 us)
Sparse Core Ops, SparseCore 0:
  11.7 79.7 all-gather.4
  95.0 88.8 all-gather.6
  187.5 89.7 all-gather.10
  280.7 123.3 all-gather.8
  446.2 272.8 reduce-scatter.4
  724.3 246.9 reduce-scatter.2

commit v2 on v1

v2 whole, which is shorter than its diff:
```python
from functools import partial
import math

import jax
import jax.numpy as jnp
from jax import lax
from jax.experimental import pallas as pl
from jax.experimental.pallas import tpu as pltpu
from jax.sharding import Mesh
from jax.sharding import PartitionSpec as P

HEADS = 24
KVH = 8
HD = 64
D = 1536
FF = 3840
MB = 3
SPAN = 64
SHARDS = 32
SEQ = 2048
PARTS = 4
ROWS = MB * SPAN
BOTH = 2 * ROWS
GROUP = HEADS // KVH
HALF_KV = KVH // 2
HQ = HALF_KV * GROUP * HD
HK = HALF_KV * HD
HF = FF // 2
QKV = HQ + 2 * HK
CHUNK = SPAN // PARTS
TILE = 4
TILES = SHARDS // TILE
BLOCK = TILE * SPAN
TROWS = GROUP * TILE * CHUNK

SHARD = ("z", "y", "xh")
branch_scale = 1.4 / math.sqrt(52.0)
eps_norm = 1e-05
NEG = -1e30
VMEM_LIMIT = 48 * 1024 * 1024


def product(left, right):
    return jnp.dot(left, right, preferred_element_type=jnp.float32)


def product_t(left, right):
    return lax.dot_general(left, right, (((1,), (1,)), ((), ())), preferred_element_type=jnp.float32)


def t_product(left, right):
    return lax.dot_general(left, right, (((0,), (0,)), ((), ())), preferred_element_type=jnp.float32)


def swap(values):
    return lax.ppermute(values, "c", [(0, 1), (1, 0)])


def exchange(values):
    return lax.all_to_all(values, SHARD, 0, 0, tiled=True)


Q_ROWS = 2 * CHUNK
ALL_ROWS = SPAN + Q_ROWS


def to_groups(rows):
    parts = [rows[:, 192 * j : 192 * j + 128] for j in range(HALF_KV)]
    parts += [rows[:, 192 * j + 128 : 192 * j + 192] for j in range(HALF_KV)]
    return jnp.concatenate(parts, axis=1)


def from_groups(rows):
    parts = []
    for j in range(HALF_KV):
        parts += [rows[:, 128 * j : 128 * j + 128], rows[:, 512 + 64 * j : 576 + 64 * j]]
    return jnp.concatenate(parts, axis=1)


def interleave(keys, values):
    parts = []
    for j in range(HALF_KV):
        parts += [keys[:, HD * j : HD * j + HD], values[:, HD * j : HD * j + HD]]
    return jnp.concatenate(parts, axis=1)


def turn(values, cosine, sine):
    lane = lax.broadcasted_iota(jnp.int32, values.shape, values.ndim - 1)
    axis = values.ndim - 1
    other = jnp.where(lane % HD < HD // 2, pltpu.roll(values, 128 - HD // 2, axis), pltpu.roll(values, HD // 2, axis))
    return values * cosine + other * sine


def project_kernel(n_ref, w_ref, table_ref, out_ref):
    rows = n_ref[...]

    def group(g, table):
        wide = product(rows, w_ref[:, 128 * g : 128 * g + 128]).reshape(2 * MB, SPAN, 128)
        return turn(wide, table_ref[table][None], table_ref[table + 1][None]).astype(jnp.bfloat16)

    for j in range(HALF_KV):
        first, both = group(j, 0), group(6 + j, 2)
        if j % 2 == 0:
            third = group(4 + j // 2, 0)
        for o in range(2):
            for m in range(MB):
                for p in range(PARTS):
                    cut = slice(p * CHUNK, (p + 1) * CHUNK)
                    out_ref[j, o, p, m, 0:SPAN, :] = both[o * MB + m]
                    out_ref[j, o, p, m, SPAN : SPAN + CHUNK, :] = first[o * MB + m, cut]
                    out_ref[j, o, p, m, SPAN + CHUNK : ALL_ROWS, :] = third[o * MB + m, cut]


def third_head(pair_even, pair_odd):
    lane = lax.broadcasted_iota(jnp.int32, pair_even.shape, pair_even.ndim - 1)
    return jnp.where(lane < HD, pair_even, pair_odd)


def out_kernel(u_ref, left_ref, right_ref, attn_ref, mine_ref, other_ref):
    for o in range(2):
        for m in range(MB):
            for p in range(PARTS):
                thirds = [
                    third_head(u_ref[2 * k, o, p, m, CHUNK:, :], u_ref[2 * k + 1, o, p, m, CHUNK:, :])
                    for k in range(2)
                ]
                parts = []
                for j in range(HALF_KV):
                    parts += [u_ref[j, o, p, m, :CHUNK, :], thirds[j // 2][:, HD * (j % 2) : HD * (j % 2) + HD]]
                at = (o * MB + m) * SPAN + p * CHUNK
                attn_ref[at : at + CHUNK, :] = jnp.concatenate(parts, axis=1)
    attn = attn_ref[...]
    for k, w_ref in enumerate((left_ref, right_ref)):
        result = product(attn, w_ref[...])
        cols = slice(k * (D // 2), (k + 1) * (D // 2))
        mine_ref[:, cols] = result[:ROWS]
        other_ref[:, cols] = result[ROWS:].astype(jnp.bfloat16)


def d_out_kernel(da_ref, left_ref, right_ref, out_ref):
    rows = product_t(da_ref[:, : D // 2], left_ref[...]) + product_t(da_ref[:, D // 2 :], right_ref[...])
    rows = rows.astype(jnp.bfloat16)
    for j in range(HALF_KV):
        first = rows[:, 192 * j : 192 * j + 128]
        if j % 2 == 0:
            third = jnp.concatenate([rows[:, 192 * j + 128 : 192 * j + 192], rows[:, 192 * j + 320 : 192 * j + 384]], axis=1)
        for o in range(2):
            for m in range(MB):
                for p in range(PARTS):
                    at = (o * MB + m) * SPAN + p * CHUNK
                    out_ref[j, o, p, m, :CHUNK, :] = first[at : at + CHUNK]
                    out_ref[j, o, p, m, CHUNK:, :] = third[at : at + CHUNK]


def collect_kernel(u_ref, table_ref, out_ref):
    def put(g, o, m, at, size, values, table, row):
        cosine = table_ref[table, row : row + size]
        sine = table_ref[table + 1, row : row + size]
        out_ref[at : at + size, 128 * g : 128 * g + 128] = turn(values, cosine, -sine).astype(jnp.bfloat16)

    wide = jnp.float32
    for o in range(2):
        for m in range(MB):
            base = (o * MB + m) * SPAN
            for j in range(HALF_KV):
                total = u_ref[j, o, 0, m, 0:SPAN, :].astype(wide)
                for p in range(1, PARTS):
                    total = total + u_ref[j, o, p, m, 0:SPAN, :].astype(wide)
                put(6 + j, o, m, base, SPAN, total, 2, 0)
            for p in range(PARTS):
                at = base + p * CHUNK
                for j in range(HALF_KV):
                    first = u_ref[j, o, p, m, SPAN : SPAN + CHUNK, :].astype(wide)
                    put(j, o, m, at, CHUNK, first, 0, p * CHUNK)
                for k in range(2):
                    third = third_head(
                        u_ref[2 * k, o, p, m, SPAN + CHUNK : ALL_ROWS, :].astype(wide),
                        u_ref[2 * k + 1, o, p, m, SPAN + CHUNK : ALL_ROWS, :].astype(wide),
                    )
                    put(4 + k, o, m, at, CHUNK, third, 0, p * CHUNK)


def stack_heads(first, third, odd):
    last = jnp.where(odd == 1, third[:, HD:], third[:, :HD])
    return jnp.concatenate([first[:, :HD], first[:, HD:], last], axis=0)


def lay_heads(rows):
    size = TILE * CHUNK
    parts = [rows[g * size : (g + 1) * size] for g in range(GROUP)]
    shape = (TILE, CHUNK, 128)
    return (
        jnp.concatenate(parts[:2], axis=1).astype(jnp.bfloat16).reshape(shape),
        jnp.concatenate([parts[2], parts[2]], axis=1).astype(jnp.bfloat16).reshape(shape),
    )


def tile_mask(part, start_rows, tile, blocks):
    wide = blocks * BLOCK
    row = lax.broadcasted_iota(jnp.int32, (TROWS, 1), 0)
    inside = lax.rem(row, TILE * CHUNK)
    q_pos = tile * BLOCK + (inside // CHUNK) * SPAN + part * CHUNK + lax.rem(inside, CHUNK)
    k_pos = (tile + 1 - blocks) * BLOCK + lax.broadcasted_iota(jnp.int32, (TROWS, wide), 1)
    return (k_pos >= start_rows) & (k_pos <= q_pos)


def tile_queries(ref, tile, begin, odd):
    where = pl.ds(tile * TILE, TILE)
    first = ref[where, 0, begin : begin + CHUNK, :].reshape(TILE * CHUNK, 128)
    third = ref[where, 0, begin + CHUNK : begin + 2 * CHUNK, :].reshape(TILE * CHUNK, 128)
    return stack_heads(first, third, odd)


def tile_keys(ref, begin, blocks):
    return ref[pl.ds(begin * TILE, blocks * TILE), 0, 0:SPAN, :].reshape(blocks * BLOCK, 128)


def each_tile(first_ref, work):
    micro = pl.program_id(0)

    def body(tile, carry):
        needed = tile + 1 - first_ref[micro * TILES + tile]
        for blocks in range(1, TILES + 1):
            pl.when(needed == blocks)(partial(work, tile, blocks))
        return carry

    lax.fori_loop(0, TILES, body, 0)


def fwd_kernel(unit_ref, first_ref, u_ref, start_ref, o_ref, lse_ref):
    part, odd = unit_ref[0], unit_ref[1]

    def work(tile, blocks):
        q_rows = tile_queries(u_ref, tile, SPAN, odd) * jnp.bfloat16(0.125)
        keys = tile_keys(u_ref, tile + 1 - blocks, blocks)
        scores = product_t(q_rows, keys[:, :HD])
        allowed = tile_mask(part, start_ref[0, tile][:, :1], tile, blocks)
        scores = jnp.where(allowed, scores, NEG)
        highest = jnp.max(scores, axis=-1, keepdims=True)
        expo = jnp.exp(scores - highest)
        total = jnp.sum(expo, axis=-1, keepdims=True)
        mixed = product(expo.astype(jnp.bfloat16), keys[:, HD:]) / total
        where = pl.ds(tile * TILE, TILE)
        o_ref[where, 0, :CHUNK, :], o_ref[where, 0, CHUNK:, :] = lay_heads(mixed)
        lse_ref[0, tile] = jnp.broadcast_to(highest + jnp.log(total), (TROWS, 128))

    each_tile(first_ref, work)


def bwd_kernel(unit_ref, first_ref, u_ref, start_ref, do_ref, lse_ref, d_ref, acc):
    part, odd = unit_ref[0], unit_ref[1]
    acc[...] = jnp.zeros_like(acc)

    def work(tile, blocks):
        begin = tile + 1 - blocks
        q_rows = tile_queries(u_ref, tile, SPAN, odd) * jnp.bfloat16(0.125)
        d_rows = tile_queries(do_ref, tile, 0, odd)
        keys = tile_keys(u_ref, begin, blocks)
        scores = product_t(q_rows, keys[:, :HD])
        allowed = tile_mask(part, start_ref[0, tile][:, :1], tile, blocks)
        probs = jnp.where(allowed, jnp.exp(scores - lse_ref[0, tile][:, :1]), 0.0)
        d_probs = product_t(d_rows, keys[:, HD:])
        offset = jnp.sum(d_probs * probs, axis=-1, keepdims=True)
        d_scores = (probs * (d_probs - offset)).astype(jnp.bfloat16)
        d_query = product(d_scores, keys[:, :HD]) * 0.125
        at = pl.ds(tile * TILE, TILE)
        d_ref[at, 0, SPAN : SPAN + CHUNK, :], d_ref[at, 0, SPAN + CHUNK : ALL_ROWS, :] = lay_heads(d_query)
        d_key = t_product(d_scores, q_rows)
        d_value = t_product(probs.astype(jnp.bfloat16), d_rows)
        where = pl.ds(begin * BLOCK, blocks * BLOCK)
        acc[where, :] += jnp.concatenate([d_key, d_value], axis=1)

    each_tile(first_ref, work)
    d_ref[:, 0, 0:SPAN, :] = acc[...].astype(jnp.bfloat16).reshape(SHARDS, SPAN, 128)


SMEM = pl.BlockSpec(memory_space=pltpu.SMEM)
UNIT_SPEC = pl.BlockSpec((SHARDS, 1, ALL_ROWS, 128), lambda m: (0, m, 0, 0))
QUERY_SPEC = pl.BlockSpec((SHARDS, 1, Q_ROWS, 128), lambda m: (0, m, 0, 0))
COL_SPEC = pl.BlockSpec((1, TILES, TROWS, 128), lambda m: (m, 0, 0, 0))
COL_SHAPE = jax.ShapeDtypeStruct((MB, TILES, TROWS, 128), jnp.float32)
PARAMS = pltpu.CompilerParams(vmem_limit_bytes=VMEM_LIMIT)


def split_units(values):
    return values.reshape((HALF_KV, 2, PARTS) + values.shape[1:])


def low_shape(*dims):
    return jax.ShapeDtypeStruct(dims, jnp.bfloat16)


def project(n1, w_qkv, tables):
    shape = low_shape(HALF_KV, 2, PARTS, MB, ALL_ROWS, 128)
    out = pl.pallas_call(project_kernel, out_shape=shape, compiler_params=PARAMS, name="project")(n1, w_qkv, tables)
    return out.reshape(SHARDS, MB, ALL_ROWS, 128)


def out_project(units, w_o):
    return pl.pallas_call(
        out_kernel,
        out_shape=[low_shape(BOTH, HQ), jax.ShapeDtypeStruct((ROWS, D), jnp.float32), low_shape(ROWS, D)],
        compiler_params=PARAMS,
        name="out_project",
    )(split_units(units), *w_o)


def d_out_project(da, w_o):
    shape = low_shape(HALF_KV, 2, PARTS, MB, Q_ROWS, 128)
    out = pl.pallas_call(d_out_kernel, out_shape=shape, compiler_params=PARAMS, name="d_out_project")(da, *w_o)
    return out.reshape(SHARDS, MB, Q_ROWS, 128)


def collect(units, tables):
    shape = low_shape(BOTH, HQ + 2 * HK)
    return pl.pallas_call(collect_kernel, out_shape=shape, compiler_params=PARAMS, name="collect")(
        split_units(units), tables
    )


def attend_fwd(unit, first, units, starts):
    return pl.pallas_call(
        fwd_kernel,
        grid=(MB,),
        in_specs=[SMEM, SMEM, UNIT_SPEC, COL_SPEC],
        out_specs=[QUERY_SPEC, COL_SPEC],
        out_shape=[low_shape(SHARDS, MB, Q_ROWS, 128), COL_SHAPE],
        compiler_params=PARAMS,
        name="attend_forward",
    )(unit, first, units, starts)


def attend_bwd(unit, first, units, starts, d_mixed, lse):
    return pl.pallas_call(
        bwd_kernel,
        grid=(MB,),
        in_specs=[SMEM, SMEM, UNIT_SPEC, COL_SPEC, QUERY_SPEC, COL_SPEC],
        out_specs=UNIT_SPEC,
        out_shape=low_shape(SHARDS, MB, ALL_ROWS, 128),
        scratch_shapes=[pltpu.VMEM((SEQ, 128), jnp.float32)],
        compiler_params=PARAMS,
        name="attend_backward",
    )(unit, first, units, starts, d_mixed, lse)


def piece_perm():
    return [(k * SHARDS + s, (s // 16) * SHARDS + 2 * (s % 16) + k) for k in range(2) for s in range(SHARDS)]


def shift(values, axis, step):
    if axis == "x":
        line = lambda x: (x % 2) * 2 + x // 2
        return lax.ppermute(values, ("xl", "xh"), [(line(i), line((i + step) % 4)) for i in range(4)])
    return lax.ppermute(values, axis, [(i, (i + step) % 4) for i in range(4)])


def place(axis):
    if axis == "x":
        return lax.axis_index("xh") * 2 + lax.axis_index("xl")
    return lax.axis_index(axis)


def flip(values, axis):
    return lax.ppermute(values, axis, [(0, 1), (1, 0)])


def col_half(core, local):
    half = local.shape[1] // 2
    return lax.dynamic_slice_in_dim(local, core * half, half, axis=1)


def fold(rows, parts):
    n, r, w = rows.shape
    return rows.reshape(n, r, parts, w // parts).transpose(0, 2, 1, 3).reshape(n, parts * r, w // parts)


def unfold(rows, parts):
    n, r, w = rows.shape
    return rows.reshape(n, parts, r // parts, w).transpose(0, 2, 1, 3).reshape(n, r // parts, parts * w)


def wide_sum(*values):
    total = values[0].astype(jnp.float32)
    for value in values[1:]:
        total = total + value.astype(jnp.float32)
    return total.astype(jnp.bfloat16)


def after(values, event):
    return lax.optimization_barrier((values, event))[0]


def total_axis(values, axis):
    return values + shift(values, axis, 1) + shift(values, axis, 2) + shift(values, axis, 3)


def reduce_pair(values, axis, dim):
    size = values.shape[dim] // 2
    me = lax.axis_index(axis)
    keep = lax.dynamic_slice_in_dim(values, me * size, size, axis=dim)
    send = lax.dynamic_slice_in_dim(values, (1 - me) * size, size, axis=dim)
    return wide_sum(keep, flip(send, axis))


def add_pair(values, axis):
    return wide_sum(values, flip(values, axis))


def join_pair(mine, axis, dim):
    other = flip(mine, axis)
    lower = lax.axis_index(axis) == 0
    return jnp.concatenate([jnp.where(lower, mine, other), jnp.where(lower, other, mine)], axis=dim)


def join_cores(mine):
    return join_pair(mine, "c", 1).astype(jnp.float32)


def scatter_sum(values):
    return jnp.sum(exchange(values).astype(jnp.float32), axis=0).astype(jnp.bfloat16)


def on_device(
    hidden_in,
    doc_ids,
    out_grad,
    norm_attn,
    w_query,
    w_key,
    w_value,
    w_out,
    norm_ffn,
    w_gate,
    w_up,
    w_down,
):
    core = lax.axis_index("c")
    shard = lax.axis_index(SHARD)
    low = jnp.bfloat16

    rows_in = lax.ppermute(jnp.concatenate([w_out, w_down], axis=0), ("c",) + SHARD, piece_perm())
    gu_piece = jnp.concatenate([col_half(core, w_gate), col_half(core, w_up)], axis=1)
    w_all = lax.all_gather(
        jnp.concatenate(
            [
                join_pair(gu_piece, "xh", 0),
                rows_in[48:144],
                fold(rows_in[144:][None], 4)[0],
                fold(rows_in[:48][None], 2)[0],
            ],
            axis=1,
        ),
        ("z", "y"),
        axis=0,
        tiled=True,
    )
    w_gu = w_all[:, :FF]
    w_d = jnp.concatenate(
        [w_all[:, FF : FF + D].reshape(16, 96, D), unfold(w_all[:, FF + D : FF + 5 * D // 4].reshape(16, 96, D // 4), 4)],
        axis=1,
    ).reshape(HF, D)
    w_o = w_all[:, FF + 5 * D // 4 :].reshape(16, 2, 48, D // 2)
    w_o = [w_o[:, k].reshape(HQ, D // 2) for k in range(2)]
    small = jnp.concatenate(
        [norm_attn[:, None], norm_ffn[:, None], doc_ids.reshape(48, 4).astype(low), jnp.zeros((48, 122), low)], axis=1
    )
    piece = jnp.concatenate(
        [to_groups(col_half(core, w_query)), interleave(col_half(core, w_key), col_half(core, w_value)), small], axis=1
    )
    w_first = exchange(jnp.broadcast_to(piece[None], (SHARDS, 48, QKV + 128)))
    small = w_first[:, :, QKV : QKV + 6]
    w_first = w_first.reshape(D, QKV + 128)
    w_qkv = w_first[:, :QKV]
    gain_attn = small[:, :, 0].reshape(1, D).astype(jnp.float32)
    gain_ffn = small[:, :, 1].reshape(1, D).astype(jnp.float32)
    docs_mine = small[:, :, 2:].reshape(SHARDS, MB, SPAN).transpose(1, 0, 2).reshape(MB, SEQ)
    docs_other = swap(docs_mine)

    x_low = hidden_in.reshape(ROWS, D)
    x = x_low.astype(jnp.float32)
    x_both = jnp.concatenate([x_low, swap(x_low)], axis=0).astype(jnp.float32)
    dy_low = out_grad.reshape(ROWS, D)
    dy = dy_low.astype(jnp.float32)
    df = (branch_scale * jnp.concatenate([dy_low, swap(dy_low)], axis=0).astype(jnp.float32)).astype(low)

    which = lax.rem(shard // PARTS, 2)
    part = lax.rem(shard, PARTS)
    docs = jnp.where(which == 0, docs_mine, docs_other).astype(jnp.float32)
    counted = jnp.sum((docs[:, None, :] < docs[:, :, None]).astype(jnp.int32), axis=-1)
    q_start = lax.dynamic_slice_in_dim(counted.reshape(MB, SHARDS, SPAN), part * CHUNK, CHUNK, axis=2)
    q_start = q_start.reshape(MB, TILES, 1, TILE * CHUNK)
    first = (q_start[:, :, 0, 0] // BLOCK).reshape(-1)
    starts = jnp.broadcast_to(q_start, (MB, TILES, GROUP, TILE * CHUNK)).reshape(MB, TILES, TROWS, 1)
    starts = jnp.broadcast_to(starts, (MB, TILES, TROWS, 128))
    unit = jnp.stack([part, lax.rem(shard // (2 * PARTS), 2)]).astype(jnp.int32)

    places = (shard * SPAN + jnp.arange(SPAN, dtype=jnp.int32)).astype(jnp.float32)
    half_size = HD // 2
    inverse = jnp.exp(-jnp.arange(half_size, dtype=jnp.float32) * (math.log(10000.0) / half_size))
    angles = places[:, None] * inverse[None, :]
    cosine, sine = jnp.cos(angles), jnp.sin(angles)
    cosine = jnp.concatenate([cosine, cosine], axis=1)
    sine = jnp.concatenate([-sine, sine], axis=1)
    tables = jnp.stack(
        [
            jnp.concatenate([cosine, cosine], axis=1),
            jnp.concatenate([sine, sine], axis=1),
            jnp.concatenate([cosine, jnp.ones_like(cosine)], axis=1),
            jnp.concatenate([sine, jnp.zeros_like(sine)], axis=1),
        ]
    )

    r1_both = lax.rsqrt(jnp.mean(x_both * x_both, axis=-1, keepdims=True) + eps_norm)
    r1 = r1_both[:ROWS]
    n1 = (x_both * r1_both * gain_attn).astype(low)
    units = exchange(project(n1, w_first, tables))
    unit_o, lse = attend_fwd(unit, first, units, starts)
    attn, y1_mine, y1_other = out_project(exchange(unit_o), w_o)
    hmid = x + branch_scale * (y1_mine + swap(y1_other).astype(jnp.float32))

    r2 = lax.rsqrt(jnp.mean(hmid * hmid, axis=-1, keepdims=True) + eps_norm)
    z2 = hmid * r2
    n2_mine = (z2 * gain_ffn).astype(low)
    n2 = jnp.concatenate([n2_mine, swap(n2_mine)], axis=0)
    gu = product(n2, w_gu)
    gate, up = gu[:, :HF], gu[:, HF:]
    sigma = jax.nn.sigmoid(gate)
    silu = gate * sigma
    act = (silu * up).astype(low)
    y2 = product(act, w_d)
    result = hmid + branch_scale * (y2[:ROWS] + swap(y2[ROWS:].astype(low)).astype(jnp.float32))

    d_act = product_t(df, w_d)
    d_gate = (d_act * up * sigma * (1.0 + gate * (1.0 - sigma))).astype(low)
    d_up = (d_act * silu).astype(low)
    d_gu = jnp.concatenate([d_gate, d_up], axis=1)
    g_down = t_product(act, df).astype(low).reshape(16, 120, D)
    g_ffn = jnp.concatenate(
        [t_product(n2, d_gu).astype(low), g_down[:, :96].reshape(D, D), fold(g_down[:, 96:], 4).reshape(D, D // 4)],
        axis=1,
    )
    s_ffn = lax.psum_scatter(g_ffn, ("z", "y"), scatter_dimension=0, tiled=True)
    dn2_both = product_t(d_gu, w_gu)
    dn2 = dn2_both[:ROWS] + swap(dn2_both[ROWS:].astype(low)).astype(jnp.float32)
    e2 = dn2 * gain_ffn
    g_gain_ffn = jnp.sum(dn2 * z2, axis=0)
    dh = dy + r2 * (e2 - z2 * jnp.mean(e2 * z2, axis=-1, keepdims=True))

    da_mine = (branch_scale * dh).astype(low)
    da = jnp.concatenate([da_mine, swap(da_mine)], axis=0)
    unit_do = exchange(d_out_project(da, w_o))
    g_o = [t_product(attn, da[:, k * (D // 2) : (k + 1) * (D // 2)]).astype(low) for k in range(2)]
    g_o = jnp.stack([g.reshape(16, 48, D // 2) for g in g_o], axis=1).reshape(SHARDS, 48, D // 2)
    s_o = scatter_sum(after(g_o, unit_do))
    unit_d = attend_bwd(unit, first, units, starts, unit_do, lse)
    d_qkv = collect(exchange(unit_d), tables)

    g_qkv = t_product(n1, d_qkv).astype(low)
    s_qkv = scatter_sum(g_qkv.reshape(SHARDS, 48, HQ + 2 * HK))
    dn1_both = product_t(d_qkv, w_qkv)
    dn1 = dn1_both[:ROWS] + swap(dn1_both[ROWS:].astype(low)).astype(jnp.float32)
    z1 = x * r1
    e1 = dn1 * gain_attn
    g_gain_attn = jnp.sum(dn1 * z1, axis=0)
    grad_in = (dh + r1 * (e1 - z1 * jnp.mean(e1 * z1, axis=-1, keepdims=True))).astype(low)

    s_ffn, s_o = after((s_ffn, s_o), d_qkv)
    back = [(b, a) for a, b in piece_perm()]
    s_o = join_cores(lax.ppermute(add_pair(s_o, "xl"), ("c",) + SHARD, back))
    s_d = jnp.concatenate([s_ffn[:, FF : FF + D], unfold(s_ffn[None, :, FF + D :], 4)[0]], axis=0)
    s_d = lax.ppermute(add_pair(s_d, "xl"), ("c",) + SHARD, back)
    s_d = s_d.astype(jnp.float32) + swap(s_d).astype(jnp.float32)
    s_gu = add_pair(reduce_pair(s_ffn[:, :FF], "xh", 0), "xl")
    other = swap(s_gu)
    lower = core == 0
    g_g, g_u = [
        jnp.concatenate([jnp.where(lower, m, t), jnp.where(lower, t, m)], axis=1).astype(jnp.float32)
        for m, t in ((s_gu[:, :HF], other[:, :HF]), (s_gu[:, HF:], other[:, HF:]))
    ]
    gains = jnp.stack([g_gain_attn, g_gain_ffn])
    gains = gains + swap(gains)
    gains = total_axis(total_axis(total_axis(gains, "x"), "y"), "z")
    gains = lax.dynamic_slice_in_dim(gains, shard * 48, 48, axis=1)
    s_qkv = add_pair(s_qkv, "xl")
    other = swap(s_qkv)
    whole = [jnp.where(lower, s_qkv, other), jnp.where(lower, other, s_qkv)]

    def heads_of(offset):
        return jnp.concatenate(
            [w[:, HQ + 128 * j + offset : HQ + 128 * j + offset + HD] for w in whole for j in range(HALF_KV)], axis=1
        ).astype(jnp.float32)

    return (
        result.reshape(1, MB, SPAN, D).astype(low),
        grad_in.reshape(1, MB, SPAN, D),
        gains[0],
        jnp.concatenate([from_groups(w[:, :HQ]) for w in whole], axis=1).astype(jnp.float32),
        heads_of(0),
        heads_of(HD),
        s_o,
        gains[1],
        g_g,
        g_u,
        s_d,
    )


def solution(mesh):
    fine = Mesh(mesh.devices.reshape(2, 2, 4, 4, 2), ("xl", "c", "z", "y", "xh"))
    replica = ("xl", "c")
    tokens = P(replica, None, SHARD, None)
    matrix = P(SHARD, None)
    vector = P(SHARD)
    return jax.shard_map(
        on_device,
        mesh=fine,
        in_specs=(
            tokens,
            P(replica, None, SHARD),
            tokens,
            vector,
            matrix,
            matrix,
            matrix,
            matrix,
            vector,
            matrix,
            matrix,
            matrix,
        ),
        out_specs=(
            tokens,
            tokens,
            vector,
            matrix,
            matrix,
            matrix,
            matrix,
            vector,
            matrix,
            matrix,
            matrix,
        ),
        check_vma=False,
    )
```

time: 1010 us -> 632 us (0.63)
  waiting for transfers between devices: 540 us -> 259 us
  local copies, waits for them, and re-layouts: 103 us -> 40.3 us
  blocking collectives: 41.9 us -> 21.9 us
  starting transfers between devices: 144 us -> 127 us
  matrix products: 67.3 us -> 53 us
  Pallas kernels: 46 us -> 58.4 us
  other arithmetic: 38.1 us -> 49.5 us
    reduce_scatter x2 -> x1, waiting for transfers between devices: 227 us -> 0.01 us  [on_device(): s_ffn = lax.psum_scatter(g_ffn, ('z', 'y'), scatter_dimension=0, tiled=True)]
    all_gather x4 -> x1, waiting for transfers between devices: 194 us -> 37.3 us  [on_device(): lax.all_gather(jnp.concatenate([join_pair(gu_piece, 'xh', 0), rows_in[48:...]
    all_to_all x8 -> x6, waiting for transfers between devices: 34.8 us -> 148 us  [exchange(): return lax.all_to_all(values, SHARD, 0, 0, tiled=True)]
    reshape x16 -> x3, local copies, waits for them, and re-layouts: 56.1 us -> 6.53 us  [the longest x1 3.25 us: fold(): rows.reshape(n, r, parts, w // parts).transpose(0, 2, 1, 3)]
    all_to_all x2 -> x1, blocking collectives: 41.9 us -> 21.9 us  [exchange(): return lax.all_to_all(values, SHARD, 0, 0, tiled=True)]
    concatenate x5 -> x6, other arithmetic: 2.89 us -> 17.3 us  [the longest x1 12 us: on_device(): jnp.concatenate([t_product(n2, d_gu).astype(low), g_down[:, :96].reshape(...]
    reduce_scatter x2 -> x1, starting transfers between devices: 12.5 us -> 0.04 us  [on_device(): s_ffn = lax.psum_scatter(g_ffn, ('z', 'y'), scatter_dimension=0, tiled=True)]
    pallas_call x2 -> x6, Pallas kernels: 46 us -> 58.4 us  [the longest x1 27.4 us: attend_bwd(): pl.pallas_call(bwd_kernel, grid=(MB,), in_specs=[SMEM, SMEM, UNIT_SPEC, C...]
  transfers between devices with their start and end apart: 40 -> 40, of which waited for: 27 -> 21; matrix products, arithmetic and copies ran while one was open for 16% -> 13% of each run, Pallas kernels for 5% -> 9%
where the time goes in v2:
time: 632 us; the launch traced here: 625 us
  waiting for transfers between devices  259 us (41%)
  starting transfers between devices  127 us (20%)
  Pallas kernels  58.4 us (9%)
  matrix products  53 us (8%)
  other arithmetic  49.5 us (8%)
  local copies, waits for them, and re-layouts  40.3 us (6%)
  blocking collectives  21.9 us (3%)
  between operations  15.6 us (2%)
    all_to_all x6, waiting for transfers between devices, exchange(): return lax.all_to_all(values, SHARD, 0, 0, tiled=True)  148 us
    all_to_all x6, starting transfers between devices, exchange(): return lax.all_to_all(values, SHARD, 0, 0, tiled=True)  72.7 us
    all_gather x1, waiting for transfers between devices, on_device(): lax.all_gather(jnp.concatenate([join_pair(gu_piece, 'xh', 0), rows_in[48:...  37.3 us
    ppermute x3, waiting for transfers between devices, shift(): lax.ppermute(values, ('xl', 'xh'), [(line(i), line((i + step) % 4)) for i...  29.5 us
    pallas_call x1, Pallas kernels, attend_bwd(): pl.pallas_call(bwd_kernel, grid=(MB,), in_specs=[SMEM, SMEM, UNIT_SPEC, C...  27.4 us
    all_to_all x1, blocking collectives, exchange(): return lax.all_to_all(values, SHARD, 0, 0, tiled=True)  21.9 us
    dot_general x5, matrix products, t_product(): lax.dot_general(left, right, (((0,), (0,)), ((), ())), preferred_element_...  20.5 us
    pallas_call x1, Pallas kernels, attend_fwd(): pl.pallas_call(fwd_kernel, grid=(MB,), in_specs=[SMEM, SMEM, UNIT_SPEC, C...  19.9 us
  transfers between devices with their start and end apart: 40, of which 21 were waited for; matrix products, arithmetic and copies ran while one was open for 13% of the time, Pallas kernels for 9%

profile of v2, /device:TPU:49, one launch (start us, length us, event | category | flops | bytes accessed | tf_op | source)
XLA Modules:
  0.0 624.5 jit_solution(10775510144902392780)
XLA Ops:
  12.2 5.2 collective-permute-start.3
  19.5 5.6 collective-permute-done.3
  29.7 11.7 %all-to-all-start = ((bf16[32,48,1408]{2,1,0:T(8,128)(2,1)}), bf16[32,48,1408]{2,1,0:T(8,128)(2,1)}, u32[]{:S(2)}, u32[]{:S(2)}) async-start(bf16[32,48,1408]{2,1,0:T(8,128)(2,1)} %broadcast_in_dim.46), calls=%async_computation | async-start | bytes 8650752 | tf_op jit(solution)/shard_map/all_to_all | solution.py:60
  44.5 61.8 %all-to-all-done = bf16[32,48,1408]{2,1,0:T(8,128)(2,1)} async-done(((bf16[32,48,1408]{2,1,0:T(8,128)(2,1)}), bf16[32,48,1408]{2,1,0:T(8,128)(2,1)}, u32[]{:S(2)}, u32[]{:S(2)}) %all-to-all-start) | async-done | bytes 4325408 | tf_op jit(solution)/shard_map/all_to_all | solution.py:60
  109.2 6.0 project.1
  116.7 11.9 %all-to-all-start.1 = ((bf16[32,3,96,128]{3,2,1,0:T(8,128)(2,1)}), bf16[32,3,96,128]{3,2,1,0:T(8,128)(2,1)S(1)}, u32[]{:S(2)}, u32[]{:S(2)}) async-start(bf16[32,3,96,128]{3,2,1,0:T(8,128)(2,1)} %bitcast.82), calls=%async_computation.1 | async-start | bytes 4718592 | tf_op jit(solution)/shard_map/all_to_all | solution.py:60
  133.0 5.8 convert_reduce_fusion
  139.6 27.2 %all-to-all-done.1.u_ref = bf16[32,3,96,128]{3,2,1,0:T(8,128)(2,1)S(1)} async-done(((bf16[32,3,96,128]{3,2,1,0:T(8,128)(2,1)}), bf16[32,3,96,128]{3,2,1,0:T(8,128)(2,1)S(1)}, u32[]{:S(2)}, u32[]{:S(2)}) %all-to-all-start.1) | async-done | bytes 2359328 | tf_op jit(solution)/shard_map/all_to_all | solution.py:60
  169.2 19.9 %attend_forward.1 = (bf16[32,3,32,128]{3,2,1,0:T(8,128)(2,1)}, f32[3,8,192,128]{3,2,1,0:T(8,128)S(1)}) custom-call(s32[2]{0:T(128)S(1)} %pad_add_fusion.unit_ref, s32[24]{0:T(128)S(1)} %and_select_fusion.first_ref, bf16[32,3,96,128]{3,2,1,0:T(8,128)(2,1)S(1)} %all-to-all-done.1.u_ref, s32[3,8,192,128]{3,2,1,0:T(8,128)} %broadcast_in_dim.52.start_ref), custom_call_target="tpu_custom_call" | custom-call | tf_op jit(solution)/shard_map/attend_forward/pallas_call | solution.py:322
  190.5 11.5 %all-to-all-start.2 = ((bf16[32,3,32,128]{3,2,1,0:T(8,128)(2,1)}), bf16[32,3,32,128]{3,2,1,0:T(8,128)(2,1)}, u32[]{:S(2)}, u32[]{:S(2)}) async-start(bf16[32,3,32,128]{3,2,1,0:T(8,128)(2,1)} %get-tuple-element.19), calls=%async_computation.2 | async-start | bytes 1572864 | tf_op jit(solution)/shard_map/all_to_all | solution.py:60
  202.1 37.3 %all-gather.2.cloned.1.call-done = bf16[1536,6528]{1,0:T(8,128)(2,1)} async-done(((bf16[96,6528]{1,0:T(8,128)(2,1)}), bf16[1536,6528]{1,0:T(8,128)(2,1)}) %all-gather.2.cloned.1.call-update) | async-done | bytes 20054032 | tf_op jit(solution)/shard_map/all_gather | solution.py:443
  265.0 8.3 %fusion.2 = f32[384,3840]{1,0:T(8,128)S(1)} fusion(bf16[1536,6528]{1,0:T(8,128)(2,1)} %all-gather.2.cloned.1.call-done, bf16[192,1536]{1,0:T(8,128)(2,1)} %collective-permute-done.5, bf16[192,1536]{1,0:T(8,128)(2,1)} %multiply_convert_fusion.5), kind=kOutput, calls=%fused_computation.5 | convolution fusion | flops 4532207616 | bytes 18874368 | tf_op jit(solution)/shard_map/dot_general | solution.py:44
  273.4 6.4 %multiply_convert_fusion.1 = (bf16[384,1920]{1,0:T(8,128)(2,1)}, bf16[384,1920]{1,0:T(8,128)(2,1)}, bf16[384,1920]{1,0:T(8,128)(2,1)S(1)}) fusion(f32[384,3840]{1,0:T(8,128)S(1)} %fusion.2, bf16[1920,1536]{1,0:T(8,128)(2,1)S(1)} %bitcast.96, bf16[192,1536]{1,0:T(8,128)(2,1)} %collective-permute-done.7, bf16[192,1536]{1,0:T(8,128)(2,1)} %bitcast.26), kind=kOutput, calls=%fused_computation.14 | convolution fusion | flops 2279522304 | bytes 17399808 | tf_op jit(solution)/shard_map/dot_general | solution.py:48
  279.8 5.5 convolution_convert_fusion.1
  294.0 8.3 %convolution_convert_fusion = bf16[1536,3840]{1,0:T(8,128)(2,1)S(1)} fusion(bf16[384,1920]{1,0:T(8,128)(2,1)} %get-tuple-element.36, bf16[384,1920]{1,0:T(8,128)(2,1)S(1)} %copy-done.40, bf16[192,1536]{1,0:T(8,128)(2,1)} %collective-permute-done.5, bf16[192,1536]{1,0:T(8,128)(2,1)} %multiply_convert_fusion.5), kind=kOutput, calls=%fused_computation.2 | convolution fusion | flops 4544004096 | bytes 15925248 | tf_op jit(solution)/shard_map/dot_general | solution.py:52
  302.3 12.0 %pad_maximum_fusion = bf16[1536,5760]{1,0:T(8,128)(2,1)} fusion(bf16[1536,384]{1,0:T(8,128)(2,1)S(1)} %bitcast.99, bf16[1536,1536]{1,0:T(8,128)(2,1)S(1)} %bitcast.90, bf16[1536,3840]{1,0:T(8,128)(2,1)S(1)} %convolution_convert_fusion), kind=kLoop, calls=%fused_computation.1 | loop fusion | flops 53084160 | bytes 35389440 | tf_op jit(solution)/shard_map/concatenate | solution.py:538
  314.4 8.7 %fusion = f32[384,1536]{1,0:T(8,128)S(1)} fusion(bf16[1536,6528]{1,0:T(8,128)(2,1)} %all-gather.2.cloned.1.call-done, bf16[384,1920]{1,0:T(8,128)(2,1)} %get-tuple-element.36, bf16[384,1920]{1,0:T(8,128)(2,1)} %get-tuple-element.35), kind=kOutput, calls=%fused_computation.3 | convolution fusion | flops 4535746560 | bytes 17104896 | tf_op jit(solution)/shard_map/dot_general | solution.py:48
  323.6 5.1 fusion.50
  337.4 21.9 %all_to_all.35.do_ref = bf16[32,3,32,128]{3,2,1,0:T(8,128)(2,1)S(1)} all-to-all(bf16[32,3,32,128]{3,2,1,0:T(8,128)(2,1)S(1)} %bitcast.83), channel_id=1, replica_groups=mesh['xl'=2,'c'=2,'z'=4,'y'=4,'xh'=2] {'z','y','xh'}, dimensions={0} | all-to-all | bytes 1572864 | tf_op jit(solution)/shard_map/all_to_all | solution.py:60
  359.2 27.4 %attend_backward.1 = bf16[32,3,96,128]{3,2,1,0:T(8,128)(2,1)S(1)} custom-call(s32[2]{0:T(128)S(1)} %pad_add_fusion.unit_ref, s32[24]{0:T(128)S(1)} %and_select_fusion.first_ref, bf16[32,3,96,128]{3,2,1,0:T(8,128)(2,1)S(1)} %all-to-all-done.1.u_ref, s32[3,8,192,128]{3,2,1,0:T(8,128)} %broadcast_in_dim.52.start_ref, ...), custom_call_target="tpu_custom_call" | custom-call | tf_op jit(solution)/shard_map/attend_backward/pallas_call | solution.py:334
  388.0 11.2 %all-to-all-start.4 = ((bf16[32,3,96,128]{3,2,1,0:T(8,128)(2,1)}), bf16[32,3,96,128]{3,2,1,0:T(8,128)(2,1)S(1)}, u32[]{:S(2)}, u32[]{:S(2)}) async-start(bf16[32,3,96,128]{3,2,1,0:T(8,128)(2,1)} %copy-done.3), calls=%async_computation.4 | async-start | bytes 4718592 | tf_op jit(solution)/shard_map/all_to_all | solution.py:60
  403.5 28.4 %all-to-all-done.4 = bf16[32,3,96,128]{3,2,1,0:T(8,128)(2,1)S(1)} async-done(((bf16[32,3,96,128]{3,2,1,0:T(8,128)(2,1)}), bf16[32,3,96,128]{3,2,1,0:T(8,128)(2,1)S(1)}, u32[]{:S(2)}, u32[]{:S(2)}) %all-to-all-start.4) | async-done | bytes 2359328 | tf_op jit(solution)/shard_map/all_to_all | solution.py:60
  431.8 12.4 %all-to-all-start.6 = ((bf16[32,48,768]{2,1,0:T(8,128)(2,1)}), bf16[32,48,768]{2,1,0:T(8,128)(2,1)}, u32[]{:S(2)}, u32[]{:S(2)}) async-start(bf16[32,48,768]{2,1,0:T(8,128)(2,1)} %bitcast.94), calls=%async_computation.7 | async-start | bytes 4718592 | tf_op jit(solution)/shard_map/all_to_all | solution.py:60
  445.5 4.1 convolution_convert_fusion.2
  449.7 30.4 %all-to-all-done.6 = bf16[32,48,768]{2,1,0:T(8,128)(2,1)} async-done(((bf16[32,48,768]{2,1,0:T(8,128)(2,1)}), bf16[32,48,768]{2,1,0:T(8,128)(2,1)}, u32[]{:S(2)}, u32[]{:S(2)}) %all-to-all-start.6) | async-done | bytes 2359328 | tf_op jit(solution)/shard_map/all_to_all | solution.py:60
  480.1 13.9 %all-to-all-start.5 = ((bf16[32,48,1280]{2,1,0:T(8,128)(2,1)}), bf16[32,48,1280]{2,1,0:T(8,128)(2,1)}, u32[]{:S(2)}, u32[]{:S(2)}) async-start(bf16[32,48,1280]{2,1,0:T(8,128)(2,1)} %bitcast.102), calls=%async_computation.5 | async-start | bytes 7864320 | tf_op jit(solution)/shard_map/all_to_all | solution.py:60
  509.5 29.2 %collective-permute-done.13 = f32[2,1536]{1,0:T(2,128)S(1)} collective-permute-done((f32[2,1536]{1,0:T(2,128)S(1)}, f32[2,1536]{1,0:T(2,128)S(1)}, u32[]{:S(2)}, u32[]{:S(2)}) %collective-permute-start.13) | collective-permute-done | bytes 12320 | tf_op jit(solution)/shard_map/ppermute | solution.py:353
  539.0 4.4 collective-permute-start.17
  557.8 5.4 collective-permute-start.22
  575.6 12.7 %collective-permute-done.24 = bf16[48,768]{1,0:T(8,128)(2,1)S(1)} collective-permute-done((bf16[48,768]{1,0:T(8,128)(2,1)S(1)}, bf16[48,768]{1,0:T(8,128)(2,1)S(1)}, u32[]{:S(2)}, u32[]{:S(2)}) %collective-permute-start.24) | collective-permute-done | bytes 73760 | tf_op jit(solution)/shard_map/ppermute | solution.py:569
  589.1 5.2 collective-permute-start.30
  600.4 10.6 %collective-permute-done.30 = bf16[120,1536]{1,0:T(8,128)(2,1)S(1)} collective-permute-done((bf16[120,1536]{1,0:T(8,128)(2,1)S(1)}, bf16[120,1536]{1,0:T(8,128)(2,1)S(1)}, u32[]{:S(2)}, u32[]{:S(2)}) %collective-permute-start.30) | collective-permute-done | bytes 368672 | tf_op jit(solution)/shard_map/ppermute | solution.py:571
  (279 shorter events, 133.4 us)
Async XLA Ops:
  7.2 232.1 %all-gather.2.cloned.1.call-start = ((), (), s32[]{:S(2)}) async-start(), calls=%async_computation.8 | async-start | bytes 21307392 | tf_op jit(solution)/shard_map/all_gather | solution.py:443
  8.3 11.0 %collective-permute-start.2 = (bf16[48,3840]{1,0:T(8,128)(2,1)S(1)}, bf16[48,3840]{1,0:T(8,128)(2,1)S(1)}, u32[]{:S(2)}, u32[]{:S(2)}) collective-permute-start(bf16[48,3840]{1,0:T(8,128)(2,1)S(1)} %pad_maximum_fusion.13), channel_id=1, source_target_pairs={{0,1},{1,0},{2,3},{3,2},{4,5},{5,4},{6,7},{7,6},{8,9},{9,8},{10,11... | collective-permute-start | bytes 1105928 | tf_op jit(solution)/shard_map/ppermute | solution.py:364
  12.2 12.9 %collective-permute-start.3 = (bf16[168,1536]{1,0:T(8,128)(2,1)S(1)}, bf16[168,1536]{1,0:T(8,128)(2,1)S(1)}, u32[]{:S(2)}, u32[]{:S(2)}) collective-permute-start(bf16[168,1536]{1,0:T(8,128)(2,1)S(1)} %pad_maximum_fusion.12), channel_id=1, source_target_pairs={{0,0},{1,2},{2,4},{3,6},{4,8},{5,10},{6,12},{7,14},{8,16},{9,18},{... | collective-permute-start | bytes 1548296 | tf_op jit(solution)/shard_map/ppermute | solution.py:441
  29.7 76.6 %all-to-all-start = ((bf16[32,48,1408]{2,1,0:T(8,128)(2,1)}), bf16[32,48,1408]{2,1,0:T(8,128)(2,1)}, u32[]{:S(2)}, u32[]{:S(2)}) async-start(bf16[32,48,1408]{2,1,0:T(8,128)(2,1)} %broadcast_in_dim.46), calls=%async_computation | async-start | bytes 8650752 | tf_op jit(solution)/shard_map/all_to_all | solution.py:60
  116.7 50.0 %all-to-all-start.1 = ((bf16[32,3,96,128]{3,2,1,0:T(8,128)(2,1)}), bf16[32,3,96,128]{3,2,1,0:T(8,128)(2,1)S(1)}, u32[]{:S(2)}, u32[]{:S(2)}) async-start(bf16[32,3,96,128]{3,2,1,0:T(8,128)(2,1)} %bitcast.82), calls=%async_computation.1 | async-start | bytes 4718592 | tf_op jit(solution)/shard_map/all_to_all | solution.py:60
  190.5 51.7 %all-to-all-start.2 = ((bf16[32,3,32,128]{3,2,1,0:T(8,128)(2,1)}), bf16[32,3,32,128]{3,2,1,0:T(8,128)(2,1)}, u32[]{:S(2)}, u32[]{:S(2)}) async-start(bf16[32,3,32,128]{3,2,1,0:T(8,128)(2,1)} %get-tuple-element.19), calls=%async_computation.2 | async-start | bytes 1572864 | tf_op jit(solution)/shard_map/all_to_all | solution.py:60
  202.0 364.8 %reduce-scatter.2.cloned.1.call-start = ((), (), s32[]{:S(2)}) async-start(), calls=%async_computation.9 | async-start | bytes 18800640 | tf_op jit(solution)/shard_map/reduce_scatter | solution.py:542
  254.1 11.0 %collective-permute-start.5 = (bf16[192,1536]{1,0:T(8,128)(2,1)}, bf16[192,1536]{1,0:T(8,128)(2,1)}, u32[]{:S(2)}, u32[]{:S(2)}) collective-permute-start(bf16[192,1536]{1,0:T(8,128)(2,1)} %multiply_convert_fusion.5), channel_id=1, source_target_pairs={{0,32},{32,0},{1,33},{33,1},{2,34},{34,2},{3,35},{35,3},{4,36},{36... | collective-permute-start | bytes 1769480 | tf_op jit(solution)/shard_map/ppermute | solution.py:56
  254.4 19.0 %collective-permute-start.7 = (bf16[192,1536]{1,0:T(8,128)(2,1)}, bf16[192,1536]{1,0:T(8,128)(2,1)}, u32[]{:S(2)}, u32[]{:S(2)}) collective-permute-start(bf16[192,1536]{1,0:T(8,128)(2,1)} %bitcast.26), channel_id=1, source_target_pairs={{0,32},{32,0},{1,33},{33,1},{2,34},{34,2},{3,35},{35,3},{4,36},{36... | collective-permute-start | bytes 1769480 | tf_op jit(solution)/shard_map/ppermute | solution.py:56
  323.2 6.0 collective-permute-start.8
  388.0 43.9 %all-to-all-start.4 = ((bf16[32,3,96,128]{3,2,1,0:T(8,128)(2,1)}), bf16[32,3,96,128]{3,2,1,0:T(8,128)(2,1)S(1)}, u32[]{:S(2)}, u32[]{:S(2)}) async-start(bf16[32,3,96,128]{3,2,1,0:T(8,128)(2,1)} %copy-done.3), calls=%async_computation.4 | async-start | bytes 4718592 | tf_op jit(solution)/shard_map/all_to_all | solution.py:60
  431.8 48.3 %all-to-all-start.6 = ((bf16[32,48,768]{2,1,0:T(8,128)(2,1)}), bf16[32,48,768]{2,1,0:T(8,128)(2,1)}, u32[]{:S(2)}, u32[]{:S(2)}) async-start(bf16[32,48,768]{2,1,0:T(8,128)(2,1)} %bitcast.94), calls=%async_computation.7 | async-start | bytes 4718592 | tf_op jit(solution)/shard_map/all_to_all | solution.py:60
  480.1 70.5 %all-to-all-start.5 = ((bf16[32,48,1280]{2,1,0:T(8,128)(2,1)}), bf16[32,48,1280]{2,1,0:T(8,128)(2,1)}, u32[]{:S(2)}, u32[]{:S(2)}) async-start(bf16[32,48,1280]{2,1,0:T(8,128)(2,1)} %bitcast.102), calls=%async_computation.5 | async-start | bytes 7864320 | tf_op jit(solution)/shard_map/all_to_all | solution.py:60
  503.3 35.5 %collective-permute-start.13 = (f32[2,1536]{1,0:T(2,128)S(1)}, f32[2,1536]{1,0:T(2,128)S(1)}, u32[]{:S(2)}, u32[]{:S(2)}) collective-permute-start(f32[2,1536]{1,0:T(2,128)S(1)} %fusion.44), channel_id=1, source_target_pairs={{0,1},{64,65},{1,0},{65,64},{2,3},{66,67},{3,2},{67,66},{4,5},{68,... | collective-permute-start | bytes 36872 | tf_op jit(solution)/shard_map/ppermute | solution.py:353
  506.0 32.7 %collective-permute-start.14 = (f32[2,1536]{1,0:T(2,128)S(1)}, f32[2,1536]{1,0:T(2,128)S(1)}, u32[]{:S(2)}, u32[]{:S(2)}) collective-permute-start(f32[2,1536]{1,0:T(2,128)S(1)} %fusion.44), channel_id=1, source_target_pairs={{0,65},{64,0},{1,64},{65,1},{2,67},{66,2},{3,66},{67,3},{4,69},{68... | collective-permute-start | bytes 36872 | tf_op jit(solution)/shard_map/ppermute | solution.py:353
  506.0 32.9 %collective-permute-start.12 = (f32[2,1536]{1,0:T(2,128)S(1)}, f32[2,1536]{1,0:T(2,128)S(1)}, u32[]{:S(2)}, u32[]{:S(2)}) collective-permute-start(f32[2,1536]{1,0:T(2,128)S(1)} %fusion.44), channel_id=1, source_target_pairs={{0,64},{64,1},{1,65},{65,0},{2,66},{66,3},{3,67},{67,2},{4,68},{68... | collective-permute-start | bytes 36872 | tf_op jit(solution)/shard_map/ppermute | solution.py:353
  539.0 6.3 %collective-permute-start.17 = (f32[2,1536]{1,0:T(2,128)S(1)}, f32[2,1536]{1,0:T(2,128)S(1)}, u32[]{:S(2)}, u32[]{:S(2)}) collective-permute-start(f32[2,1536]{1,0:T(2,128)S(1)} %add_add_fusion.1), channel_id=1, source_target_pairs={{0,6},{2,0},{4,2},{6,4},{1,7},{3,1},{5,3},{7,5},{8,14},{10,8},{12,... | collective-permute-start | bytes 36872 | tf_op jit(solution)/shard_map/ppermute | solution.py:354
  543.4 4.0 collective-permute-start.16
  547.5 10.2 %collective-permute-start.20 = (f32[2,1536]{1,0:T(2,128)S(1)}, f32[2,1536]{1,0:T(2,128)S(1)}, u32[]{:S(2)}, u32[]{:S(2)}) collective-permute-start(f32[2,1536]{1,0:T(2,128)S(1)} %add_add_fusion), channel_id=1, source_target_pairs={{0,24},{8,0},{16,8},{24,16},{1,25},{9,1},{17,9},{25,17},{2,26},{10... | collective-permute-start | bytes 36872 | tf_op jit(solution)/shard_map/ppermute | solution.py:354
  547.6 10.1 %collective-permute-start.19 = (f32[2,1536]{1,0:T(2,128)S(1)}, f32[2,1536]{1,0:T(2,128)S(1)}, u32[]{:S(2)}, u32[]{:S(2)}) collective-permute-start(f32[2,1536]{1,0:T(2,128)S(1)} %add_add_fusion), channel_id=1, source_target_pairs={{0,16},{8,24},{16,0},{24,8},{1,17},{9,25},{17,1},{25,9},{2,18},{10... | collective-permute-start | bytes 36872 | tf_op jit(solution)/shard_map/ppermute | solution.py:354
  548.6 9.0 %collective-permute-start.18 = (f32[2,1536]{1,0:T(2,128)S(1)}, f32[2,1536]{1,0:T(2,128)S(1)}, u32[]{:S(2)}, u32[]{:S(2)}) collective-permute-start(f32[2,1536]{1,0:T(2,128)S(1)} %add_add_fusion), channel_id=1, source_target_pairs={{0,8},{8,16},{16,24},{24,0},{1,9},{9,17},{17,25},{25,1},{2,10},{10... | collective-permute-start | bytes 36872 | tf_op jit(solution)/shard_map/ppermute | solution.py:354
  553.4 4.4 collective-permute-start.21
  557.8 6.4 %collective-permute-start.22 = (bf16[48,1280]{1,0:T(8,128)(2,1)S(1)}, bf16[48,1280]{1,0:T(8,128)(2,1)S(1)}, u32[]{:S(2)}, u32[]{:S(2)}) collective-permute-start(bf16[48,1280]{1,0:T(8,128)(2,1)S(1)} %add_convert_fusion.3), channel_id=1, source_target_pairs={{0,32},{32,0},{1,33},{33,1},{2,34},{34,2},{3,35},{35,3},{4,36},{36... | collective-permute-start | bytes 368648 | tf_op jit(solution)/shard_map/ppermute | solution.py:56
  566.8 4.8 collective-permute-start.23
  569.9 18.4 %collective-permute-start.26 = (bf16[48,3840]{1,0:T(8,128)(2,1)S(1)}, bf16[48,3840]{1,0:T(8,128)(2,1)S(1)}, u32[]{:S(2)}, u32[]{:S(2)}) collective-permute-start(bf16[48,3840]{1,0:T(8,128)(2,1)S(1)} %constant_dynamic-slice_fusion.16), channel_id=1, source_target_pairs={{0,1},{1,0},{2,3},{3,2},{4,5},{5,4},{6,7},{7,6},{8,9},{9,8},{10,11... | collective-permute-start | bytes 1105928 | tf_op jit(solution)/shard_map/ppermute | solution.py:364
  571.6 16.6 %collective-permute-start.24 = (bf16[48,768]{1,0:T(8,128)(2,1)S(1)}, bf16[48,768]{1,0:T(8,128)(2,1)S(1)}, u32[]{:S(2)}, u32[]{:S(2)}) collective-permute-start(bf16[48,768]{1,0:T(8,128)(2,1)S(1)} %add_convert_fusion.4), channel_id=1, source_target_pairs={{0,0},{2,1},{4,2},{6,3},{8,4},{10,5},{12,6},{14,7},{16,8},{18,9},{... | collective-permute-start | bytes 221192 | tf_op jit(solution)/shard_map/ppermute | solution.py:569
  575.1 13.9 %collective-permute-start.29 = (bf16[120,1536]{1,0:T(8,128)(2,1)S(1)}, bf16[120,1536]{1,0:T(8,128)(2,1)S(1)}, u32[]{:S(2)}, u32[]{:S(2)}) collective-permute-start(bf16[120,1536]{1,0:T(8,128)(2,1)S(1)} %pad_maximum_fusion.14), channel_id=1, source_target_pairs={{0,64},{64,0},{1,65},{65,1},{2,66},{66,2},{3,67},{67,3},{4,68},{68... | collective-permute-start | bytes 1105928 | tf_op jit(solution)/shard_map/ppermute | solution.py:364
  588.2 11.4 %collective-permute-start.25 = (bf16[48,768]{1,0:T(8,128)(2,1)S(1)}, bf16[48,768]{1,0:T(8,128)(2,1)S(1)}, u32[]{:S(2)}, u32[]{:S(2)}) collective-permute-start(bf16[48,768]{1,0:T(8,128)(2,1)S(1)} %collective-permute-done.24), channel_id=1, source_target_pairs={{0,32},{32,0},{1,33},{33,1},{2,34},{34,2},{3,35},{35,3},{4,36},{36... | collective-permute-start | bytes 221192 | tf_op jit(solution)/shard_map/ppermute | solution.py:364
  588.3 9.7 %collective-permute-start.27 = (bf16[48,3840]{1,0:T(8,128)(2,1)S(1)}, bf16[48,3840]{1,0:T(8,128)(2,1)S(1)}, u32[]{:S(2)}, u32[]{:S(2)}) collective-permute-start(bf16[48,3840]{1,0:T(8,128)(2,1)S(1)} %add_convert_fusion.2), channel_id=1, source_target_pairs={{0,64},{64,0},{1,65},{65,1},{2,66},{66,2},{3,67},{67,3},{4,68},{68... | collective-permute-start | bytes 1105928 | tf_op jit(solution)/shard_map/ppermute | solution.py:364
  589.1 21.8 %collective-permute-start.30 = (bf16[120,1536]{1,0:T(8,128)(2,1)S(1)}, bf16[120,1536]{1,0:T(8,128)(2,1)S(1)}, u32[]{:S(2)}, u32[]{:S(2)}) collective-permute-start(bf16[120,1536]{1,0:T(8,128)(2,1)S(1)} %add_convert_fusion), channel_id=1, source_target_pairs={{0,0},{2,1},{4,2},{6,3},{8,4},{10,5},{12,6},{14,7},{16,8},{18,9},{... | collective-permute-start | bytes 1105928 | tf_op jit(solution)/shard_map/ppermute | solution.py:571
  598.2 16.2 %collective-permute-start.28 = (bf16[48,3840]{1,0:T(8,128)(2,1)S(1)}, bf16[48,3840]{1,0:T(8,128)(2,1)S(1)}, u32[]{:S(2)}, u32[]{:S(2)}) collective-permute-start(bf16[48,3840]{1,0:T(8,128)(2,1)S(1)} %add_convert_fusion.1), channel_id=1, source_target_pairs={{0,32},{32,0},{1,33},{33,1},{2,34},{34,2},{3,35},{35,3},{4,36},{36... | collective-permute-start | bytes 1105928 | tf_op jit(solution)/shard_map/ppermute | solution.py:56
  610.9 5.3 collective-permute-start.31
  (55 other events, 416.2 us)
Sparse Core Ops, SparseCore 0:
  26.6 212.6 all-gather.1
  314.5 173.3 reduce-scatter.1

commit v3 on v2

--- a/solution.py
+++ b/solution.py
@@ -27,6 +27,15 @@
 HK = HALF_KV * HD
 HF = FF // 2
 QKV = HQ + 2 * HK
+UNIT_FF = 128
+PAD_FF = 16 * UNIT_FF
+REST_AT = D
+GATE_AT = D + D // 3
+UP_AT = GATE_AT + PAD_FF
+OUT_AT = UP_AT + PAD_FF
+FF_TILE = 256
+FF_TILES = PAD_FF // FF_TILE
+FF_ROWS = 96 * FF_TILE // UNIT_FF
 CHUNK = SPAN // PARTS
 TILE = 4
 TILES = SHARDS // TILE
@@ -116,7 +125,12 @@
     return jnp.where(lane < HD, pair_even, pair_odd)
 
 
-def out_kernel(u_ref, left_ref, right_ref, attn_ref, mine_ref, other_ref):
+def out_halves(ref):
+    whole = ref[...].reshape(16, 2, 48, D // 2)
+    return whole[:, 0].reshape(HQ, D // 2), whole[:, 1].reshape(HQ, D // 2)
+
+
+def out_kernel(u_ref, w_ref, attn_ref, mine_ref, other_ref):
     for o in range(2):
         for m in range(MB):
             for p in range(PARTS):
@@ -130,15 +144,23 @@
                 at = (o * MB + m) * SPAN + p * CHUNK
                 attn_ref[at : at + CHUNK, :] = jnp.concatenate(parts, axis=1)
     attn = attn_ref[...]
-    for k, w_ref in enumerate((left_ref, right_ref)):
-        result = product(attn, w_ref[...])
+    for k, half in enumerate(out_halves(w_ref)):
+        result = product(attn, half)
         cols = slice(k * (D // 2), (k + 1) * (D // 2))
         mine_ref[:, cols] = result[:ROWS]
         other_ref[:, cols] = result[ROWS:].astype(jnp.bfloat16)
 
 
-def d_out_kernel(da_ref, left_ref, right_ref, out_ref):
-    rows = product_t(da_ref[:, : D // 2], left_ref[...]) + product_t(da_ref[:, D // 2 :], right_ref[...])
+def d_out_kernel(da_ref, w_ref, attn_ref, held_ref, out_ref, grad_ref, g_out, sem):
+    attn_t = attn_ref[...].T
+    for k in range(2):
+        half = product(attn_t, da_ref[:, k * (D // 2) : (k + 1) * (D // 2)]).astype(jnp.bfloat16)
+        for j in range(16):
+            g_out[j * 96 + k * 48 : j * 96 + k * 48 + 48, :] = half[j * 48 : j * 48 + 48]
+    copy = pltpu.make_async_copy(g_out, grad_ref.at[:, pl.ds(OUT_AT, D // 2)], sem)
+    copy.start()
+    left, right = out_halves(w_ref)
+    rows = product_t(da_ref[:, : D // 2], left) + product_t(da_ref[:, D // 2 :], right)
     rows = rows.astype(jnp.bfloat16)
     for j in range(HALF_KV):
         first = rows[:, 192 * j : 192 * j + 128]
@@ -150,6 +172,7 @@
                     at = (o * MB + m) * SPAN + p * CHUNK
                     out_ref[j, o, p, m, :CHUNK, :] = first[at : at + CHUNK]
                     out_ref[j, o, p, m, CHUNK:, :] = third[at : at + CHUNK]
+    copy.wait()
 
 
 def collect_kernel(u_ref, table_ref, out_ref):
@@ -292,28 +315,163 @@
 
 def project(n1, w_qkv, tables):
     shape = low_shape(HALF_KV, 2, PARTS, MB, ALL_ROWS, 128)
-    out = pl.pallas_call(project_kernel, out_shape=shape, compiler_params=PARAMS, name="project")(n1, w_qkv, tables)
+    out = pl.pallas_call(project_kernel, out_shape=shape, compiler_params=PARAMS, cost_estimate=cost(6), name="project")(n1, w_qkv, tables)
     return out.reshape(SHARDS, MB, ALL_ROWS, 128)
 
 
-def out_project(units, w_o):
+def whole_spec(*dims):
+    return pl.BlockSpec(dims, lambda i: (0,) * len(dims))
+
+
+OUT_SPEC = pl.BlockSpec((D, D // 2), lambda i: (0, OUT_AT // (D // 2)))
+
+
+def cost(micros):
+    return pl.CostEstimate(flops=int(micros * 1e9), bytes_accessed=1 << 20, transcendentals=0)
+
+
+def out_project(units, w_all):
     return pl.pallas_call(
         out_kernel,
+        grid=(1,),
+        in_specs=[whole_spec(HALF_KV, 2, PARTS, MB, Q_ROWS, 128), OUT_SPEC],
+        out_specs=[whole_spec(BOTH, HQ), whole_spec(ROWS, D), whole_spec(ROWS, D)],
         out_shape=[low_shape(BOTH, HQ), jax.ShapeDtypeStruct((ROWS, D), jnp.float32), low_shape(ROWS, D)],
         compiler_params=PARAMS,
+        cost_estimate=cost(3),
         name="out_project",
-    )(split_units(units), *w_o)
-
-
-def d_out_project(da, w_o):
-    shape = low_shape(HALF_KV, 2, PARTS, MB, Q_ROWS, 128)
-    out = pl.pallas_call(d_out_kernel, out_shape=shape, compiler_params=PARAMS, name="d_out_project")(da, *w_o)
-    return out.reshape(SHARDS, MB, Q_ROWS, 128)
+    )(split_units(units), w_all)
+
+
+def d_out_project(da, w_all, attn, g_ffn):
+    dims = (HALF_KV, 2, PARTS, MB, Q_ROWS, 128)
+    anywhere = pl.BlockSpec(memory_space=pl.ANY)
+    out, grads = pl.pallas_call(
+        d_out_kernel,
+        grid=(1,),
+        in_specs=[whole_spec(BOTH, D), OUT_SPEC, whole_spec(BOTH, HQ), anywhere],
+        out_specs=[whole_spec(*dims), anywhere],
+        out_shape=[low_shape(*dims), low_shape(*g_ffn.shape)],
+        scratch_shapes=[pltpu.VMEM((D, D // 2), jnp.bfloat16), pltpu.SemaphoreType.DMA],
+        input_output_aliases={3: 1},
+        compiler_params=PARAMS,
+        cost_estimate=cost(5),
+        name="d_out_project",
+    )(da, w_all, attn, g_ffn)
+    return out.reshape(SHARDS, MB, Q_ROWS, 128), grads
+
+
+def ffn_kernel(
+    n_ref, df_ref, main_ref, rest_ref, gate_ref, up_ref,
+    y_mine_ref, y_other_ref, dn_mine_ref, dn_other_ref, grad_ref,
+    n_t, y_acc, dn_acc, g_gate, g_up, g_main, g_rest, sems,
+):
+    step = pl.program_id(0)
+    slot = lax.rem(step, 2)
+
+    def copies(at, slot):
+        cols, rows = at * FF_TILE, at * FF_ROWS
+        return [
+            pltpu.make_async_copy(
+                g_gate.at[slot], grad_ref.at[:, pl.ds(pl.multiple_of(GATE_AT + cols, FF_TILE), FF_TILE)], sems.at[slot, 0]
+            ),
+            pltpu.make_async_copy(
+                g_up.at[slot], grad_ref.at[:, pl.ds(pl.multiple_of(UP_AT + cols, FF_TILE), FF_TILE)], sems.at[slot, 1]
+            ),
+            pltpu.make_async_copy(
+                g_main.at[slot], grad_ref.at[pl.ds(pl.multiple_of(rows, 64), FF_ROWS), pl.ds(0, D)], sems.at[slot, 2]
+            ),
+            pltpu.make_async_copy(
+                g_rest.at[slot],
+                grad_ref.at[pl.ds(pl.multiple_of(rows, 64), FF_ROWS), pl.ds(REST_AT, D // 3)],
+                sems.at[slot, 3],
+            ),
+        ]
+
+    @pl.when(step == 0)
+    def _():
+        n_t[...] = n_ref[...].T
+        y_acc[...] = jnp.zeros_like(y_acc)
+        dn_acc[...] = jnp.zeros_like(dn_acc)
+
+    @pl.when(step >= 2)
+    def _():
+        for copy in copies(step - 2, slot):
+            copy.wait()
+
+    low = jnp.bfloat16
+    units = []
+    for j in range(FF_TILE // UNIT_FF):
+        rest = [rest_ref[j * 96 + q * 32 : j * 96 + q * 32 + 32, :] for q in range(3)]
+        units += [main_ref[j * 96 : j * 96 + 96, :], jnp.concatenate(rest, axis=1)]
+    w_down = jnp.concatenate(units, axis=0)
+    rows, df = n_ref[...], df_ref[...]
+    gate, up = product(rows, gate_ref[...]), product(rows, up_ref[...])
+    sigma = jax.nn.sigmoid(gate)
+    silu = gate * sigma
+    act = (silu * up).astype(low)
+    d_act = product_t(df, w_down)
+    d_gate = (d_act * up * sigma * (1.0 + gate * (1.0 - sigma))).astype(low)
+    d_up = (d_act * silu).astype(low)
+    y_acc[...] += product(act, w_down)
+    dn_acc[...] += product_t(d_gate, gate_ref[...]) + product_t(d_up, up_ref[...])
+    g_gate[slot] = product(n_t[...], d_gate).astype(low)
+    g_up[slot] = product(n_t[...], d_up).astype(low)
+    g_down = product(act.T, df).astype(low)
+    for j in range(FF_TILE // UNIT_FF):
+        g_main[slot, j * 96 : j * 96 + 96, :] = g_down[j * UNIT_FF : j * UNIT_FF + 96]
+        for q in range(3):
+            g_rest[slot, j * 96 + q * 32 : j * 96 + q * 32 + 32, :] = g_down[
+                j * UNIT_FF + 96 : (j + 1) * UNIT_FF, q * (D // 3) : (q + 1) * (D // 3)
+            ]
+    for copy in copies(step, slot):
+        copy.start()
+
+    @pl.when(step == FF_TILES - 1)
+    def _():
+        y_mine_ref[...] = y_acc[:ROWS]
+        y_other_ref[...] = y_acc[ROWS:].astype(low)
+        dn_mine_ref[...] = dn_acc[:ROWS]
+        dn_other_ref[...] = dn_acc[ROWS:].astype(low)
+        for back in (1, 0):
+            for copy in copies(step - back, lax.rem(step - back, 2)):
+                copy.wait()
+
+
+def feed_forward(n2, df, w_all):
+    wide = jax.ShapeDtypeStruct((ROWS, D), jnp.float32)
+    return pl.pallas_call(
+        ffn_kernel,
+        grid=(FF_TILES,),
+        in_specs=[
+            whole_spec(BOTH, D),
+            whole_spec(BOTH, D),
+            pl.BlockSpec((FF_ROWS, D), lambda t: (t, 0)),
+            pl.BlockSpec((FF_ROWS, D // 3), lambda t: (t, REST_AT // (D // 3))),
+            pl.BlockSpec((D, FF_TILE), lambda t: (0, GATE_AT // FF_TILE + t)),
+            pl.BlockSpec((D, FF_TILE), lambda t: (0, UP_AT // FF_TILE + t)),
+        ],
+        out_specs=[whole_spec(ROWS, D)] * 4 + [pl.BlockSpec(memory_space=pl.ANY)],
+        out_shape=[wide, low_shape(ROWS, D), wide, low_shape(ROWS, D), low_shape(D, OUT_AT + D // 2)],
+        scratch_shapes=[
+            pltpu.VMEM((D, BOTH), jnp.bfloat16),
+            pltpu.VMEM((BOTH, D), jnp.float32),
+            pltpu.VMEM((BOTH, D), jnp.float32),
+            pltpu.VMEM((2, D, FF_TILE), jnp.bfloat16),
+            pltpu.VMEM((2, D, FF_TILE), jnp.bfloat16),
+            pltpu.VMEM((2, FF_ROWS, D), jnp.bfloat16),
+            pltpu.VMEM((2, FF_ROWS, D // 3), jnp.bfloat16),
+            pltpu.SemaphoreType.DMA((2, 4)),
+        ],
+        compiler_params=PARAMS,
+        cost_estimate=cost(30),
+        name="feed_forward",
+    )(n2, df, w_all, w_all, w_all, w_all)
 
 
 def collect(units, tables):
     shape = low_shape(BOTH, HQ + 2 * HK)
-    return pl.pallas_call(collect_kernel, out_shape=shape, compiler_params=PARAMS, name="collect")(
+    return pl.pallas_call(collect_kernel, out_shape=shape, compiler_params=PARAMS, cost_estimate=cost(4), name="collect")(
         split_units(units), tables
     )
 
@@ -326,6 +484,7 @@
         out_specs=[QUERY_SPEC, COL_SPEC],
         out_shape=[low_shape(SHARDS, MB, Q_ROWS, 128), COL_SHAPE],
         compiler_params=PARAMS,
+        cost_estimate=cost(20),
         name="attend_forward",
     )(unit, first, units, starts)
 
@@ -339,6 +498,7 @@
         out_shape=low_shape(SHARDS, MB, ALL_ROWS, 128),
         scratch_shapes=[pltpu.VMEM((SEQ, 128), jnp.float32)],
         compiler_params=PARAMS,
+        cost_estimate=cost(27),
         name="attend_backward",
     )(unit, first, units, starts, d_mixed, lse)
 
@@ -369,6 +529,14 @@
     return lax.dynamic_slice_in_dim(local, core * half, half, axis=1)
 
 
+def pad_units(local):
+    return jnp.pad(local.reshape(-1, 16, 120), ((0, 0), (0, 0), (0, UNIT_FF - 120))).reshape(-1, PAD_FF)
+
+
+def crop_units(local):
+    return local.reshape(-1, 16, UNIT_FF)[:, :, :120].reshape(-1, HF)
+
+
 def fold(rows, parts):
     n, r, w = rows.shape
     return rows.reshape(n, r, parts, w // parts).transpose(0, 2, 1, 3).reshape(n, parts * r, w // parts)
@@ -394,12 +562,24 @@
     return values + shift(values, axis, 1) + shift(values, axis, 2) + shift(values, axis, 3)
 
 
-def reduce_pair(values, axis, dim):
-    size = values.shape[dim] // 2
-    me = lax.axis_index(axis)
-    keep = lax.dynamic_slice_in_dim(values, me * size, size, axis=dim)
-    send = lax.dynamic_slice_in_dim(values, (1 - me) * size, size, axis=dim)
-    return wide_sum(keep, flip(send, axis))
+def reduce_x(values):
+    size = values.shape[0] // 2
+    me = lax.axis_index("xh")
+    keep = lax.dynamic_slice_in_dim(values, me * size, size, axis=0)
+    send = lax.dynamic_slice_in_dim(values, (1 - me) * size, size, axis=0)
+    cross = lax.ppermute(send, ("xl", "xh"), [(i, 3 - i) for i in range(4)])
+    return wide_sum(keep, flip(keep, "xl"), flip(send, "xh"), cross)
+
+
+def return_rows(rows, a, b):
+    pairs = []
+    for xl in range(2):
+        for c in range(2):
+            for j in range(16):
+                for xh in range(2):
+                    source = ((xl * 2 + c) * 16 + j) * 2 + xh
+                    pairs.append((source, ((xl ^ b) * 2 + (xh ^ a)) * SHARDS + 16 * c + j))
+    return lax.ppermute(rows, ("xl", "c") + SHARD, pairs)
 
 
 def add_pair(values, axis):
@@ -439,13 +619,13 @@
     low = jnp.bfloat16
 
     rows_in = lax.ppermute(jnp.concatenate([w_out, w_down], axis=0), ("c",) + SHARD, piece_perm())
-    gu_piece = jnp.concatenate([col_half(core, w_gate), col_half(core, w_up)], axis=1)
+    gu_piece = jnp.concatenate([pad_units(col_half(core, w_gate)), pad_units(col_half(core, w_up))], axis=1)
     w_all = lax.all_gather(
         jnp.concatenate(
             [
+                rows_in[48:144],
+                fold(jnp.pad(rows_in[144:], ((0, 8), (0, 0)))[None], 3)[0],
                 join_pair(gu_piece, "xh", 0),
-                rows_in[48:144],
-                fold(rows_in[144:][None], 4)[0],
                 fold(rows_in[:48][None], 2)[0],
             ],
             axis=1,
@@ -454,13 +634,6 @@
         axis=0,
         tiled=True,
     )
-    w_gu = w_all[:, :FF]
-    w_d = jnp.concatenate(
-        [w_all[:, FF : FF + D].reshape(16, 96, D), unfold(w_all[:, FF + D : FF + 5 * D // 4].reshape(16, 96, D // 4), 4)],
-        axis=1,
-    ).reshape(HF, D)
-    w_o = w_all[:, FF + 5 * D // 4 :].reshape(16, 2, 48, D // 2)
-    w_o = [w_o[:, k].reshape(HQ, D // 2) for k in range(2)]
     small = jnp.concatenate(
         [norm_attn[:, None], norm_ffn[:, None], doc_ids.reshape(48, 4).astype(low), jnp.zeros((48, 122), low)], axis=1
     )
@@ -515,43 +688,26 @@
     n1 = (x_both * r1_both * gain_attn).astype(low)
     units = exchange(project(n1, w_first, tables))
     unit_o, lse = attend_fwd(unit, first, units, starts)
-    attn, y1_mine, y1_other = out_project(exchange(unit_o), w_o)
+    attn, y1_mine, y1_other = out_project(exchange(unit_o), w_all)
     hmid = x + branch_scale * (y1_mine + swap(y1_other).astype(jnp.float32))
 
     r2 = lax.rsqrt(jnp.mean(hmid * hmid, axis=-1, keepdims=True) + eps_norm)
     z2 = hmid * r2
     n2_mine = (z2 * gain_ffn).astype(low)
     n2 = jnp.concatenate([n2_mine, swap(n2_mine)], axis=0)
-    gu = product(n2, w_gu)
-    gate, up = gu[:, :HF], gu[:, HF:]
-    sigma = jax.nn.sigmoid(gate)
-    silu = gate * sigma
-    act = (silu * up).astype(low)
-    y2 = product(act, w_d)
-    result = hmid + branch_scale * (y2[:ROWS] + swap(y2[ROWS:].astype(low)).astype(jnp.float32))
-
-    d_act = product_t(df, w_d)
-    d_gate = (d_act * up * sigma * (1.0 + gate * (1.0 - sigma))).astype(low)
-    d_up = (d_act * silu).astype(low)
-    d_gu = jnp.concatenate([d_gate, d_up], axis=1)
-    g_down = t_product(act, df).astype(low).reshape(16, 120, D)
-    g_ffn = jnp.concatenate(
-        [t_product(n2, d_gu).astype(low), g_down[:, :96].reshape(D, D), fold(g_down[:, 96:], 4).reshape(D, D // 4)],
-        axis=1,
-    )
-    s_ffn = lax.psum_scatter(g_ffn, ("z", "y"), scatter_dimension=0, tiled=True)
-    dn2_both = product_t(d_gu, w_gu)
-    dn2 = dn2_both[:ROWS] + swap(dn2_both[ROWS:].astype(low)).astype(jnp.float32)
+    y2_mine, y2_other, dn2_mine, dn2_other, g_ffn = feed_forward(n2, df, w_all)
+    result = hmid + branch_scale * (y2_mine + swap(y2_other).astype(jnp.float32))
+
+    dn2 = dn2_mine + swap(dn2_other).astype(jnp.float32)
     e2 = dn2 * gain_ffn
     g_gain_ffn = jnp.sum(dn2 * z2, axis=0)
     dh = dy + r2 * (e2 - z2 * jnp.mean(e2 * z2, axis=-1, keepdims=True))
 
     da_mine = (branch_scale * dh).astype(low)
     da = jnp.concatenate([da_mine, swap(da_mine)], axis=0)
-    unit_do = exchange(d_out_project(da, w_o))
-    g_o = [t_product(attn, da[:, k * (D // 2) : (k + 1) * (D // 2)]).astype(low) for k in range(2)]
-    g_o = jnp.stack([g.reshape(16, 48, D // 2) for g in g_o], axis=1).reshape(SHARDS, 48, D // 2)
-    s_o = scatter_sum(after(g_o, unit_do))
+    unit_do, g_all = d_out_project(da, w_all, attn, g_ffn)
+    s_all = lax.psum_scatter(g_all, ("z", "y"), scatter_dimension=0, tiled=True)
+    unit_do = exchange(unit_do)
     unit_d = attend_bwd(unit, first, units, starts, unit_do, lse)
     d_qkv = collect(exchange(unit_d), tables)
 
@@ -564,23 +720,28 @@
     g_gain_attn = jnp.sum(dn1 * z1, axis=0)
     grad_in = (dh + r1 * (e1 - z1 * jnp.mean(e1 * z1, axis=-1, keepdims=True))).astype(low)
 
-    s_ffn, s_o = after((s_ffn, s_o), d_qkv)
-    back = [(b, a) for a, b in piece_perm()]
-    s_o = join_cores(lax.ppermute(add_pair(s_o, "xl"), ("c",) + SHARD, back))
-    s_d = jnp.concatenate([s_ffn[:, FF : FF + D], unfold(s_ffn[None, :, FF + D :], 4)[0]], axis=0)
-    s_d = lax.ppermute(add_pair(s_d, "xl"), ("c",) + SHARD, back)
-    s_d = s_d.astype(jnp.float32) + swap(s_d).astype(jnp.float32)
-    s_gu = add_pair(reduce_pair(s_ffn[:, :FF], "xh", 0), "xl")
+    gains = jnp.stack([g_gain_attn, g_gain_ffn])
+    gains = gains + swap(gains)
+    gains = total_axis(total_axis(total_axis(gains, "x"), "y"), "z")
+    gains = lax.dynamic_slice_in_dim(gains, shard * 48, 48, axis=1)
+    s_all = after(s_all, gains)
+    rows = jnp.concatenate(
+        [
+            unfold(s_all[None, :, OUT_AT:], 2)[0],
+            s_all[:, :D],
+            unfold(s_all[None, :, REST_AT:GATE_AT], 3)[0][:24],
+        ],
+        axis=0,
+    )
+    rows = sum(return_rows(rows, a, b).astype(jnp.float32) for a in range(2) for b in range(2))
+    s_gu = reduce_x(s_all[:, GATE_AT:OUT_AT])
+    s_gu = jnp.concatenate([crop_units(s_gu[:, :PAD_FF]), crop_units(s_gu[:, PAD_FF:])], axis=1)
     other = swap(s_gu)
     lower = core == 0
     g_g, g_u = [
         jnp.concatenate([jnp.where(lower, m, t), jnp.where(lower, t, m)], axis=1).astype(jnp.float32)
         for m, t in ((s_gu[:, :HF], other[:, :HF]), (s_gu[:, HF:], other[:, HF:]))
     ]
-    gains = jnp.stack([g_gain_attn, g_gain_ffn])
-    gains = gains + swap(gains)
-    gains = total_axis(total_axis(total_axis(gains, "x"), "y"), "z")
-    gains = lax.dynamic_slice_in_dim(gains, shard * 48, 48, axis=1)
     s_qkv = add_pair(s_qkv, "xl")
     other = swap(s_qkv)
     whole = [jnp.where(lower, s_qkv, other), jnp.where(lower, other, s_qkv)]
@@ -597,11 +758,11 @@
         jnp.concatenate([from_groups(w[:, :HQ]) for w in whole], axis=1).astype(jnp.float32),
         heads_of(0),
         heads_of(HD),
-        s_o,
+        rows[:48],
         gains[1],
         g_g,
         g_u,
-        s_d,
+        rows[48:],
     )
 
 

time: 632 us -> 640 us (1.013)
  blocking collectives: 21.9 us -> 95.1 us
  matrix products: 53 us -> 8.08 us
  starting transfers between devices: 127 us -> 85.7 us
  Pallas kernels: 58.4 us -> 93.4 us
  other arithmetic: 49.5 us -> 29.9 us
  waiting for transfers between devices: 259 us -> 278 us
  local copies, waits for them, and re-layouts: 40.3 us -> 22.6 us
    all_to_all x1 -> x3, blocking collectives: 21.9 us -> 95.1 us  [exchange(): return lax.all_to_all(values, SHARD, 0, 0, tiled=True)]
    all_to_all x6 -> x3, waiting for transfers between devices: 148 us -> 89.6 us  [exchange(): return lax.all_to_all(values, SHARD, 0, 0, tiled=True)]
    ppermute x2 -> x5, waiting for transfers between devices: 23.2 us -> 65.4 us  [the longest x4 65.4 us: return_rows(): return lax.ppermute(rows, ('xl', 'c') + SHARD, pairs)]
    all_to_all x6 -> x3, starting transfers between devices: 72.7 us -> 34.6 us  [exchange(): return lax.all_to_all(values, SHARD, 0, 0, tiled=True)]
    pallas_call x4 -> x5, Pallas kernels: 11.1 us -> 45.7 us  [the longest x1 30.4 us: feed_forward(): pl.pallas_call(ffn_kernel, grid=(FF_TILES,), in_specs=[whole_spec(BOTH, D...]
    reduce_scatter x1, waiting for transfers between devices: 0.01 us -> 21.1 us  [on_device(): s_all = lax.psum_scatter(g_all, ('z', 'y'), scatter_dimension=0, tiled=True)]
    dot_general x5 -> x1, matrix products: 20.5 us -> 4.17 us  [t_product(): lax.dot_general(left, right, (((0,), (0,)), ((), ())), preferred_element_...]
    dot_general x3 -> x1, matrix products: 19 us -> 3.91 us  [product_t(): lax.dot_general(left, right, (((1,), (1,)), ((), ())), preferred_element_...]
  transfers between devices with their start and end apart: 40 -> 36, of which waited for: 21 -> 25; matrix products, arithmetic and copies ran while one was open for 13% -> 7% of each run, Pallas kernels for 9% -> 9%
where the time goes in v3:
time: 640 us; the launch traced here: 627 us
  waiting for transfers between devices  278 us (43%)
  blocking collectives  95.1 us (15%)
  Pallas kernels  93.4 us (15%)
  starting transfers between devices  85.7 us (13%)
  other arithmetic  29.9 us (5%)
  local copies, waits for them, and re-layouts  22.6 us (4%)
  between operations  15 us (2%)
  matrix products  8.08 us (1%)
    all_to_all x3, blocking collectives, exchange(): return lax.all_to_all(values, SHARD, 0, 0, tiled=True)  95.1 us
    all_to_all x3, waiting for transfers between devices, exchange(): return lax.all_to_all(values, SHARD, 0, 0, tiled=True)  89.6 us
    ppermute x4, waiting for transfers between devices, return_rows(): return lax.ppermute(rows, ('xl', 'c') + SHARD, pairs)  65.4 us
    all_to_all x3, starting transfers between devices, exchange(): return lax.all_to_all(values, SHARD, 0, 0, tiled=True)  34.6 us
    all_gather x1, waiting for transfers between devices, on_device(): lax.all_gather(jnp.concatenate([rows_in[48:144], fold(jnp.pad(rows_in[144...  30.9 us
    pallas_call x1, Pallas kernels, feed_forward(): pl.pallas_call(ffn_kernel, grid=(FF_TILES,), in_specs=[whole_spec(BOTH, D...  30.4 us
    ppermute x3, waiting for transfers between devices, shift(): lax.ppermute(values, ('xl', 'xh'), [(line(i), line((i + step) % 4)) for i...  30.1 us
    pallas_call x1, Pallas kernels, attend_bwd(): pl.pallas_call(bwd_kernel, grid=(MB,), in_specs=[SMEM, SMEM, UNIT_SPEC, C...  28.1 us
  transfers between devices with their start and end apart: 36, of which 25 were waited for; matrix products, arithmetic and copies ran while one was open for 7% of the time, Pallas kernels for 9%

profile of v3, /device:TPU:49, one launch (start us, length us, event | category | flops | bytes accessed | tf_op | source)
XLA Modules:
  0.0 627.5 jit_solution(1240580059428806421)
XLA Ops:
  12.2 5.2 collective-permute-start.2
  17.4 3.5 collective-permute-done.3
  21.0 5.7 collective-permute-done.2
  32.0 11.7 %all-to-all-start = ((bf16[32,48,1408]{2,1,0:T(8,128)(2,1)}), bf16[32,48,1408]{2,1,0:T(8,128)(2,1)}, u32[]{:S(2)}, u32[]{:S(2)}) async-start(bf16[32,48,1408]{2,1,0:T(8,128)(2,1)} %broadcast_in_dim.46), calls=%async_computation | async-start | bytes 8650752 | tf_op jit(solution)/shard_map/all_to_all | solution.py:69
  46.7 62.5 %all-to-all-done = bf16[32,48,1408]{2,1,0:T(8,128)(2,1)} async-done(((bf16[32,48,1408]{2,1,0:T(8,128)(2,1)}), bf16[32,48,1408]{2,1,0:T(8,128)(2,1)}, u32[]{:S(2)}, u32[]{:S(2)}) %all-to-all-start) | async-done | bytes 4325408 | tf_op jit(solution)/shard_map/all_to_all | solution.py:69
  111.4 6.0 project.1
  118.9 12.0 %all-to-all-start.1 = ((bf16[32,3,96,128]{3,2,1,0:T(8,128)(2,1)}), bf16[32,3,96,128]{3,2,1,0:T(8,128)(2,1)S(1)}, u32[]{:S(2)}, u32[]{:S(2)}) async-start(bf16[32,3,96,128]{3,2,1,0:T(8,128)(2,1)} %bitcast.69), calls=%async_computation.1 | async-start | bytes 4718592 | tf_op jit(solution)/shard_map/all_to_all | solution.py:69
  135.2 5.8 convert_reduce_fusion
  141.7 27.2 %all-to-all-done.1.u_ref = bf16[32,3,96,128]{3,2,1,0:T(8,128)(2,1)S(1)} async-done(((bf16[32,3,96,128]{3,2,1,0:T(8,128)(2,1)}), bf16[32,3,96,128]{3,2,1,0:T(8,128)(2,1)S(1)}, u32[]{:S(2)}, u32[]{:S(2)}) %all-to-all-start.1) | async-done | bytes 2359328 | tf_op jit(solution)/shard_map/all_to_all | solution.py:69
  171.3 19.6 %attend_forward.1 = (bf16[32,3,32,128]{3,2,1,0:T(8,128)(2,1)S(1)}, f32[3,8,192,128]{3,2,1,0:T(8,128)S(1)}) custom-call(s32[2]{0:T(128)S(1)} %pad_add_fusion.unit_ref, s32[24]{0:T(128)S(1)} %and_select_fusion.first_ref, bf16[32,3,96,128]{3,2,1,0:T(8,128)(2,1)S(1)} %all-to-all-done.1.u_ref, s32[3,8,192,128]{3,2,1,0:T(8,128)} %broadcast_in_dim.52.start_ref), custom_call_target="tpu_custom_call" | custom-call | flops 20000000000 | bytes 1048576 | tf_op jit(solution)/shard_map/attend_forward/pallas_call | solution.py:480
  192.3 23.8 %all_to_all.30 = bf16[32,3,32,128]{3,2,1,0:T(8,128)(2,1)S(1)} all-to-all(bf16[32,3,32,128]{3,2,1,0:T(8,128)(2,1)S(1)} %get-tuple-element.24), channel_id=1, replica_groups=mesh['xl'=2,'c'=2,'z'=4,'y'=4,'xh'=2] {'z','y','xh'}, dimensions={0} | all-to-all | bytes 1572864 | tf_op jit(solution)/shard_map/all_to_all | solution.py:69
  216.1 30.9 %all-gather.2.cloned.1.call-done.w_ref.main_ref.rest_ref.gate_ref.up_ref = bf16[1536,6912]{1,0:T(8,128)(2,1)} async-done(((bf16[96,6912]{1,0:T(8,128)(2,1)}), bf16[1536,6912]{1,0:T(8,128)(2,1)}) %all-gather.2.cloned.1.call-update) | async-done | bytes 21233680 | tf_op jit(solution)/shard_map/all_gather | solution.py:623
  247.0 3.6 out_project.1
  259.6 30.4 %feed_forward.1 = (f32[192,1536]{1,0:T(8,128)S(1)}, bf16[192,1536]{1,0:T(8,128)(2,1)S(1)}, f32[192,1536]{1,0:T(8,128)S(1)}, bf16[192,1536]{1,0:T(8,128)(2,1)S(1)}, bf16[1536,6912]{1,0:T(8,128)(2,1)}) custom-call(bf16[384,1536]{1,0:T(8,128)(2,1)S(1)} %pad_maximum_fusion.2.n_ref, bf16[384,1536]{1,0:T(8,128)(2,1)S(1)} %multiply_convert_fusion.df_ref, ...), custom_call_target="tpu_custom_call" | custom-call | flops 30000001024 | bytes 1048576 | tf_op jit(solution)/shard_map/feed_forward/pallas_call | solution.py:443
  298.1 4.9 d_out_project.1
  303.0 22.3 %all_to_all.31.do_ref = bf16[32,3,32,128]{3,2,1,0:T(8,128)(2,1)S(1)} all-to-all(bf16[32,3,32,128]{3,2,1,0:T(8,128)(2,1)S(1)} %bitcast.71), channel_id=1, replica_groups=mesh['xl'=2,'c'=2,'z'=4,'y'=4,'xh'=2] {'z','y','xh'}, dimensions={0} | all-to-all | bytes 1572864 | tf_op jit(solution)/shard_map/all_to_all | solution.py:69
  325.3 28.1 %attend_backward.1 = bf16[32,3,96,128]{3,2,1,0:T(8,128)(2,1)S(1)} custom-call(s32[2]{0:T(128)S(1)} %pad_add_fusion.unit_ref, s32[24]{0:T(128)S(1)} %and_select_fusion.first_ref, bf16[32,3,96,128]{3,2,1,0:T(8,128)(2,1)S(1)} %all-to-all-done.1.u_ref, s32[3,8,192,128]{3,2,1,0:T(8,128)} %broadcast_in_dim.52.start_ref, ...), custom_call_target="tpu_custom_call" | custom-call | flops 27000000512 | bytes 1048576 | tf_op jit(solution)/shard_map/attend_backward/pallas_call | solution.py:493
  353.4 49.1 %all_to_all.32 = bf16[32,3,96,128]{3,2,1,0:T(8,128)(2,1)S(1)} all-to-all(bf16[32,3,96,128]{3,2,1,0:T(8,128)(2,1)S(1)} %attend_backward.1), channel_id=1, replica_groups=mesh['xl'=2,'c'=2,'z'=4,'y'=4,'xh'=2] {'z','y','xh'}, dimensions={0} | all-to-all | bytes 4718592 | tf_op jit(solution)/shard_map/all_to_all | solution.py:69
  403.7 4.2 convolution_convert_fusion
  407.9 10.9 %all-to-all-start.5 = ((bf16[32,48,1280]{2,1,0:T(8,128)(2,1)}), bf16[32,48,1280]{2,1,0:T(8,128)(2,1)}, u32[]{:S(2)}, u32[]{:S(2)}) async-start(bf16[32,48,1280]{2,1,0:T(8,128)(2,1)} %bitcast.76), calls=%async_computation.5 | async-start | bytes 7864320 | tf_op jit(solution)/shard_map/all_to_all | solution.py:69
  418.8 3.9 fusion
  432.9 30.0 %collective-permute-done.13 = f32[2,1536]{1,0:T(2,128)S(1)} collective-permute-done((f32[2,1536]{1,0:T(2,128)S(1)}, f32[2,1536]{1,0:T(2,128)S(1)}, u32[]{:S(2)}, u32[]{:S(2)}) %collective-permute-start.13) | collective-permute-done | bytes 12320 | tf_op jit(solution)/shard_map/ppermute | solution.py:513
  466.3 9.9 %collective-permute-done.17 = f32[2,1536]{1,0:T(2,128)S(1)} collective-permute-done((f32[2,1536]{1,0:T(2,128)S(1)}, f32[2,1536]{1,0:T(2,128)S(1)}, u32[]{:S(2)}, u32[]{:S(2)}) %collective-permute-start.17) | collective-permute-done | bytes 12320 | tf_op jit(solution)/shard_map/ppermute | solution.py:514
  486.8 4.1 collective-permute-start.22
  493.5 21.1 %reduce-scatter.2.cloned.1.call-done = bf16[96,6912]{1,0:T(8,128)(2,1)} async-done(((bf16[1536,6912]{1,0:T(8,128)(2,1)}), bf16[96,6912]{1,0:T(8,128)(2,1)}) %reduce-scatter.2.cloned.1.call-update) | async-done | bytes 1327120 | tf_op jit(solution)/shard_map/reduce_scatter | solution.py:709
  524.4 3.4 collective-permute-start.25
  527.9 9.0 %collective-permute-done.27 = bf16[48,4096]{1,0:T(8,128)(2,1)} collective-permute-done((bf16[48,4096]{1,0:T(8,128)(2,1)S(1)}, bf16[48,4096]{1,0:T(8,128)(2,1)}, u32[]{:S(2)}, u32[]{:S(2)}) %collective-permute-start.27) | collective-permute-done | bytes 393248 | tf_op jit(solution)/shard_map/ppermute | solution.py:524
  536.9 5.5 collective-permute-start.24
  542.5 4.8 collective-permute-start.23
  550.1 21.8 %collective-permute-done.26 = bf16[168,1536]{1,0:T(8,128)(2,1)S(1)} collective-permute-done((bf16[168,1536]{1,0:T(8,128)(2,1)S(1)}, bf16[168,1536]{1,0:T(8,128)(2,1)S(1)}, u32[]{:S(2)}, u32[]{:S(2)}) %collective-permute-start.26) | collective-permute-done | bytes 516128 | tf_op jit(solution)/shard_map/ppermute | solution.py:582
  571.9 34.7 %collective-permute-done.25 = bf16[168,1536]{1,0:T(8,128)(2,1)S(1)} collective-permute-done((bf16[168,1536]{1,0:T(8,128)(2,1)S(1)}, bf16[168,1536]{1,0:T(8,128)(2,1)S(1)}, u32[]{:S(2)}, u32[]{:S(2)}) %collective-permute-start.25) | collective-permute-done | bytes 516128 | tf_op jit(solution)/shard_map/ppermute | solution.py:582
  606.6 8.9 %collective-permute-done.23 = bf16[168,1536]{1,0:T(8,128)(2,1)} collective-permute-done((bf16[168,1536]{1,0:T(8,128)(2,1)S(1)}, bf16[168,1536]{1,0:T(8,128)(2,1)}, u32[]{:S(2)}, u32[]{:S(2)}) %collective-permute-start.23) | collective-permute-done | bytes 516128 | tf_op jit(solution)/shard_map/ppermute | solution.py:582
  (216 shorter events, 88.0 us)
Async XLA Ops:
  7.2 239.8 %all-gather.2.cloned.1.call-start = ((), (), s32[]{:S(2)}) async-start(), calls=%async_computation.7 | async-start | bytes 22560768 | tf_op jit(solution)/shard_map/all_gather | solution.py:623
  9.4 11.6 %collective-permute-start.3 = (bf16[48,4096]{1,0:T(8,128)(2,1)S(1)}, bf16[48,4096]{1,0:T(8,128)(2,1)S(1)}, u32[]{:S(2)}, u32[]{:S(2)}) collective-permute-start(bf16[48,4096]{1,0:T(8,128)(2,1)S(1)} %bitcast_dynamic-update-slice_fusion), channel_id=1, source_target_pairs={{0,1},{1,0},{2,3},{3,2},{4,5},{5,4},{6,7},{7,6},{8,9},{9,8},{10,11... | collective-permute-start | bytes 1179656 | tf_op jit(solution)/shard_map/ppermute | solution.py:524
  12.2 14.4 %collective-permute-start.2 = (bf16[168,1536]{1,0:T(8,128)(2,1)S(1)}, bf16[168,1536]{1,0:T(8,128)(2,1)S(1)}, u32[]{:S(2)}, u32[]{:S(2)}) collective-permute-start(bf16[168,1536]{1,0:T(8,128)(2,1)S(1)} %pad_maximum_fusion.4), channel_id=1, source_target_pairs={{0,0},{1,2},{2,4},{3,6},{4,8},{5,10},{6,12},{7,14},{8,16},{9,18},{... | collective-permute-start | bytes 1548296 | tf_op jit(solution)/shard_map/ppermute | solution.py:621
  32.0 77.2 %all-to-all-start = ((bf16[32,48,1408]{2,1,0:T(8,128)(2,1)}), bf16[32,48,1408]{2,1,0:T(8,128)(2,1)}, u32[]{:S(2)}, u32[]{:S(2)}) async-start(bf16[32,48,1408]{2,1,0:T(8,128)(2,1)} %broadcast_in_dim.46), calls=%async_computation | async-start | bytes 8650752 | tf_op jit(solution)/shard_map/all_to_all | solution.py:69
  43.7 2.7 collective-permute-start.1
  118.9 50.1 %all-to-all-start.1 = ((bf16[32,3,96,128]{3,2,1,0:T(8,128)(2,1)}), bf16[32,3,96,128]{3,2,1,0:T(8,128)(2,1)S(1)}, u32[]{:S(2)}, u32[]{:S(2)}) async-start(bf16[32,3,96,128]{3,2,1,0:T(8,128)(2,1)} %bitcast.69), calls=%async_computation.1 | async-start | bytes 4718592 | tf_op jit(solution)/shard_map/all_to_all | solution.py:69
  130.8 383.8 %reduce-scatter.2.cloned.1.call-start = ((), (), s32[]{:S(2)}) async-start(), calls=%async_computation.8 | async-start | bytes 22560768 | tf_op jit(solution)/shard_map/reduce_scatter | solution.py:709
  132.7 2.5 collective-permute-start
  252.5 3.0 collective-permute-start.4
  253.1 4.8 collective-permute-start.6
  290.5 2.5 collective-permute-start.7
  407.9 72.3 %all-to-all-start.5 = ((bf16[32,48,1280]{2,1,0:T(8,128)(2,1)}), bf16[32,48,1280]{2,1,0:T(8,128)(2,1)}, u32[]{:S(2)}, u32[]{:S(2)}) async-start(bf16[32,48,1280]{2,1,0:T(8,128)(2,1)} %bitcast.76), calls=%async_computation.5 | async-start | bytes 7864320 | tf_op jit(solution)/shard_map/all_to_all | solution.py:69
  422.8 3.9 collective-permute-start.10
  428.7 34.2 %collective-permute-start.13 = (f32[2,1536]{1,0:T(2,128)S(1)}, f32[2,1536]{1,0:T(2,128)S(1)}, u32[]{:S(2)}, u32[]{:S(2)}) collective-permute-start(f32[2,1536]{1,0:T(2,128)S(1)} %fusion.22), channel_id=1, source_target_pairs={{0,1},{64,65},{1,0},{65,64},{2,3},{66,67},{3,2},{67,66},{4,5},{68,... | collective-permute-start | bytes 36872 | tf_op jit(solution)/shard_map/ppermute | solution.py:513
  431.5 31.5 %collective-permute-start.14 = (f32[2,1536]{1,0:T(2,128)S(1)}, f32[2,1536]{1,0:T(2,128)S(1)}, u32[]{:S(2)}, u32[]{:S(2)}) collective-permute-start(f32[2,1536]{1,0:T(2,128)S(1)} %fusion.22), channel_id=1, source_target_pairs={{0,65},{64,0},{1,64},{65,1},{2,67},{66,2},{3,66},{67,3},{4,69},{68... | collective-permute-start | bytes 36872 | tf_op jit(solution)/shard_map/ppermute | solution.py:513
  431.6 31.5 %collective-permute-start.12 = (f32[2,1536]{1,0:T(2,128)S(1)}, f32[2,1536]{1,0:T(2,128)S(1)}, u32[]{:S(2)}, u32[]{:S(2)}) collective-permute-start(f32[2,1536]{1,0:T(2,128)S(1)} %fusion.22), channel_id=1, source_target_pairs={{0,64},{64,1},{1,65},{65,0},{2,66},{66,3},{3,67},{67,2},{4,68},{68... | collective-permute-start | bytes 36872 | tf_op jit(solution)/shard_map/ppermute | solution.py:513
  463.1 13.2 %collective-permute-start.17 = (f32[2,1536]{1,0:T(2,128)S(1)}, f32[2,1536]{1,0:T(2,128)S(1)}, u32[]{:S(2)}, u32[]{:S(2)}) collective-permute-start(f32[2,1536]{1,0:T(2,128)S(1)} %add_add_fusion.1), channel_id=1, source_target_pairs={{0,6},{2,0},{4,2},{6,4},{1,7},{3,1},{5,3},{7,5},{8,14},{10,8},{12,... | collective-permute-start | bytes 36872 | tf_op jit(solution)/shard_map/ppermute | solution.py:514
  464.4 12.3 %collective-permute-start.16 = (f32[2,1536]{1,0:T(2,128)S(1)}, f32[2,1536]{1,0:T(2,128)S(1)}, u32[]{:S(2)}, u32[]{:S(2)}) collective-permute-start(f32[2,1536]{1,0:T(2,128)S(1)} %add_add_fusion.1), channel_id=1, source_target_pairs={{0,4},{2,6},{4,0},{6,2},{1,5},{3,7},{5,1},{7,3},{8,12},{10,14},{12... | collective-permute-start | bytes 36872 | tf_op jit(solution)/shard_map/ppermute | solution.py:514
  465.5 11.1 %collective-permute-start.15 = (f32[2,1536]{1,0:T(2,128)S(1)}, f32[2,1536]{1,0:T(2,128)S(1)}, u32[]{:S(2)}, u32[]{:S(2)}) collective-permute-start(f32[2,1536]{1,0:T(2,128)S(1)} %add_add_fusion.1), channel_id=1, source_target_pairs={{0,2},{2,4},{4,6},{6,0},{1,3},{3,5},{5,7},{7,1},{8,10},{10,12},{12... | collective-permute-start | bytes 36872 | tf_op jit(solution)/shard_map/ppermute | solution.py:514
  476.7 8.8 %collective-permute-start.20 = (f32[2,1536]{1,0:T(2,128)S(1)}, f32[2,1536]{1,0:T(2,128)S(1)}, u32[]{:S(2)}, u32[]{:S(2)}) collective-permute-start(f32[2,1536]{1,0:T(2,128)S(1)} %add_add_fusion), channel_id=1, source_target_pairs={{0,24},{8,0},{16,8},{24,16},{1,25},{9,1},{17,9},{25,17},{2,26},{10... | collective-permute-start | bytes 36872 | tf_op jit(solution)/shard_map/ppermute | solution.py:514
  477.9 7.6 %collective-permute-start.19 = (f32[2,1536]{1,0:T(2,128)S(1)}, f32[2,1536]{1,0:T(2,128)S(1)}, u32[]{:S(2)}, u32[]{:S(2)}) collective-permute-start(f32[2,1536]{1,0:T(2,128)S(1)} %add_add_fusion), channel_id=1, source_target_pairs={{0,16},{8,24},{16,0},{24,8},{1,17},{9,25},{17,1},{25,9},{2,18},{10... | collective-permute-start | bytes 36872 | tf_op jit(solution)/shard_map/ppermute | solution.py:514
  479.0 6.5 %collective-permute-start.18 = (f32[2,1536]{1,0:T(2,128)S(1)}, f32[2,1536]{1,0:T(2,128)S(1)}, u32[]{:S(2)}, u32[]{:S(2)}) collective-permute-start(f32[2,1536]{1,0:T(2,128)S(1)} %add_add_fusion), channel_id=1, source_target_pairs={{0,8},{8,16},{16,24},{24,0},{1,9},{9,17},{17,25},{25,1},{2,10},{10... | collective-permute-start | bytes 36872 | tf_op jit(solution)/shard_map/ppermute | solution.py:514
  482.9 3.8 collective-permute-start.21
  486.8 5.0 collective-permute-start.22
  516.6 25.9 %collective-permute-start.29 = (bf16[48,4096]{1,0:T(8,128)(2,1)}, bf16[48,4096]{1,0:T(8,128)(2,1)}, u32[]{:S(2)}, u32[]{:S(2)}) collective-permute-start(bf16[48,4096]{1,0:T(8,128)(2,1)} %get-tuple-element.47), channel_id=1, source_target_pairs={{0,65},{1,64},{64,1},{65,0},{2,67},{3,66},{66,3},{67,2},{4,69},{5,... | collective-permute-start | bytes 1179656 | tf_op jit(solution)/shard_map/ppermute | solution.py:570
  519.0 28.3 %collective-permute-start.28 = (bf16[48,4096]{1,0:T(8,128)(2,1)}, bf16[48,4096]{1,0:T(8,128)(2,1)}, u32[]{:S(2)}, u32[]{:S(2)}) collective-permute-start(bf16[48,4096]{1,0:T(8,128)(2,1)} %get-tuple-element.47), channel_id=1, source_target_pairs={{0,1},{1,0},{2,3},{3,2},{4,5},{5,4},{6,7},{7,6},{8,9},{9,8},{10,11... | collective-permute-start | bytes 1179656 | tf_op jit(solution)/shard_map/ppermute | solution.py:524
  519.5 17.4 %collective-permute-start.27 = (bf16[48,4096]{1,0:T(8,128)(2,1)S(1)}, bf16[48,4096]{1,0:T(8,128)(2,1)}, u32[]{:S(2)}, u32[]{:S(2)}) collective-permute-start(bf16[48,4096]{1,0:T(8,128)(2,1)S(1)} %get-tuple-element.46), channel_id=1, source_target_pairs={{0,64},{64,0},{1,65},{65,1},{2,66},{66,2},{3,67},{67,3},{4,68},{68... | collective-permute-start | bytes 1179656 | tf_op jit(solution)/shard_map/ppermute | solution.py:524
  521.9 50.0 %collective-permute-start.26 = (bf16[168,1536]{1,0:T(8,128)(2,1)S(1)}, bf16[168,1536]{1,0:T(8,128)(2,1)S(1)}, u32[]{:S(2)}, u32[]{:S(2)}) collective-permute-start(bf16[168,1536]{1,0:T(8,128)(2,1)S(1)} %pad_maximum_fusion.5), channel_id=1, source_target_pairs={{0,96},{1,64},{2,97},{3,65},{4,98},{5,66},{6,99},{7,67},{8,100},{9... | collective-permute-start | bytes 1548296 | tf_op jit(solution)/shard_map/ppermute | solution.py:582
  524.4 82.2 %collective-permute-start.25 = (bf16[168,1536]{1,0:T(8,128)(2,1)S(1)}, bf16[168,1536]{1,0:T(8,128)(2,1)S(1)}, u32[]{:S(2)}, u32[]{:S(2)}) collective-permute-start(bf16[168,1536]{1,0:T(8,128)(2,1)S(1)} %pad_maximum_fusion.5), channel_id=1, source_target_pairs={{0,32},{1,0},{2,33},{3,1},{4,34},{5,2},{6,35},{7,3},{8,36},{9,4},{... | collective-permute-start | bytes 1548296 | tf_op jit(solution)/shard_map/ppermute | solution.py:582
  536.9 69.7 %collective-permute-start.24 = (bf16[168,1536]{1,0:T(8,128)(2,1)S(1)}, bf16[168,1536]{1,0:T(8,128)(2,1)S(1)}, u32[]{:S(2)}, u32[]{:S(2)}) collective-permute-start(bf16[168,1536]{1,0:T(8,128)(2,1)S(1)} %pad_maximum_fusion.5), channel_id=1, source_target_pairs={{0,64},{1,96},{2,65},{3,97},{4,66},{5,98},{6,67},{7,99},{8,68},{9,... | collective-permute-start | bytes 1548296 | tf_op jit(solution)/shard_map/ppermute | solution.py:582
  542.5 73.1 %collective-permute-start.23 = (bf16[168,1536]{1,0:T(8,128)(2,1)S(1)}, bf16[168,1536]{1,0:T(8,128)(2,1)}, u32[]{:S(2)}, u32[]{:S(2)}) collective-permute-start(bf16[168,1536]{1,0:T(8,128)(2,1)S(1)} %pad_maximum_fusion.5), channel_id=1, source_target_pairs={{0,0},{1,32},{2,1},{3,33},{4,2},{5,34},{6,3},{7,35},{8,4},{9,36},{... | collective-permute-start | bytes 1548296 | tf_op jit(solution)/shard_map/ppermute | solution.py:582
  549.3 69.2 %collective-permute-start.30 = (bf16[48,3840]{1,0:T(8,128)(2,1)S(1)}, bf16[48,3840]{1,0:T(8,128)(2,1)S(1)}, u32[]{:S(2)}, u32[]{:S(2)}) collective-permute-start(bf16[48,3840]{1,0:T(8,128)(2,1)S(1)} %pad_maximum_fusion.6), channel_id=1, source_target_pairs={{0,32},{32,0},{1,33},{33,1},{2,34},{34,2},{3,35},{35,3},{4,36},{36... | collective-permute-start | bytes 1105928 | tf_op jit(solution)/shard_map/ppermute | solution.py:65
  (27 other events, 69.5 us)
Sparse Core Ops, SparseCore 0:
  28.3 218.6 all-gather.1
  303.1 211.5 reduce-scatter.1

commit v4 on v3

--- a/solution.py
+++ b/solution.py
@@ -151,14 +151,7 @@
         other_ref[:, cols] = result[ROWS:].astype(jnp.bfloat16)
 
 
-def d_out_kernel(da_ref, w_ref, attn_ref, held_ref, out_ref, grad_ref, g_out, sem):
-    attn_t = attn_ref[...].T
-    for k in range(2):
-        half = product(attn_t, da_ref[:, k * (D // 2) : (k + 1) * (D // 2)]).astype(jnp.bfloat16)
-        for j in range(16):
-            g_out[j * 96 + k * 48 : j * 96 + k * 48 + 48, :] = half[j * 48 : j * 48 + 48]
-    copy = pltpu.make_async_copy(g_out, grad_ref.at[:, pl.ds(OUT_AT, D // 2)], sem)
-    copy.start()
+def d_out_kernel(da_ref, w_ref, out_ref):
     left, right = out_halves(w_ref)
     rows = product_t(da_ref[:, : D // 2], left) + product_t(da_ref[:, D // 2 :], right)
     rows = rows.astype(jnp.bfloat16)
@@ -172,7 +165,6 @@
                     at = (o * MB + m) * SPAN + p * CHUNK
                     out_ref[j, o, p, m, :CHUNK, :] = first[at : at + CHUNK]
                     out_ref[j, o, p, m, CHUNK:, :] = third[at : at + CHUNK]
-    copy.wait()
 
 
 def collect_kernel(u_ref, table_ref, out_ref):
@@ -343,22 +335,19 @@
     )(split_units(units), w_all)
 
 
-def d_out_project(da, w_all, attn, g_ffn):
+def d_out_project(da, w_all):
     dims = (HALF_KV, 2, PARTS, MB, Q_ROWS, 128)
-    anywhere = pl.BlockSpec(memory_space=pl.ANY)
-    out, grads = pl.pallas_call(
+    out = pl.pallas_call(
         d_out_kernel,
         grid=(1,),
-        in_specs=[whole_spec(BOTH, D), OUT_SPEC, whole_spec(BOTH, HQ), anywhere],
-        out_specs=[whole_spec(*dims), anywhere],
-        out_shape=[low_shape(*dims), low_shape(*g_ffn.shape)],
-        scratch_shapes=[pltpu.VMEM((D, D // 2), jnp.bfloat16), pltpu.SemaphoreType.DMA],
-        input_output_aliases={3: 1},
+        in_specs=[whole_spec(BOTH, D), OUT_SPEC],
+        out_specs=whole_spec(*dims),
+        out_shape=low_shape(*dims),
         compiler_params=PARAMS,
-        cost_estimate=cost(5),
+        cost_estimate=cost(3),
         name="d_out_project",
-    )(da, w_all, attn, g_ffn)
-    return out.reshape(SHARDS, MB, Q_ROWS, 128), grads
+    )(da, w_all)
+    return out.reshape(SHARDS, MB, Q_ROWS, 128)
 
 
 def ffn_kernel(
@@ -452,7 +441,7 @@
             pl.BlockSpec((D, FF_TILE), lambda t: (0, UP_AT // FF_TILE + t)),
         ],
         out_specs=[whole_spec(ROWS, D)] * 4 + [pl.BlockSpec(memory_space=pl.ANY)],
-        out_shape=[wide, low_shape(ROWS, D), wide, low_shape(ROWS, D), low_shape(D, OUT_AT + D // 2)],
+        out_shape=[wide, low_shape(ROWS, D), wide, low_shape(ROWS, D), low_shape(D, OUT_AT)],
         scratch_shapes=[
             pltpu.VMEM((D, BOTH), jnp.bfloat16),
             pltpu.VMEM((BOTH, D), jnp.float32),
@@ -498,7 +487,7 @@
         out_shape=low_shape(SHARDS, MB, ALL_ROWS, 128),
         scratch_shapes=[pltpu.VMEM((SEQ, 128), jnp.float32)],
         compiler_params=PARAMS,
-        cost_estimate=cost(27),
+        cost_estimate=cost(40),
         name="attend_backward",
     )(unit, first, units, starts, d_mixed, lse)
 
@@ -562,24 +551,13 @@
     return values + shift(values, axis, 1) + shift(values, axis, 2) + shift(values, axis, 3)
 
 
-def reduce_x(values):
-    size = values.shape[0] // 2
+def reduce_x(values, dim):
+    size = values.shape[dim] // 2
     me = lax.axis_index("xh")
-    keep = lax.dynamic_slice_in_dim(values, me * size, size, axis=0)
-    send = lax.dynamic_slice_in_dim(values, (1 - me) * size, size, axis=0)
+    keep = lax.dynamic_slice_in_dim(values, me * size, size, axis=dim)
+    send = lax.dynamic_slice_in_dim(values, (1 - me) * size, size, axis=dim)
     cross = lax.ppermute(send, ("xl", "xh"), [(i, 3 - i) for i in range(4)])
     return wide_sum(keep, flip(keep, "xl"), flip(send, "xh"), cross)
-
-
-def return_rows(rows, a, b):
-    pairs = []
-    for xl in range(2):
-        for c in range(2):
-            for j in range(16):
-                for xh in range(2):
-                    source = ((xl * 2 + c) * 16 + j) * 2 + xh
-                    pairs.append((source, ((xl ^ b) * 2 + (xh ^ a)) * SHARDS + 16 * c + j))
-    return lax.ppermute(rows, ("xl", "c") + SHARD, pairs)
 
 
 def add_pair(values, axis):
@@ -698,6 +676,7 @@
     y2_mine, y2_other, dn2_mine, dn2_other, g_ffn = feed_forward(n2, df, w_all)
     result = hmid + branch_scale * (y2_mine + swap(y2_other).astype(jnp.float32))
 
+    s_ffn = lax.psum_scatter(g_ffn, ("z", "y"), scatter_dimension=0, tiled=True)
     dn2 = dn2_mine + swap(dn2_other).astype(jnp.float32)
     e2 = dn2 * gain_ffn
     g_gain_ffn = jnp.sum(dn2 * z2, axis=0)
@@ -705,11 +684,12 @@
 
     da_mine = (branch_scale * dh).astype(low)
     da = jnp.concatenate([da_mine, swap(da_mine)], axis=0)
-    unit_do, g_all = d_out_project(da, w_all, attn, g_ffn)
-    s_all = lax.psum_scatter(g_all, ("z", "y"), scatter_dimension=0, tiled=True)
-    unit_do = exchange(unit_do)
+    unit_do = exchange(d_out_project(da, w_all))
+    g_o = [t_product(attn, da[:, k * (D // 2) : (k + 1) * (D // 2)]).astype(low) for k in range(2)]
+    g_o = jnp.stack([g.reshape(16, 48, D // 2) for g in g_o], axis=1).reshape(SHARDS, 48, D // 2)
+    s_o = scatter_sum(after(g_o, unit_do))
     unit_d = attend_bwd(unit, first, units, starts, unit_do, lse)
-    d_qkv = collect(exchange(unit_d), tables)
+    d_qkv = collect(exchange(after(unit_d, s_o)), tables)
 
     g_qkv = t_product(n1, d_qkv).astype(low)
     s_qkv = scatter_sum(g_qkv.reshape(SHARDS, 48, HQ + 2 * HK))
@@ -724,17 +704,11 @@
     gains = gains + swap(gains)
     gains = total_axis(total_axis(total_axis(gains, "x"), "y"), "z")
     gains = lax.dynamic_slice_in_dim(gains, shard * 48, 48, axis=1)
-    s_all = after(s_all, gains)
-    rows = jnp.concatenate(
-        [
-            unfold(s_all[None, :, OUT_AT:], 2)[0],
-            s_all[:, :D],
-            unfold(s_all[None, :, REST_AT:GATE_AT], 3)[0][:24],
-        ],
-        axis=0,
-    )
-    rows = sum(return_rows(rows, a, b).astype(jnp.float32) for a in range(2) for b in range(2))
-    s_gu = reduce_x(s_all[:, GATE_AT:OUT_AT])
+    s_ffn, s_o = after((s_ffn, s_o), gains)
+    s_d = jnp.concatenate([s_ffn[:, :D], unfold(s_ffn[None, :, REST_AT:GATE_AT], 3)[0][:24]], axis=0)
+    rows = jnp.concatenate([add_pair(s_o, "xl"), reduce_x(s_d, 1)], axis=0)
+    rows = join_cores(lax.ppermute(rows, ("c",) + SHARD, [(b, a) for a, b in piece_perm()]))
+    s_gu = reduce_x(s_ffn[:, GATE_AT:], 0)
     s_gu = jnp.concatenate([crop_units(s_gu[:, :PAD_FF]), crop_units(s_gu[:, PAD_FF:])], axis=1)
     other = swap(s_gu)
     lower = core == 0

time: 640 us -> 590 us (0.922)
  waiting for transfers between devices: 278 us -> 221 us
  blocking collectives: 95.1 us -> 76.8 us
  starting transfers between devices: 85.7 us -> 101 us
    ppermute x4 -> x1, waiting for transfers between devices: 65.4 us -> 5.68 us  [on_device(): lax.ppermute(rows, ('c',) + SHARD, [(b, a) for a, b in piece_perm()])]
    all_to_all x3 -> x5, starting transfers between devices: 34.6 us -> 55.8 us  [exchange(): return lax.all_to_all(values, SHARD, 0, 0, tiled=True)]
    reduce_scatter x1, waiting for transfers between devices: 21.1 us -> 0.01 us  [on_device(): s_ffn = lax.psum_scatter(g_ffn, ('z', 'y'), scatter_dimension=0, tiled=True)]
    all_to_all x3 -> x2, blocking collectives: 95.1 us -> 76.8 us  [exchange(): return lax.all_to_all(values, SHARD, 0, 0, tiled=True)]
    all_to_all x3 -> x5, waiting for transfers between devices: 89.6 us -> 104 us  [exchange(): return lax.all_to_all(values, SHARD, 0, 0, tiled=True)]
    ppermute x4 -> x1, starting transfers between devices: 16.3 us -> 2.41 us  [on_device(): lax.ppermute(rows, ('c',) + SHARD, [(b, a) for a, b in piece_perm()])]
    ppermute x4 -> x8, waiting for transfers between devices: 13.7 us -> 24.5 us  [flip(): return lax.ppermute(values, axis, [(0, 1), (1, 0)])]
  transfers between devices with their start and end apart: 36 -> 40, of which waited for: 25 -> 26; matrix products, arithmetic and copies ran while one was open for 7% -> 9% of each run, Pallas kernels for 9% -> 10%
where the time goes in v4:
time: 590 us; the launch traced here: 579 us
  waiting for transfers between devices  221 us (37%)
  starting transfers between devices  101 us (17%)
  Pallas kernels  92.7 us (16%)
  blocking collectives  76.8 us (13%)
  other arithmetic  35.5 us (6%)
  local copies, waits for them, and re-layouts  26.3 us (4%)
  between operations  15.2 us (3%)
  matrix products  11 us (2%)
    all_to_all x5, waiting for transfers between devices, exchange(): return lax.all_to_all(values, SHARD, 0, 0, tiled=True)  104 us
    all_to_all x2, blocking collectives, exchange(): return lax.all_to_all(values, SHARD, 0, 0, tiled=True)  76.8 us
    all_to_all x5, starting transfers between devices, exchange(): return lax.all_to_all(values, SHARD, 0, 0, tiled=True)  55.8 us
    pallas_call x1, Pallas kernels, feed_forward(): pl.pallas_call(ffn_kernel, grid=(FF_TILES,), in_specs=[whole_spec(BOTH, D...  30.3 us
    all_gather x1, waiting for transfers between devices, on_device(): lax.all_gather(jnp.concatenate([rows_in[48:144], fold(jnp.pad(rows_in[144...  29.6 us
    ppermute x3, waiting for transfers between devices, shift(): lax.ppermute(values, ('xl', 'xh'), [(line(i), line((i + step) % 4)) for i...  28.4 us
    pallas_call x1, Pallas kernels, attend_bwd(): pl.pallas_call(bwd_kernel, grid=(MB,), in_specs=[SMEM, SMEM, UNIT_SPEC, C...  28.3 us
    ppermute x8, waiting for transfers between devices, flip(): return lax.ppermute(values, axis, [(0, 1), (1, 0)])  24.5 us
  transfers between devices with their start and end apart: 40, of which 26 were waited for; matrix products, arithmetic and copies ran while one was open for 9% of the time, Pallas kernels for 10%

profile of v4, /device:TPU:49, one launch (start us, length us, event | category | flops | bytes accessed | tf_op | source)
XLA Modules:
  0.0 578.8 jit_solution(3343525319200763634)
XLA Ops:
  12.2 5.2 collective-permute-start.2
  17.4 3.5 collective-permute-done.3
  21.0 5.7 collective-permute-done.2
  32.0 11.7 %all-to-all-start = ((bf16[32,48,1408]{2,1,0:T(8,128)(2,1)}), bf16[32,48,1408]{2,1,0:T(8,128)(2,1)}, u32[]{:S(2)}, u32[]{:S(2)}) async-start(bf16[32,48,1408]{2,1,0:T(8,128)(2,1)} %broadcast_in_dim.46), calls=%async_computation | async-start | bytes 8650752 | tf_op jit(solution)/shard_map/all_to_all | solution.py:69
  46.7 62.4 %all-to-all-done = bf16[32,48,1408]{2,1,0:T(8,128)(2,1)} async-done(((bf16[32,48,1408]{2,1,0:T(8,128)(2,1)}), bf16[32,48,1408]{2,1,0:T(8,128)(2,1)}, u32[]{:S(2)}, u32[]{:S(2)}) %all-to-all-start) | async-done | bytes 4325408 | tf_op jit(solution)/shard_map/all_to_all | solution.py:69
  112.0 6.0 %project.1 = bf16[4,2,4,3,96,128]{5,4,3,2,1,0:T(8,128)(2,1)S(1)} custom-call(bf16[384,1536]{1,0:T(8,128)(2,1)S(1)} %fusion.4.n_ref, bf16[1536,1408]{1,0:T(8,128)(2,1)} %bitcast.7.w_ref, f32[4,64,128]{2,1,0:T(8,128)S(1)} %pad_maximum_fusion.9.table_ref), custom_call_target="tpu_custom_call" | custom-call | flops 6000000000 | bytes 1048576 | tf_op jit(solution)/shard_map/project/pallas_call | solution.py:310
  119.4 12.0 %all-to-all-start.1 = ((bf16[32,3,96,128]{3,2,1,0:T(8,128)(2,1)}), bf16[32,3,96,128]{3,2,1,0:T(8,128)(2,1)S(1)}, u32[]{:S(2)}, u32[]{:S(2)}) async-start(bf16[32,3,96,128]{3,2,1,0:T(8,128)(2,1)} %bitcast.73), calls=%async_computation.1 | async-start | bytes 4718592 | tf_op jit(solution)/shard_map/all_to_all | solution.py:69
  135.8 5.8 %convert_reduce_fusion = s32[3,2048]{1,0:T(4,128)S(1)} fusion(f32[3,2048]{1,0:T(4,128)S(1)} %select_convert_fusion), kind=kLoop, calls=%fused_computation | loop fusion | flops 37742592 | bytes 49152 | tf_op jit(solution)/shard_map/reduce_sum | solution.py:640
  142.3 27.2 %all-to-all-done.1.u_ref = bf16[32,3,96,128]{3,2,1,0:T(8,128)(2,1)S(1)} async-done(((bf16[32,3,96,128]{3,2,1,0:T(8,128)(2,1)}), bf16[32,3,96,128]{3,2,1,0:T(8,128)(2,1)S(1)}, u32[]{:S(2)}, u32[]{:S(2)}) %all-to-all-start.1) | async-done | bytes 2359328 | tf_op jit(solution)/shard_map/all_to_all | solution.py:69
  171.8 19.8 %attend_forward.1 = (bf16[32,3,32,128]{3,2,1,0:T(8,128)(2,1)S(1)}, f32[3,8,192,128]{3,2,1,0:T(8,128)S(1)}) custom-call(s32[2]{0:T(128)S(1)} %pad_add_fusion.unit_ref, s32[24]{0:T(128)S(1)} %and_select_fusion.first_ref, bf16[32,3,96,128]{3,2,1,0:T(8,128)(2,1)S(1)} %all-to-all-done.1.u_ref, s32[3,8,192,128]{3,2,1,0:T(8,128)} %broadcast_in_dim.52.start_ref), custom_call_target="tpu_custom_call" | custom-call | flops 20000000000 | bytes 1048576 | tf_op jit(solution)/shard_map/attend_forward/pallas_call | solution.py:469
  193.0 24.4 %all_to_all.35 = bf16[32,3,32,128]{3,2,1,0:T(8,128)(2,1)S(1)} all-to-all(bf16[32,3,32,128]{3,2,1,0:T(8,128)(2,1)S(1)} %get-tuple-element.25), channel_id=1, replica_groups=mesh['xl'=2,'c'=2,'z'=4,'y'=4,'xh'=2] {'z','y','xh'}, dimensions={0} | all-to-all | bytes 1572864 | tf_op jit(solution)/shard_map/all_to_all | solution.py:69
  217.4 29.6 %all-gather.2.cloned.1.call-done.w_ref.main_ref.rest_ref.gate_ref.up_ref = bf16[1536,6912]{1,0:T(8,128)(2,1)} async-done(((bf16[96,6912]{1,0:T(8,128)(2,1)}), bf16[1536,6912]{1,0:T(8,128)(2,1)}) %all-gather.2.cloned.1.call-update) | async-done | bytes 21233680 | tf_op jit(solution)/shard_map/all_gather | solution.py:601
  247.0 3.6 out_project.1
  259.7 30.3 %feed_forward.1 = (f32[192,1536]{1,0:T(8,128)S(1)}, bf16[192,1536]{1,0:T(8,128)(2,1)S(1)}, f32[192,1536]{1,0:T(8,128)S(1)}, bf16[192,1536]{1,0:T(8,128)(2,1)S(1)}, bf16[1536,6144]{1,0:T(8,128)(2,1)}) custom-call(bf16[384,1536]{1,0:T(8,128)(2,1)S(1)} %pad_maximum_fusion.4.n_ref, bf16[384,1536]{1,0:T(8,128)(2,1)S(1)} %multiply_convert_fusion.df_ref, ...), custom_call_target="tpu_custom_call" | custom-call | flops 30000001024 | bytes 1048576 | tf_op jit(solution)/shard_map/feed_forward/pallas_call | solution.py:432
  303.4 3.9 d_out_project.1
  307.4 9.1 %all-to-all-start.3 = ((bf16[32,3,32,128]{3,2,1,0:T(8,128)(2,1)}), bf16[32,3,32,128]{3,2,1,0:T(8,128)(2,1)S(1)}, u32[]{:S(2)}, u32[]{:S(2)}) async-start(bf16[32,3,32,128]{3,2,1,0:T(8,128)(2,1)} %bitcast.20), calls=%async_computation.3 | async-start | bytes 1572864 | tf_op jit(solution)/shard_map/all_to_all | solution.py:69
  321.2 8.4 %all-to-all-done.3.do_ref = bf16[32,3,32,128]{3,2,1,0:T(8,128)(2,1)S(1)} async-done(((bf16[32,3,32,128]{3,2,1,0:T(8,128)(2,1)}), bf16[32,3,32,128]{3,2,1,0:T(8,128)(2,1)S(1)}, u32[]{:S(2)}, u32[]{:S(2)}) %all-to-all-start.3) | async-done | bytes 786464 | tf_op jit(solution)/shard_map/all_to_all | solution.py:69
  329.6 12.2 %all-to-all-start.4 = ((bf16[32,48,768]{2,1,0:T(8,128)(2,1)}), bf16[32,48,768]{2,1,0:T(8,128)(2,1)}, u32[]{:S(2)}, u32[]{:S(2)}) async-start(bf16[32,48,768]{2,1,0:T(8,128)(2,1)} %bitcast.79), calls=%async_computation.4 | async-start | bytes 4718592 | tf_op jit(solution)/shard_map/all_to_all | solution.py:69
  341.8 28.3 %attend_backward.1 = bf16[32,3,96,128]{3,2,1,0:T(8,128)(2,1)S(1)} custom-call(s32[2]{0:T(128)S(1)} %pad_add_fusion.unit_ref, s32[24]{0:T(128)S(1)} %and_select_fusion.first_ref, bf16[32,3,96,128]{3,2,1,0:T(8,128)(2,1)S(1)} %all-to-all-done.1.u_ref, s32[3,8,192,128]{3,2,1,0:T(8,128)} %broadcast_in_dim.52.start_ref, ...), custom_call_target="tpu_custom_call" | custom-call | flops 40000000000 | bytes 1048576 | tf_op jit(solution)/shard_map/attend_backward/pallas_call | solution.py:482
  371.5 6.3 %all-to-all-done.4 = bf16[32,48,768]{2,1,0:T(8,128)(2,1)} async-done(((bf16[32,48,768]{2,1,0:T(8,128)(2,1)}), bf16[32,48,768]{2,1,0:T(8,128)(2,1)}, u32[]{:S(2)}, u32[]{:S(2)}) %all-to-all-start.4) | async-done | bytes 2359328 | tf_op jit(solution)/shard_map/all_to_all | solution.py:69
  380.3 52.5 %all_to_all.36 = bf16[32,3,96,128]{3,2,1,0:T(8,128)(2,1)S(1)} all-to-all(bf16[32,3,96,128]{3,2,1,0:T(8,128)(2,1)S(1)} %copy-done.2), channel_id=1, replica_groups=mesh['xl'=2,'c'=2,'z'=4,'y'=4,'xh'=2] {'z','y','xh'}, dimensions={0} | all-to-all | bytes 4718592 | tf_op jit(solution)/shard_map/all_to_all | solution.py:69
  434.0 4.2 convolution_convert_fusion
  438.2 10.7 %all-to-all-start.6 = ((bf16[32,48,1280]{2,1,0:T(8,128)(2,1)}), bf16[32,48,1280]{2,1,0:T(8,128)(2,1)}, u32[]{:S(2)}, u32[]{:S(2)}) async-start(bf16[32,48,1280]{2,1,0:T(8,128)(2,1)} %bitcast.80), calls=%async_computation.6 | async-start | bytes 7864320 | tf_op jit(solution)/shard_map/all_to_all | solution.py:69
  449.0 3.8 fusion
  452.9 3.2 collective-permute-start.10
  464.5 26.1 %collective-permute-done.12 = f32[2,1536]{1,0:T(2,128)S(1)} collective-permute-done((f32[2,1536]{1,0:T(2,128)S(1)}, f32[2,1536]{1,0:T(2,128)S(1)}, u32[]{:S(2)}, u32[]{:S(2)}) %collective-permute-start.12) | collective-permute-done | bytes 12320 | tf_op jit(solution)/shard_map/ppermute | solution.py:502
  495.4 8.1 %collective-permute-done.15 = f32[2,1536]{1,0:T(2,128)S(1)} collective-permute-done((f32[2,1536]{1,0:T(2,128)S(1)}, f32[2,1536]{1,0:T(2,128)S(1)}, u32[]{:S(2)}, u32[]{:S(2)}) %collective-permute-start.15) | collective-permute-done | bytes 12320 | tf_op jit(solution)/shard_map/ppermute | solution.py:503
  503.6 5.3 collective-permute-done.17
  519.8 6.1 %collective-permute-start.22 = (bf16[48,1280]{1,0:T(8,128)(2,1)S(1)}, bf16[48,1280]{1,0:T(8,128)(2,1)S(1)}, u32[]{:S(2)}, u32[]{:S(2)}) collective-permute-start(bf16[48,1280]{1,0:T(8,128)(2,1)S(1)} %add_convert_fusion.3), channel_id=1, source_target_pairs={{0,32},{32,0},{1,33},{33,1},{2,34},{34,2},{3,35},{35,3},{4,36},{36... | collective-permute-start | bytes 368648 | tf_op jit(solution)/shard_map/ppermute | solution.py:65
  540.0 3.2 collective-permute-done.24
  546.8 13.3 %collective-permute-done.29 = bf16[48,4096]{1,0:T(8,128)(2,1)S(1)} collective-permute-done((bf16[48,4096]{1,0:T(8,128)(2,1)S(1)}, bf16[48,4096]{1,0:T(8,128)(2,1)S(1)}, u32[]{:S(2)}, u32[]{:S(2)}) %collective-permute-start.29) | collective-permute-done | bytes 393248 | tf_op jit(solution)/shard_map/ppermute | solution.py:513
  560.9 5.7 collective-permute-done.27
  (267 shorter events, 106.0 us)
Async XLA Ops:
  7.2 239.8 %all-gather.2.cloned.1.call-start = ((), (), s32[]{:S(2)}) async-start(), calls=%async_computation.8 | async-start | bytes 22560768 | tf_op jit(solution)/shard_map/all_gather | solution.py:601
  9.4 11.6 %collective-permute-start.3 = (bf16[48,4096]{1,0:T(8,128)(2,1)S(1)}, bf16[48,4096]{1,0:T(8,128)(2,1)S(1)}, u32[]{:S(2)}, u32[]{:S(2)}) collective-permute-start(bf16[48,4096]{1,0:T(8,128)(2,1)S(1)} %bitcast_dynamic-update-slice_fusion), channel_id=1, source_target_pairs={{0,1},{1,0},{2,3},{3,2},{4,5},{5,4},{6,7},{7,6},{8,9},{9,8},{10,11... | collective-permute-start | bytes 1179656 | tf_op jit(solution)/shard_map/ppermute | solution.py:513
  12.2 14.4 %collective-permute-start.2 = (bf16[168,1536]{1,0:T(8,128)(2,1)S(1)}, bf16[168,1536]{1,0:T(8,128)(2,1)S(1)}, u32[]{:S(2)}, u32[]{:S(2)}) collective-permute-start(bf16[168,1536]{1,0:T(8,128)(2,1)S(1)} %pad_maximum_fusion.5), channel_id=1, source_target_pairs={{0,0},{1,2},{2,4},{3,6},{4,8},{5,10},{6,12},{7,14},{8,16},{9,18},{... | collective-permute-start | bytes 1548296 | tf_op jit(solution)/shard_map/ppermute | solution.py:599
  32.0 77.2 %all-to-all-start = ((bf16[32,48,1408]{2,1,0:T(8,128)(2,1)}), bf16[32,48,1408]{2,1,0:T(8,128)(2,1)}, u32[]{:S(2)}, u32[]{:S(2)}) async-start(bf16[32,48,1408]{2,1,0:T(8,128)(2,1)} %broadcast_in_dim.46), calls=%async_computation | async-start | bytes 8650752 | tf_op jit(solution)/shard_map/all_to_all | solution.py:69
  119.4 50.1 %all-to-all-start.1 = ((bf16[32,3,96,128]{3,2,1,0:T(8,128)(2,1)}), bf16[32,3,96,128]{3,2,1,0:T(8,128)(2,1)S(1)}, u32[]{:S(2)}, u32[]{:S(2)}) async-start(bf16[32,3,96,128]{3,2,1,0:T(8,128)(2,1)} %bitcast.73), calls=%async_computation.1 | async-start | bytes 4718592 | tf_op jit(solution)/shard_map/all_to_all | solution.py:69
  131.4 398.1 %reduce-scatter.2.cloned.1.call-start = ((), (), s32[]{:S(2)}) async-start(), calls=%async_computation.9 | async-start | bytes 20054016 | tf_op jit(solution)/shard_map/reduce_scatter | solution.py:679
  253.1 4.9 collective-permute-start.6
  293.1 4.4 collective-permute-start.7
  307.4 22.2 %all-to-all-start.3 = ((bf16[32,3,32,128]{3,2,1,0:T(8,128)(2,1)}), bf16[32,3,32,128]{3,2,1,0:T(8,128)(2,1)S(1)}, u32[]{:S(2)}, u32[]{:S(2)}) async-start(bf16[32,3,32,128]{3,2,1,0:T(8,128)(2,1)} %bitcast.20), calls=%async_computation.3 | async-start | bytes 1572864 | tf_op jit(solution)/shard_map/all_to_all | solution.py:69
  329.6 48.2 %all-to-all-start.4 = ((bf16[32,48,768]{2,1,0:T(8,128)(2,1)}), bf16[32,48,768]{2,1,0:T(8,128)(2,1)}, u32[]{:S(2)}, u32[]{:S(2)}) async-start(bf16[32,48,768]{2,1,0:T(8,128)(2,1)} %bitcast.79), calls=%async_computation.4 | async-start | bytes 4718592 | tf_op jit(solution)/shard_map/all_to_all | solution.py:69
  438.2 74.6 %all-to-all-start.6 = ((bf16[32,48,1280]{2,1,0:T(8,128)(2,1)}), bf16[32,48,1280]{2,1,0:T(8,128)(2,1)}, u32[]{:S(2)}, u32[]{:S(2)}) async-start(bf16[32,48,1280]{2,1,0:T(8,128)(2,1)} %bitcast.80), calls=%async_computation.6 | async-start | bytes 7864320 | tf_op jit(solution)/shard_map/all_to_all | solution.py:69
  452.9 4.8 collective-permute-start.10
  459.7 30.9 %collective-permute-start.12 = (f32[2,1536]{1,0:T(2,128)S(1)}, f32[2,1536]{1,0:T(2,128)S(1)}, u32[]{:S(2)}, u32[]{:S(2)}) collective-permute-start(f32[2,1536]{1,0:T(2,128)S(1)} %fusion.31), channel_id=1, source_target_pairs={{0,64},{64,1},{1,65},{65,0},{2,66},{66,3},{3,67},{67,2},{4,68},{68... | collective-permute-start | bytes 36872 | tf_op jit(solution)/shard_map/ppermute | solution.py:502
  460.5 32.4 %collective-permute-start.13 = (f32[2,1536]{1,0:T(2,128)S(1)}, f32[2,1536]{1,0:T(2,128)S(1)}, u32[]{:S(2)}, u32[]{:S(2)}) collective-permute-start(f32[2,1536]{1,0:T(2,128)S(1)} %fusion.31), channel_id=1, source_target_pairs={{0,1},{64,65},{1,0},{65,64},{2,3},{66,67},{3,2},{67,66},{4,5},{68,... | collective-permute-start | bytes 36872 | tf_op jit(solution)/shard_map/ppermute | solution.py:502
  463.4 29.6 %collective-permute-start.14 = (f32[2,1536]{1,0:T(2,128)S(1)}, f32[2,1536]{1,0:T(2,128)S(1)}, u32[]{:S(2)}, u32[]{:S(2)}) collective-permute-start(f32[2,1536]{1,0:T(2,128)S(1)} %fusion.31), channel_id=1, source_target_pairs={{0,65},{64,0},{1,64},{65,1},{2,67},{66,2},{3,66},{67,3},{4,69},{68... | collective-permute-start | bytes 36872 | tf_op jit(solution)/shard_map/ppermute | solution.py:502
  493.0 10.6 %collective-permute-start.15 = (f32[2,1536]{1,0:T(2,128)S(1)}, f32[2,1536]{1,0:T(2,128)S(1)}, u32[]{:S(2)}, u32[]{:S(2)}) collective-permute-start(f32[2,1536]{1,0:T(2,128)S(1)} %add_add_fusion.1), channel_id=1, source_target_pairs={{0,2},{2,4},{4,6},{6,0},{1,3},{3,5},{5,7},{7,1},{8,10},{10,12},{12... | collective-permute-start | bytes 36872 | tf_op jit(solution)/shard_map/ppermute | solution.py:503
  494.0 9.6 %collective-permute-start.16 = (f32[2,1536]{1,0:T(2,128)S(1)}, f32[2,1536]{1,0:T(2,128)S(1)}, u32[]{:S(2)}, u32[]{:S(2)}) collective-permute-start(f32[2,1536]{1,0:T(2,128)S(1)} %add_add_fusion.1), channel_id=1, source_target_pairs={{0,4},{2,6},{4,0},{6,2},{1,5},{3,7},{5,1},{7,3},{8,12},{10,14},{12... | collective-permute-start | bytes 36872 | tf_op jit(solution)/shard_map/ppermute | solution.py:503
  494.5 14.4 %collective-permute-start.17 = (f32[2,1536]{1,0:T(2,128)S(1)}, f32[2,1536]{1,0:T(2,128)S(1)}, u32[]{:S(2)}, u32[]{:S(2)}) collective-permute-start(f32[2,1536]{1,0:T(2,128)S(1)} %add_add_fusion.1), channel_id=1, source_target_pairs={{0,6},{2,0},{4,2},{6,4},{1,7},{3,1},{5,3},{7,5},{8,14},{10,8},{12,... | collective-permute-start | bytes 36872 | tf_op jit(solution)/shard_map/ppermute | solution.py:503
  508.9 9.3 %collective-permute-start.18 = (f32[2,1536]{1,0:T(2,128)S(1)}, f32[2,1536]{1,0:T(2,128)S(1)}, u32[]{:S(2)}, u32[]{:S(2)}) collective-permute-start(f32[2,1536]{1,0:T(2,128)S(1)} %add_add_fusion), channel_id=1, source_target_pairs={{0,8},{8,16},{16,24},{24,0},{1,9},{9,17},{17,25},{25,1},{2,10},{10... | collective-permute-start | bytes 36872 | tf_op jit(solution)/shard_map/ppermute | solution.py:503
  509.9 8.4 %collective-permute-start.19 = (f32[2,1536]{1,0:T(2,128)S(1)}, f32[2,1536]{1,0:T(2,128)S(1)}, u32[]{:S(2)}, u32[]{:S(2)}) collective-permute-start(f32[2,1536]{1,0:T(2,128)S(1)} %add_add_fusion), channel_id=1, source_target_pairs={{0,16},{8,24},{16,0},{24,8},{1,17},{9,25},{17,1},{25,9},{2,18},{10... | collective-permute-start | bytes 36872 | tf_op jit(solution)/shard_map/ppermute | solution.py:503
  511.0 7.3 %collective-permute-start.20 = (f32[2,1536]{1,0:T(2,128)S(1)}, f32[2,1536]{1,0:T(2,128)S(1)}, u32[]{:S(2)}, u32[]{:S(2)}) collective-permute-start(f32[2,1536]{1,0:T(2,128)S(1)} %add_add_fusion), channel_id=1, source_target_pairs={{0,24},{8,0},{16,8},{24,16},{1,25},{9,1},{17,9},{25,17},{2,26},{10... | collective-permute-start | bytes 36872 | tf_op jit(solution)/shard_map/ppermute | solution.py:503
  515.6 4.1 collective-permute-start.21
  519.8 7.1 %collective-permute-start.22 = (bf16[48,1280]{1,0:T(8,128)(2,1)S(1)}, bf16[48,1280]{1,0:T(8,128)(2,1)S(1)}, u32[]{:S(2)}, u32[]{:S(2)}) collective-permute-start(bf16[48,1280]{1,0:T(8,128)(2,1)S(1)} %add_convert_fusion.3), channel_id=1, source_target_pairs={{0,32},{32,0},{1,33},{33,1},{2,34},{34,2},{3,35},{35,3},{4,36},{36... | collective-permute-start | bytes 368648 | tf_op jit(solution)/shard_map/ppermute | solution.py:65
  530.7 13.6 %collective-permute-start.25 = (bf16[120,768]{1,0:T(8,128)(2,1)S(1)}, bf16[120,768]{1,0:T(8,128)(2,1)S(1)}, u32[]{:S(2)}, u32[]{:S(2)}) collective-permute-start(bf16[120,768]{1,0:T(8,128)(2,1)S(1)} %get-tuple-element.63), channel_id=1, source_target_pairs={{0,1},{1,0},{2,3},{3,2},{4,5},{5,4},{6,7},{7,6},{8,9},{9,8},{10,11... | collective-permute-start | bytes 552968 | tf_op jit(solution)/shard_map/ppermute | solution.py:513
  532.8 11.5 %collective-permute-start.26 = (bf16[120,768]{1,0:T(8,128)(2,1)S(1)}, bf16[120,768]{1,0:T(8,128)(2,1)S(1)}, u32[]{:S(2)}, u32[]{:S(2)}) collective-permute-start(bf16[120,768]{1,0:T(8,128)(2,1)S(1)} %get-tuple-element.63), channel_id=1, source_target_pairs={{0,65},{1,64},{64,1},{65,0},{2,67},{3,66},{66,3},{67,2},{4,69},{5,... | collective-permute-start | bytes 552968 | tf_op jit(solution)/shard_map/ppermute | solution.py:559
  533.5 5.8 collective-permute-start.23
  533.7 9.5 %collective-permute-start.24 = (bf16[120,768]{1,0:T(8,128)(2,1)S(1)}, bf16[120,768]{1,0:T(8,128)(2,1)S(1)}, u32[]{:S(2)}, u32[]{:S(2)}) collective-permute-start(bf16[120,768]{1,0:T(8,128)(2,1)S(1)} %get-tuple-element.62), channel_id=1, source_target_pairs={{0,64},{64,0},{1,65},{65,1},{2,66},{66,2},{3,67},{67,3},{4,68},{68... | collective-permute-start | bytes 552968 | tf_op jit(solution)/shard_map/ppermute | solution.py:513
  535.2 24.9 %collective-permute-start.30 = (bf16[48,4096]{1,0:T(8,128)(2,1)S(1)}, bf16[48,4096]{1,0:T(8,128)(2,1)S(1)}, u32[]{:S(2)}, u32[]{:S(2)}) collective-permute-start(bf16[48,4096]{1,0:T(8,128)(2,1)S(1)} %get-tuple-element.49), channel_id=1, source_target_pairs={{0,1},{1,0},{2,3},{3,2},{4,5},{5,4},{6,7},{7,6},{8,9},{9,8},{10,11... | collective-permute-start | bytes 1179656 | tf_op jit(solution)/shard_map/ppermute | solution.py:513
  539.3 20.9 %collective-permute-start.31 = (bf16[48,4096]{1,0:T(8,128)(2,1)S(1)}, bf16[48,4096]{1,0:T(8,128)(2,1)S(1)}, u32[]{:S(2)}, u32[]{:S(2)}) collective-permute-start(bf16[48,4096]{1,0:T(8,128)(2,1)S(1)} %get-tuple-element.49), channel_id=1, source_target_pairs={{0,65},{1,64},{64,1},{65,0},{2,67},{3,66},{66,3},{67,2},{4,69},{5,... | collective-permute-start | bytes 1179656 | tf_op jit(solution)/shard_map/ppermute | solution.py:559
  543.2 16.9 %collective-permute-start.29 = (bf16[48,4096]{1,0:T(8,128)(2,1)S(1)}, bf16[48,4096]{1,0:T(8,128)(2,1)S(1)}, u32[]{:S(2)}, u32[]{:S(2)}) collective-permute-start(bf16[48,4096]{1,0:T(8,128)(2,1)S(1)} %get-tuple-element.48), channel_id=1, source_target_pairs={{0,64},{64,0},{1,65},{65,1},{2,66},{66,2},{3,67},{67,3},{4,68},{68... | collective-permute-start | bytes 1179656 | tf_op jit(solution)/shard_map/ppermute | solution.py:513
  544.4 22.1 %collective-permute-start.27 = (bf16[168,768]{1,0:T(8,128)(2,1)S(1)}, bf16[168,768]{1,0:T(8,128)(2,1)S(1)}, u32[]{:S(2)}, u32[]{:S(2)}) collective-permute-start(bf16[168,768]{1,0:T(8,128)(2,1)S(1)} %pad_maximum_fusion.8), channel_id=1, source_target_pairs={{0,0},{2,1},{4,2},{6,3},{8,4},{10,5},{12,6},{14,7},{16,8},{18,9},{... | collective-permute-start | bytes 774152 | tf_op jit(solution)/shard_map/ppermute | solution.py:710
  566.6 3.2 collective-permute-start.32
  (50 other events, 296.7 us)
Sparse Core Ops, SparseCore 0:
  28.2 218.6 all-gather.1
  292.7 222.5 reduce-scatter.1

commit v5 on v3

--- a/solution.py
+++ b/solution.py
@@ -571,15 +571,11 @@
     return wide_sum(keep, flip(keep, "xl"), flip(send, "xh"), cross)
 
 
-def return_rows(rows, a, b):
-    pairs = []
-    for xl in range(2):
-        for c in range(2):
-            for j in range(16):
-                for xh in range(2):
-                    source = ((xl * 2 + c) * 16 + j) * 2 + xh
-                    pairs.append((source, ((xl ^ b) * 2 + (xh ^ a)) * SHARDS + 16 * c + j))
-    return lax.ppermute(rows, ("xl", "c") + SHARD, pairs)
+def to_owner(values, a):
+    pairs = [
+        ((c * 16 + j) * 2 + xh, (xh ^ a) * SHARDS + 16 * c + j) for c in range(2) for j in range(16) for xh in range(2)
+    ]
+    return lax.ppermute(values, ("c",) + SHARD, pairs)
 
 
 def add_pair(values, axis):
@@ -712,7 +708,6 @@
     d_qkv = collect(exchange(unit_d), tables)
 
     g_qkv = t_product(n1, d_qkv).astype(low)
-    s_qkv = scatter_sum(g_qkv.reshape(SHARDS, 48, HQ + 2 * HK))
     dn1_both = product_t(d_qkv, w_qkv)
     dn1 = dn1_both[:ROWS] + swap(dn1_both[ROWS:].astype(low)).astype(jnp.float32)
     z1 = x * r1
@@ -720,21 +715,19 @@
     g_gain_attn = jnp.sum(dn1 * z1, axis=0)
     grad_in = (dh + r1 * (e1 - z1 * jnp.mean(e1 * z1, axis=-1, keepdims=True))).astype(low)
 
-    gains = jnp.stack([g_gain_attn, g_gain_ffn])
-    gains = gains + swap(gains)
-    gains = total_axis(total_axis(total_axis(gains, "x"), "y"), "z")
-    gains = lax.dynamic_slice_in_dim(gains, shard * 48, 48, axis=1)
-    s_all = after(s_all, gains)
-    rows = jnp.concatenate(
-        [
-            unfold(s_all[None, :, OUT_AT:], 2)[0],
-            s_all[:, :D],
-            unfold(s_all[None, :, REST_AT:GATE_AT], 3)[0][:24],
-        ],
-        axis=0,
-    )
-    rows = sum(return_rows(rows, a, b).astype(jnp.float32) for a in range(2) for b in range(2))
-    s_gu = reduce_x(s_all[:, GATE_AT:OUT_AT])
+    gains = jnp.concatenate(
+        [g_gain_attn[:, None].astype(low), g_gain_ffn[:, None].astype(low), jnp.zeros((D, 126), low)], axis=1
+    )
+    g_qkv = jnp.concatenate([g_qkv, gains], axis=1)
+    s_qkv = add_pair(scatter_sum(g_qkv.reshape(SHARDS, 48, QKV + 128)), "xl")
+    s_all = reduce_x(after(s_all, d_qkv))
+    rows = jnp.concatenate([s_all[:, :GATE_AT], s_all[:, OUT_AT:]], axis=1)
+    here, there = to_owner(rows, 0), to_owner(rows, 1)
+    rows = jnp.concatenate([jnp.where(core == 0, here, there), jnp.where(core == 0, there, here)], axis=0)
+    g_o = unfold(rows[None, :, GATE_AT:], 2)[0].astype(jnp.float32)
+    rest = unfold(rows[None, :, REST_AT:GATE_AT], 3)[0][:24]
+    g_d = jnp.concatenate([rows[:, :D], rest], axis=0).astype(jnp.float32)
+    s_gu = s_all[:, GATE_AT:OUT_AT]
     s_gu = jnp.concatenate([crop_units(s_gu[:, :PAD_FF]), crop_units(s_gu[:, PAD_FF:])], axis=1)
     other = swap(s_gu)
     lower = core == 0
@@ -742,9 +735,9 @@
         jnp.concatenate([jnp.where(lower, m, t), jnp.where(lower, t, m)], axis=1).astype(jnp.float32)
         for m, t in ((s_gu[:, :HF], other[:, :HF]), (s_gu[:, HF:], other[:, HF:]))
     ]
-    s_qkv = add_pair(s_qkv, "xl")
     other = swap(s_qkv)
     whole = [jnp.where(lower, s_qkv, other), jnp.where(lower, other, s_qkv)]
+    gains = s_qkv[:, QKV : QKV + 2].astype(jnp.float32) + other[:, QKV : QKV + 2].astype(jnp.float32)
 
     def heads_of(offset):
         return jnp.concatenate(
@@ -754,15 +747,15 @@
     return (
         result.reshape(1, MB, SPAN, D).astype(low),
         grad_in.reshape(1, MB, SPAN, D),
-        gains[0],
+        gains[:, 0],
         jnp.concatenate([from_groups(w[:, :HQ]) for w in whole], axis=1).astype(jnp.float32),
         heads_of(0),
         heads_of(HD),
-        rows[:48],
-        gains[1],
+        g_o,
+        gains[:, 1],
         g_g,
         g_u,
-        rows[48:],
+        g_d,
     )
 
 

time: 640 us -> 602 us (0.941)
  waiting for transfers between devices: 278 us -> 244 us
  local copies, waits for them, and re-layouts: 22.6 us -> 37.9 us
  starting transfers between devices: 85.7 us -> 71.6 us
    ppermute x13 -> x2, waiting for transfers between devices: 106 us -> 17.6 us  [to_owner(): return lax.ppermute(values, ('c',) + SHARD, pairs)]
    all_to_all x3, waiting for transfers between devices: 89.6 us -> 152 us  [exchange(): return lax.all_to_all(values, SHARD, 0, 0, tiled=True)]
    reduce_scatter x1, waiting for transfers between devices: 21.1 us -> 0.01 us  [on_device(): s_all = lax.psum_scatter(g_all, ('z', 'y'), scatter_dimension=0, tiled=True)]
    ppermute x1, waiting for transfers between devices: 0.01 us -> 19.5 us  [reduce_x(): cross = lax.ppermute(send, ('xl', 'xh'), [(i, 3 - i) for i in range(4)])]
    ppermute x13 -> x2, starting transfers between devices: 27.2 us -> 13 us  [to_owner(): return lax.ppermute(values, ('c',) + SHARD, pairs)]
    concatenate x0 -> x1, local copies, waits for them, and re-layouts: none -> 7.75 us  [on_device(): g_qkv = jnp.concatenate([g_qkv, gains], axis=1)]
    ppermute x12 -> x11, starting transfers between devices: 12.3 us -> 13.6 us  [swap(): return lax.ppermute(values, 'c', [(0, 1), (1, 0)])]
  transfers between devices with their start and end apart: 36 -> 24, of which waited for: 25 -> 18; matrix products, arithmetic and copies ran while one was open for 7% -> 10% of each run, Pallas kernels for 9% -> 9%
where the time goes in v5:
time: 602 us; the launch traced here: 592 us
  waiting for transfers between devices  244 us (41%)
  blocking collectives  94.1 us (16%)
  Pallas kernels  91.4 us (15%)
  starting transfers between devices  71.6 us (12%)
  local copies, waits for them, and re-layouts  37.9 us (6%)
  other arithmetic  30.4 us (5%)
  between operations  15.2 us (3%)
  matrix products  8.12 us (1%)
    all_to_all x3, waiting for transfers between devices, exchange(): return lax.all_to_all(values, SHARD, 0, 0, tiled=True)  152 us
    all_to_all x3, blocking collectives, exchange(): return lax.all_to_all(values, SHARD, 0, 0, tiled=True)  94.1 us
    all_to_all x3, starting transfers between devices, exchange(): return lax.all_to_all(values, SHARD, 0, 0, tiled=True)  33.6 us
    all_gather x1, waiting for transfers between devices, on_device(): lax.all_gather(jnp.concatenate([rows_in[48:144], fold(jnp.pad(rows_in[144...  32.4 us
    pallas_call x1, Pallas kernels, feed_forward(): pl.pallas_call(ffn_kernel, grid=(FF_TILES,), in_specs=[whole_spec(BOTH, D...  30.3 us
    pallas_call x1, Pallas kernels, attend_bwd(): pl.pallas_call(bwd_kernel, grid=(MB,), in_specs=[SMEM, SMEM, UNIT_SPEC, C...  26.8 us
    ppermute x1, waiting for transfers between devices, reduce_x(): cross = lax.ppermute(send, ('xl', 'xh'), [(i, 3 - i) for i in range(4)])  19.5 us
    pallas_call x1, Pallas kernels, attend_fwd(): pl.pallas_call(fwd_kernel, grid=(MB,), in_specs=[SMEM, SMEM, UNIT_SPEC, C...  18.9 us
  transfers between devices with their start and end apart: 24, of which 18 were waited for; matrix products, arithmetic and copies ran while one was open for 10% of the time, Pallas kernels for 9%

profile of v5, /device:TPU:49, one launch (start us, length us, event | category | flops | bytes accessed | tf_op | source)
XLA Modules:
  0.0 592.3 jit_solution(18232537329011981571)
XLA Ops:
  12.2 5.2 collective-permute-start.2
  17.4 3.5 collective-permute-done.3
  21.0 5.7 collective-permute-done.2
  31.9 11.7 %all-to-all-start = ((bf16[32,48,1408]{2,1,0:T(8,128)(2,1)}), bf16[32,48,1408]{2,1,0:T(8,128)(2,1)}, u32[]{:S(2)}, u32[]{:S(2)}) async-start(bf16[32,48,1408]{2,1,0:T(8,128)(2,1)} %broadcast_in_dim.25), calls=%async_computation | async-start | bytes 8650752 | tf_op jit(solution)/shard_map/all_to_all | solution.py:69
  46.6 62.5 %all-to-all-done = bf16[32,48,1408]{2,1,0:T(8,128)(2,1)} async-done(((bf16[32,48,1408]{2,1,0:T(8,128)(2,1)}), bf16[32,48,1408]{2,1,0:T(8,128)(2,1)}, u32[]{:S(2)}, u32[]{:S(2)}) %all-to-all-start) | async-done | bytes 4325408 | tf_op jit(solution)/shard_map/all_to_all | solution.py:69
  111.3 6.0 %project.1 = bf16[4,2,4,3,96,128]{5,4,3,2,1,0:T(8,128)(2,1)S(1)} custom-call(bf16[384,1536]{1,0:T(8,128)(2,1)S(1)} %fusion.4.n_ref, bf16[1536,1408]{1,0:T(8,128)(2,1)} %bitcast.7.w_ref, f32[4,64,128]{2,1,0:T(8,128)S(1)} %pad_maximum_fusion.8.table_ref), custom_call_target="tpu_custom_call" | custom-call | flops 6000000000 | bytes 1048576 | tf_op jit(solution)/shard_map/project/pallas_call | solution.py:318
  118.8 12.0 %all-to-all-start.1 = ((bf16[32,3,96,128]{3,2,1,0:T(8,128)(2,1)}), bf16[32,3,96,128]{3,2,1,0:T(8,128)(2,1)S(1)}, u32[]{:S(2)}, u32[]{:S(2)}) async-start(bf16[32,3,96,128]{3,2,1,0:T(8,128)(2,1)} %bitcast.67), calls=%async_computation.1 | async-start | bytes 4718592 | tf_op jit(solution)/shard_map/all_to_all | solution.py:69
  135.4 5.8 convert_reduce_fusion
  142.0 26.8 %all-to-all-done.1.u_ref = bf16[32,3,96,128]{3,2,1,0:T(8,128)(2,1)S(1)} async-done(((bf16[32,3,96,128]{3,2,1,0:T(8,128)(2,1)}), bf16[32,3,96,128]{3,2,1,0:T(8,128)(2,1)S(1)}, u32[]{:S(2)}, u32[]{:S(2)}) %all-to-all-start.1) | async-done | bytes 2359328 | tf_op jit(solution)/shard_map/all_to_all | solution.py:69
  171.2 18.9 %attend_forward.1 = (bf16[32,3,32,128]{3,2,1,0:T(8,128)(2,1)S(1)}, f32[3,8,192,128]{3,2,1,0:T(8,128)S(1)}) custom-call(s32[2]{0:T(128)S(1)} %pad_add_fusion.unit_ref, s32[24]{0:T(128)S(1)} %and_select_fusion.first_ref, bf16[32,3,96,128]{3,2,1,0:T(8,128)(2,1)S(1)} %all-to-all-done.1.u_ref, s32[3,8,192,128]{3,2,1,0:T(8,128)} %broadcast_in_dim.57.start_ref), custom_call_target="tpu_custom_call" | custom-call | flops 20000000000 | bytes 1048576 | tf_op jit(solution)/shard_map/attend_forward/pallas_call | solution.py:480
  191.4 23.0 %all_to_all.30 = bf16[32,3,32,128]{3,2,1,0:T(8,128)(2,1)S(1)} all-to-all(bf16[32,3,32,128]{3,2,1,0:T(8,128)(2,1)S(1)} %get-tuple-element.24), channel_id=1, replica_groups=mesh['xl'=2,'c'=2,'z'=4,'y'=4,'xh'=2] {'z','y','xh'}, dimensions={0} | all-to-all | bytes 1572864 | tf_op jit(solution)/shard_map/all_to_all | solution.py:69
  214.5 32.4 %all-gather.2.cloned.1.call-done.w_ref.main_ref.rest_ref.gate_ref.up_ref = bf16[1536,6912]{1,0:T(8,128)(2,1)} async-done(((bf16[96,6912]{1,0:T(8,128)(2,1)}), bf16[1536,6912]{1,0:T(8,128)(2,1)}) %all-gather.2.cloned.1.call-update) | async-done | bytes 21233680 | tf_op jit(solution)/shard_map/all_gather | solution.py:619
  246.9 3.6 out_project.1
  259.9 30.3 %feed_forward.1 = (f32[192,1536]{1,0:T(8,128)S(1)}, bf16[192,1536]{1,0:T(8,128)(2,1)S(1)}, f32[192,1536]{1,0:T(8,128)S(1)}, bf16[192,1536]{1,0:T(8,128)(2,1)S(1)}, bf16[1536,6912]{1,0:T(8,128)(2,1)}) custom-call(bf16[384,1536]{1,0:T(8,128)(2,1)S(1)} %pad_maximum_fusion.2.n_ref, bf16[384,1536]{1,0:T(8,128)(2,1)S(1)} %multiply_convert_fusion.df_ref, ...), custom_call_target="tpu_custom_call" | custom-call | flops 30000001024 | bytes 1048576 | tf_op jit(solution)/shard_map/feed_forward/pallas_call | solution.py:443
  298.3 4.9 d_out_project.1
  303.2 22.1 %all_to_all.31.do_ref = bf16[32,3,32,128]{3,2,1,0:T(8,128)(2,1)S(1)} all-to-all(bf16[32,3,32,128]{3,2,1,0:T(8,128)(2,1)S(1)} %bitcast.69), channel_id=1, replica_groups=mesh['xl'=2,'c'=2,'z'=4,'y'=4,'xh'=2] {'z','y','xh'}, dimensions={0} | all-to-all | bytes 1572864 | tf_op jit(solution)/shard_map/all_to_all | solution.py:69
  325.2 26.8 %attend_backward.1 = bf16[32,3,96,128]{3,2,1,0:T(8,128)(2,1)S(1)} custom-call(s32[2]{0:T(128)S(1)} %pad_add_fusion.unit_ref, s32[24]{0:T(128)S(1)} %and_select_fusion.first_ref, bf16[32,3,96,128]{3,2,1,0:T(8,128)(2,1)S(1)} %all-to-all-done.1.u_ref, s32[3,8,192,128]{3,2,1,0:T(8,128)} %broadcast_in_dim.57.start_ref, ...), custom_call_target="tpu_custom_call" | custom-call | flops 27000000512 | bytes 1048576 | tf_op jit(solution)/shard_map/attend_backward/pallas_call | solution.py:493
  352.1 49.0 %all_to_all.32 = bf16[32,3,96,128]{3,2,1,0:T(8,128)(2,1)S(1)} all-to-all(bf16[32,3,96,128]{3,2,1,0:T(8,128)(2,1)S(1)} %attend_backward.1), channel_id=1, replica_groups=mesh['xl'=2,'c'=2,'z'=4,'y'=4,'xh'=2] {'z','y','xh'}, dimensions={0} | all-to-all | bytes 4718592 | tf_op jit(solution)/shard_map/all_to_all | solution.py:69
  401.9 3.9 fusion
  408.1 3.7 collective-permute-start.10
  413.2 4.2 convolution_convert_fusion
  418.9 7.8 %concatenate.92 = bf16[32,48,1408]{2,1,0:T(8,128)(2,1)} concatenate(bf16[32,48,1280]{2,1,0:T(8,128)(2,1)} %bitcast.74, bf16[32,48,1]{2,1,0:T(8,128)(2,1)S(1)} %convert_element_type.249, bf16[32,48,1]{2,1,0:T(8,128)(2,1)S(1)} %copy-done.12, bf16[32,48,126]{2,1,0:T(8,128)(2,1)S(1)} %broadcast_in_dim.58), dimensions={2} | concatenate | bytes 8650752 | tf_op jit(solution)/shard_map/concatenate | solution.py:721
  426.6 9.9 %all-to-all-start.5 = ((bf16[32,48,1408]{2,1,0:T(8,128)(2,1)}), bf16[32,48,1408]{2,1,0:T(8,128)(2,1)}, u32[]{:S(2)}, u32[]{:S(2)}) async-start(bf16[32,48,1408]{2,1,0:T(8,128)(2,1)} %concatenate.92), calls=%async_computation.5 | async-start | bytes 8650752 | tf_op jit(solution)/shard_map/all_to_all | solution.py:69
  436.5 62.8 %all-to-all-done.5 = bf16[32,48,1408]{2,1,0:T(8,128)(2,1)} async-done(((bf16[32,48,1408]{2,1,0:T(8,128)(2,1)}), bf16[32,48,1408]{2,1,0:T(8,128)(2,1)}, u32[]{:S(2)}, u32[]{:S(2)}) %all-to-all-start.5) | async-done | bytes 4325408 | tf_op jit(solution)/shard_map/all_to_all | solution.py:69
  499.3 3.1 reduce_sum.82
  502.5 4.2 collective-permute-done.11
  506.8 3.2 collective-permute-start.12
  527.8 19.5 %collective-permute-done.15 = bf16[48,6912]{1,0:T(8,128)(2,1)S(1)} collective-permute-done((bf16[48,6912]{1,0:T(8,128)(2,1)S(1)}, bf16[48,6912]{1,0:T(8,128)(2,1)S(1)}, u32[]{:S(2)}, u32[]{:S(2)}) %collective-permute-start.15) | collective-permute-done | bytes 663584 | tf_op jit(solution)/shard_map/ppermute | solution.py:570
  548.1 9.7 %collective-permute-start.16 = (bf16[48,2816]{1,0:T(8,128)(2,1)S(1)}, bf16[48,2816]{1,0:T(8,128)(2,1)S(1)}, u32[]{:S(2)}, u32[]{:S(2)}) collective-permute-start(bf16[48,2816]{1,0:T(8,128)(2,1)S(1)} %pad_maximum_fusion.6), channel_id=1, source_target_pairs={{0,0},{1,32},{2,1},{3,33},{4,2},{5,34},{6,3},{7,35},{8,4},{9,36},{... | collective-permute-start | bytes 811016 | tf_op jit(solution)/shard_map/ppermute | solution.py:578
  557.9 3.3 collective-permute-start.17
  563.3 11.8 %collective-permute-done.16 = bf16[48,2816]{1,0:T(8,128)(2,1)S(1)} collective-permute-done((bf16[48,2816]{1,0:T(8,128)(2,1)S(1)}, bf16[48,2816]{1,0:T(8,128)(2,1)S(1)}, u32[]{:S(2)}, u32[]{:S(2)}) %collective-permute-start.16) | collective-permute-done | bytes 270368 | tf_op jit(solution)/shard_map/ppermute | solution.py:578
  575.1 5.8 collective-permute-done.17
  (194 shorter events, 73.8 us)
Async XLA Ops:
  7.2 239.7 %all-gather.2.cloned.1.call-start = ((), (), s32[]{:S(2)}) async-start(), calls=%async_computation.7 | async-start | bytes 22560768 | tf_op jit(solution)/shard_map/all_gather | solution.py:619
  8.3 3.9 copy-start.14
  9.4 11.6 %collective-permute-start.3 = (bf16[48,4096]{1,0:T(8,128)(2,1)S(1)}, bf16[48,4096]{1,0:T(8,128)(2,1)S(1)}, u32[]{:S(2)}, u32[]{:S(2)}) collective-permute-start(bf16[48,4096]{1,0:T(8,128)(2,1)S(1)} %bitcast_dynamic-update-slice_fusion), channel_id=1, source_target_pairs={{0,1},{1,0},{2,3},{3,2},{4,5},{5,4},{6,7},{7,6},{8,9},{9,8},{10,11... | collective-permute-start | bytes 1179656 | tf_op jit(solution)/shard_map/ppermute | solution.py:524
  12.2 14.4 %collective-permute-start.2 = (bf16[168,1536]{1,0:T(8,128)(2,1)S(1)}, bf16[168,1536]{1,0:T(8,128)(2,1)S(1)}, u32[]{:S(2)}, u32[]{:S(2)}) collective-permute-start(bf16[168,1536]{1,0:T(8,128)(2,1)S(1)} %pad_maximum_fusion.4), channel_id=1, source_target_pairs={{0,0},{1,2},{2,4},{3,6},{4,8},{5,10},{6,12},{7,14},{8,16},{9,18},{... | collective-permute-start | bytes 1548296 | tf_op jit(solution)/shard_map/ppermute | solution.py:617
  31.9 11.7 %copy-start.7 = (bf16[1,3,64,1536]{3,2,1,0:T(8,128)(2,1)S(1)}, bf16[1,3,64,1536]{3,2,1,0:T(8,128)(2,1)}, u32[]{:S(2)}) copy-start(bf16[1,3,64,1536]{3,2,1,0:T(8,128)(2,1)} %param.12) | copy-start | bytes 1769476
  31.9 77.2 %all-to-all-start = ((bf16[32,48,1408]{2,1,0:T(8,128)(2,1)}), bf16[32,48,1408]{2,1,0:T(8,128)(2,1)}, u32[]{:S(2)}, u32[]{:S(2)}) async-start(bf16[32,48,1408]{2,1,0:T(8,128)(2,1)} %broadcast_in_dim.25), calls=%async_computation | async-start | bytes 8650752 | tf_op jit(solution)/shard_map/all_to_all | solution.py:69
  43.6 2.7 collective-permute-start.1
  111.3 6.0 %copy-start.2 = (bf16[384,1536]{1,0:T(8,128)(2,1)}, bf16[384,1536]{1,0:T(8,128)(2,1)S(1)}, u32[]{:S(2)}) copy-start(bf16[384,1536]{1,0:T(8,128)(2,1)S(1)} %fusion.4.n_ref) | copy-start | bytes 3538948
  118.8 50.0 %all-to-all-start.1 = ((bf16[32,3,96,128]{3,2,1,0:T(8,128)(2,1)}), bf16[32,3,96,128]{3,2,1,0:T(8,128)(2,1)S(1)}, u32[]{:S(2)}, u32[]{:S(2)}) async-start(bf16[32,3,96,128]{3,2,1,0:T(8,128)(2,1)} %bitcast.67), calls=%async_computation.1 | async-start | bytes 4718592 | tf_op jit(solution)/shard_map/all_to_all | solution.py:69
  130.7 383.2 %reduce-scatter.2.cloned.1.call-start = ((), (), s32[]{:S(2)}) async-start(), calls=%async_computation.8 | async-start | bytes 22560768 | tf_op jit(solution)/shard_map/reduce_scatter | solution.py:705
  132.6 2.8 collective-permute-start
  252.4 3.3 collective-permute-start.4
  253.1 5.1 collective-permute-start.6
  257.7 2.1 collective-permute-start.5
  290.2 2.1 collective-permute-start.8
  290.7 2.5 collective-permute-start.7
  296.2 2.0 collective-permute-start.9
  407.2 6.0 %copy-start.3 = (bf16[384,1536]{1,0:T(8,128)(2,1)S(1)}, bf16[384,1536]{1,0:T(8,128)(2,1)}, u32[]{:S(2)}) copy-start(bf16[384,1536]{1,0:T(8,128)(2,1)} %copy-done.2) | copy-start | bytes 3538948
  408.1 9.3 %collective-permute-start.10 = (bf16[192,1536]{1,0:T(8,128)(2,1)}, bf16[192,1536]{1,0:T(8,128)(2,1)S(1)}, u32[]{:S(2)}, u32[]{:S(2)}) collective-permute-start(bf16[192,1536]{1,0:T(8,128)(2,1)} %slice.417), channel_id=1, source_target_pairs={{0,32},{32,0},{1,33},{33,1},{2,34},{34,2},{3,35},{35,3},{4,36},{36... | collective-permute-start | bytes 1769480 | tf_op jit(solution)/shard_map/ppermute | solution.py:65
  413.2 4.2 copy-start.8
  413.2 4.2 copy-start.11
  426.6 72.7 %all-to-all-start.5 = ((bf16[32,48,1408]{2,1,0:T(8,128)(2,1)}), bf16[32,48,1408]{2,1,0:T(8,128)(2,1)}, u32[]{:S(2)}, u32[]{:S(2)}) async-start(bf16[32,48,1408]{2,1,0:T(8,128)(2,1)} %concatenate.92), calls=%async_computation.5 | async-start | bytes 8650752 | tf_op jit(solution)/shard_map/all_to_all | solution.py:69
  499.3 10.7 %copy-start.9 = (f32[192,1536]{1,0:T(8,128)S(1)}, f32[192,1536]{1,0:T(8,128)}, u32[]{:S(2)}) copy-start(f32[192,1536]{1,0:T(8,128)} %get-tuple-element.46) | copy-start | bytes 3538948
  502.4 4.3 collective-permute-start.11
  506.8 5.7 copy-start.13
  506.8 5.7 collective-permute-start.12
  515.3 32.0 %collective-permute-start.15 = (bf16[48,6912]{1,0:T(8,128)(2,1)S(1)}, bf16[48,6912]{1,0:T(8,128)(2,1)S(1)}, u32[]{:S(2)}, u32[]{:S(2)}) collective-permute-start(bf16[48,6912]{1,0:T(8,128)(2,1)S(1)} %get-tuple-element.48), channel_id=1, source_target_pairs={{0,65},{1,64},{64,1},{65,0},{2,67},{3,66},{66,3},{67,2},{4,69},{5,... | collective-permute-start | bytes 1990664 | tf_op jit(solution)/shard_map/ppermute | solution.py:570
  515.4 32.0 %collective-permute-start.14 = (bf16[48,6912]{1,0:T(8,128)(2,1)S(1)}, bf16[48,6912]{1,0:T(8,128)(2,1)S(1)}, u32[]{:S(2)}, u32[]{:S(2)}) collective-permute-start(bf16[48,6912]{1,0:T(8,128)(2,1)S(1)} %get-tuple-element.48), channel_id=1, source_target_pairs={{0,1},{1,0},{2,3},{3,2},{4,5},{5,4},{6,7},{7,6},{8,9},{9,8},{10,11... | collective-permute-start | bytes 1990664 | tf_op jit(solution)/shard_map/ppermute | solution.py:524
  517.0 30.7 %collective-permute-start.13 = (bf16[48,6912]{1,0:T(8,128)(2,1)S(1)}, bf16[48,6912]{1,0:T(8,128)(2,1)S(1)}, u32[]{:S(2)}, u32[]{:S(2)}) collective-permute-start(bf16[48,6912]{1,0:T(8,128)(2,1)S(1)} %get-tuple-element.47), channel_id=1, source_target_pairs={{0,64},{64,0},{1,65},{65,1},{2,66},{66,2},{3,67},{67,3},{4,68},{68... | collective-permute-start | bytes 1990664 | tf_op jit(solution)/shard_map/ppermute | solution.py:524
  548.1 27.0 %collective-permute-start.16 = (bf16[48,2816]{1,0:T(8,128)(2,1)S(1)}, bf16[48,2816]{1,0:T(8,128)(2,1)S(1)}, u32[]{:S(2)}, u32[]{:S(2)}) collective-permute-start(bf16[48,2816]{1,0:T(8,128)(2,1)S(1)} %pad_maximum_fusion.6), channel_id=1, source_target_pairs={{0,0},{1,32},{2,1},{3,33},{4,2},{5,34},{6,3},{7,35},{8,4},{9,36},{... | collective-permute-start | bytes 811016 | tf_op jit(solution)/shard_map/ppermute | solution.py:578
  557.9 23.0 %collective-permute-start.17 = (bf16[48,2816]{1,0:T(8,128)(2,1)S(1)}, bf16[48,2816]{1,0:T(8,128)(2,1)S(1)}, u32[]{:S(2)}, u32[]{:S(2)}) collective-permute-start(bf16[48,2816]{1,0:T(8,128)(2,1)S(1)} %pad_maximum_fusion.6), channel_id=1, source_target_pairs={{0,32},{1,0},{2,33},{3,1},{4,34},{5,2},{6,35},{7,3},{8,36},{9,4},{... | collective-permute-start | bytes 811016 | tf_op jit(solution)/shard_map/ppermute | solution.py:578
  561.7 21.4 %collective-permute-start.18 = (bf16[48,3840]{1,0:T(8,128)(2,1)S(1)}, bf16[48,3840]{1,0:T(8,128)(2,1)S(1)}, u32[]{:S(2)}, u32[]{:S(2)}) collective-permute-start(bf16[48,3840]{1,0:T(8,128)(2,1)S(1)} %pad_maximum_fusion.5), channel_id=1, source_target_pairs={{0,32},{32,0},{1,33},{33,1},{2,34},{34,2},{3,35},{35,3},{4,36},{36... | collective-permute-start | bytes 1105928 | tf_op jit(solution)/shard_map/ppermute | solution.py:65
  (15 other events, 22.0 us)
Sparse Core Ops, SparseCore 0:
  28.2 218.6 all-gather.1
  303.3 206.4 reduce-scatter.1

commit v6 on v4

--- a/solution.py
+++ b/solution.py
@@ -195,6 +195,12 @@
                     put(4 + k, o, m, at, CHUNK, third, 0, p * CHUNK)
 
 
+def gradient_kernel(n_ref, d_ref, gains_ref, out_ref):
+    out_ref[:, :QKV] = product(n_ref[...].T, d_ref[...]).astype(jnp.bfloat16)
+    gains = jnp.concatenate([gains_ref[...], jnp.zeros((120, D), jnp.float32)], axis=0)
+    out_ref[:, QKV:] = gains.T.astype(jnp.bfloat16)
+
+
 def stack_heads(first, third, odd):
     last = jnp.where(odd == 1, third[:, HD:], third[:, :HD])
     return jnp.concatenate([first[:, :HD], first[:, HD:], last], axis=0)
@@ -463,6 +469,16 @@
     return pl.pallas_call(collect_kernel, out_shape=shape, compiler_params=PARAMS, cost_estimate=cost(4), name="collect")(
         split_units(units), tables
     )
+
+
+def gradients(n1, d_qkv, gains):
+    return pl.pallas_call(
+        gradient_kernel,
+        out_shape=low_shape(D, QKV + 128),
+        compiler_params=PARAMS,
+        cost_estimate=cost(5),
+        name="gradients",
+    )(n1, d_qkv, gains)
 
 
 def attend_fwd(unit, first, units, starts):
@@ -690,9 +706,8 @@
     s_o = scatter_sum(after(g_o, unit_do))
     unit_d = attend_bwd(unit, first, units, starts, unit_do, lse)
     d_qkv = collect(exchange(after(unit_d, s_o)), tables)
-
-    g_qkv = t_product(n1, d_qkv).astype(low)
-    s_qkv = scatter_sum(g_qkv.reshape(SHARDS, 48, HQ + 2 * HK))
+    s_o = add_pair(s_o, "xl")
+
     dn1_both = product_t(d_qkv, w_qkv)
     dn1 = dn1_both[:ROWS] + swap(dn1_both[ROWS:].astype(low)).astype(jnp.float32)
     z1 = x * r1
@@ -700,15 +715,15 @@
     g_gain_attn = jnp.sum(dn1 * z1, axis=0)
     grad_in = (dh + r1 * (e1 - z1 * jnp.mean(e1 * z1, axis=-1, keepdims=True))).astype(low)
 
-    gains = jnp.stack([g_gain_attn, g_gain_ffn])
-    gains = gains + swap(gains)
-    gains = total_axis(total_axis(total_axis(gains, "x"), "y"), "z")
-    gains = lax.dynamic_slice_in_dim(gains, shard * 48, 48, axis=1)
-    s_ffn, s_o = after((s_ffn, s_o), gains)
+    gains = jnp.concatenate([g_gain_attn[None], g_gain_ffn[None], jnp.zeros((6, D), jnp.float32)], axis=0)
+    g_qkv = gradients(n1, d_qkv, gains)
+    received = exchange(g_qkv.reshape(SHARDS, 48, QKV + 128))
+    s_ffn = after(s_ffn, d_qkv)
     s_d = jnp.concatenate([s_ffn[:, :D], unfold(s_ffn[None, :, REST_AT:GATE_AT], 3)[0][:24]], axis=0)
-    rows = jnp.concatenate([add_pair(s_o, "xl"), reduce_x(s_d, 1)], axis=0)
-    rows = join_cores(lax.ppermute(rows, ("c",) + SHARD, [(b, a) for a, b in piece_perm()]))
+    rows_x = jnp.concatenate([s_o, reduce_x(s_d, 1)], axis=0)
+    rows = join_cores(lax.ppermute(rows_x, ("c",) + SHARD, [(b, a) for a, b in piece_perm()]))
     s_gu = reduce_x(s_ffn[:, GATE_AT:], 0)
+    received = after(received, (s_gu, rows_x))
     s_gu = jnp.concatenate([crop_units(s_gu[:, :PAD_FF]), crop_units(s_gu[:, PAD_FF:])], axis=1)
     other = swap(s_gu)
     lower = core == 0
@@ -716,9 +731,10 @@
         jnp.concatenate([jnp.where(lower, m, t), jnp.where(lower, t, m)], axis=1).astype(jnp.float32)
         for m, t in ((s_gu[:, :HF], other[:, :HF]), (s_gu[:, HF:], other[:, HF:]))
     ]
-    s_qkv = add_pair(s_qkv, "xl")
+    s_qkv = add_pair(jnp.sum(received.astype(jnp.float32), axis=0).astype(low), "xl")
     other = swap(s_qkv)
     whole = [jnp.where(lower, s_qkv, other), jnp.where(lower, other, s_qkv)]
+    gains = s_qkv[:, QKV : QKV + 2].astype(jnp.float32) + other[:, QKV : QKV + 2].astype(jnp.float32)
 
     def heads_of(offset):
         return jnp.concatenate(
@@ -728,12 +744,12 @@
     return (
         result.reshape(1, MB, SPAN, D).astype(low),
         grad_in.reshape(1, MB, SPAN, D),
-        gains[0],
+        gains[:, 0],
         jnp.concatenate([from_groups(w[:, :HQ]) for w in whole], axis=1).astype(jnp.float32),
         heads_of(0),
         heads_of(HD),
         rows[:48],
-        gains[1],
+        gains[:, 1],
         g_g,
         g_u,
         rows[48:],

time: 590 us -> 590 us (level)
  starting transfers between devices: 101 us -> 94.6 us
  waiting for transfers between devices: 221 us -> 227 us
    ppermute x10 -> x1, waiting for transfers between devices: 47.6 us -> 1.4 us  [on_device(): lax.ppermute(rows_x, ('c',) + SHARD, [(b, a) for a, b in piece_perm()])]
    ppermute x8, waiting for transfers between devices: 24.5 us -> 59.2 us  [flip(): return lax.ppermute(values, axis, [(0, 1), (1, 0)])]
    reduce_scatter x1, waiting for transfers between devices: 0.01 us -> 11.3 us  [on_device(): s_ffn = lax.psum_scatter(g_ffn, ('z', 'y'), scatter_dimension=0, tiled=True)]
    ppermute x12 -> x11, starting transfers between devices: 15 us -> 9.99 us  [swap(): return lax.ppermute(values, 'c', [(0, 1), (1, 0)])]
    ppermute x10 -> x1, starting transfers between devices: 13.6 us -> 12.8 us  [on_device(): lax.ppermute(rows_x, ('c',) + SHARD, [(b, a) for a, b in piece_perm()])]
  transfers between devices with their start and end apart: 40 -> 30, of which waited for: 26 -> 22; matrix products, arithmetic and copies ran while one was open for 9% -> 9% of each run, Pallas kernels for 10% -> 11%
where the time goes in v6:
time: 590 us; the launch traced here: 579 us
  waiting for transfers between devices  227 us (38%)
  Pallas kernels  96.4 us (16%)
  starting transfers between devices  94.6 us (16%)
  blocking collectives  76.4 us (13%)
  other arithmetic  36.8 us (6%)
  local copies, waits for them, and re-layouts  25.2 us (4%)
  between operations  15.4 us (3%)
  matrix products  6.85 us (1%)
    all_to_all x5, waiting for transfers between devices, exchange(): return lax.all_to_all(values, SHARD, 0, 0, tiled=True)  105 us
    all_to_all x2, blocking collectives, exchange(): return lax.all_to_all(values, SHARD, 0, 0, tiled=True)  76.4 us
    ppermute x8, waiting for transfers between devices, flip(): return lax.ppermute(values, axis, [(0, 1), (1, 0)])  59.2 us
    all_to_all x5, starting transfers between devices, exchange(): return lax.all_to_all(values, SHARD, 0, 0, tiled=True)  54.7 us
    all_gather x1, waiting for transfers between devices, on_device(): lax.all_gather(jnp.concatenate([rows_in[48:144], fold(jnp.pad(rows_in[144...  31.2 us
    pallas_call x1, Pallas kernels, feed_forward(): pl.pallas_call(ffn_kernel, grid=(FF_TILES,), in_specs=[whole_spec(BOTH, D...  30.3 us
    pallas_call x1, Pallas kernels, attend_bwd(): pl.pallas_call(bwd_kernel, grid=(MB,), in_specs=[SMEM, SMEM, UNIT_SPEC, C...  27.6 us
    pallas_call x1, Pallas kernels, attend_fwd(): pl.pallas_call(fwd_kernel, grid=(MB,), in_specs=[SMEM, SMEM, UNIT_SPEC, C...  19.3 us
  transfers between devices with their start and end apart: 30, of which 22 were waited for; matrix products, arithmetic and copies ran while one was open for 9% of the time, Pallas kernels for 11%

profile of v6, /device:TPU:49, one launch (start us, length us, event | category | flops | bytes accessed | tf_op | source)
XLA Modules:
  0.0 578.8 jit_solution(17974971287140575316)
XLA Ops:
  12.2 5.2 collective-permute-start.2
  17.4 3.5 collective-permute-done.3
  21.0 5.7 collective-permute-done.2
  32.0 11.7 %all-to-all-start = ((bf16[32,48,1408]{2,1,0:T(8,128)(2,1)}), bf16[32,48,1408]{2,1,0:T(8,128)(2,1)}, u32[]{:S(2)}, u32[]{:S(2)}) async-start(bf16[32,48,1408]{2,1,0:T(8,128)(2,1)} %broadcast_in_dim.55), calls=%async_computation | async-start | bytes 8650752 | tf_op jit(solution)/shard_map/all_to_all | solution.py:69
  46.7 62.5 %all-to-all-done = bf16[32,48,1408]{2,1,0:T(8,128)(2,1)} async-done(((bf16[32,48,1408]{2,1,0:T(8,128)(2,1)}), bf16[32,48,1408]{2,1,0:T(8,128)(2,1)}, u32[]{:S(2)}, u32[]{:S(2)}) %all-to-all-start) | async-done | bytes 4325408 | tf_op jit(solution)/shard_map/all_to_all | solution.py:69
  111.4 6.0 %project.1 = bf16[4,2,4,3,96,128]{5,4,3,2,1,0:T(8,128)(2,1)S(1)} custom-call(bf16[384,1536]{1,0:T(8,128)(2,1)S(1)} %fusion.4.n_ref, bf16[1536,1408]{1,0:T(8,128)(2,1)} %bitcast.7.w_ref, f32[4,64,128]{2,1,0:T(8,128)S(1)} %pad_maximum_fusion.9.table_ref), custom_call_target="tpu_custom_call" | custom-call | flops 6000000000 | bytes 1048576 | tf_op jit(solution)/shard_map/project/pallas_call | solution.py:316
  118.8 12.0 %all-to-all-start.1 = ((bf16[32,3,96,128]{3,2,1,0:T(8,128)(2,1)}), bf16[32,3,96,128]{3,2,1,0:T(8,128)(2,1)S(1)}, u32[]{:S(2)}, u32[]{:S(2)}) async-start(bf16[32,3,96,128]{3,2,1,0:T(8,128)(2,1)} %bitcast.67), calls=%async_computation.1 | async-start | bytes 4718592 | tf_op jit(solution)/shard_map/all_to_all | solution.py:69
  135.4 5.8 %convert_reduce_fusion = s32[3,2048]{1,0:T(4,128)S(1)} fusion(f32[3,2048]{1,0:T(4,128)S(1)} %select_convert_fusion), kind=kLoop, calls=%fused_computation | loop fusion | flops 37742592 | bytes 49152 | tf_op jit(solution)/shard_map/reduce_sum | solution.py:656
  141.9 26.9 %all-to-all-done.1.u_ref = bf16[32,3,96,128]{3,2,1,0:T(8,128)(2,1)S(1)} async-done(((bf16[32,3,96,128]{3,2,1,0:T(8,128)(2,1)}), bf16[32,3,96,128]{3,2,1,0:T(8,128)(2,1)S(1)}, u32[]{:S(2)}, u32[]{:S(2)}) %all-to-all-start.1) | async-done | bytes 2359328 | tf_op jit(solution)/shard_map/all_to_all | solution.py:69
  171.2 19.3 %attend_forward.1 = (bf16[32,3,32,128]{3,2,1,0:T(8,128)(2,1)S(1)}, f32[3,8,192,128]{3,2,1,0:T(8,128)S(1)}) custom-call(s32[2]{0:T(128)S(1)} %pad_add_fusion.unit_ref, s32[24]{0:T(128)S(1)} %and_select_fusion.first_ref, bf16[32,3,96,128]{3,2,1,0:T(8,128)(2,1)S(1)} %all-to-all-done.1.u_ref, s32[3,8,192,128]{3,2,1,0:T(8,128)} %broadcast_in_dim.61.start_ref), custom_call_target="tpu_custom_call" | custom-call | flops 20000000000 | bytes 1048576 | tf_op jit(solution)/shard_map/attend_forward/pallas_call | solution.py:485
  191.9 23.8 %all_to_all.35 = bf16[32,3,32,128]{3,2,1,0:T(8,128)(2,1)S(1)} all-to-all(bf16[32,3,32,128]{3,2,1,0:T(8,128)(2,1)S(1)} %get-tuple-element.25), channel_id=1, replica_groups=mesh['xl'=2,'c'=2,'z'=4,'y'=4,'xh'=2] {'z','y','xh'}, dimensions={0} | all-to-all | bytes 1572864 | tf_op jit(solution)/shard_map/all_to_all | solution.py:69
  215.7 31.2 %all-gather.2.cloned.1.call-done.w_ref.main_ref.rest_ref.gate_ref.up_ref = bf16[1536,6912]{1,0:T(8,128)(2,1)} async-done(((bf16[96,6912]{1,0:T(8,128)(2,1)}), bf16[1536,6912]{1,0:T(8,128)(2,1)}) %all-gather.2.cloned.1.call-update) | async-done | bytes 21233680 | tf_op jit(solution)/shard_map/all_gather | solution.py:617
  246.9 3.6 out_project.1
  261.6 30.3 %feed_forward.1 = (f32[192,1536]{1,0:T(8,128)S(1)}, bf16[192,1536]{1,0:T(8,128)(2,1)S(1)}, f32[192,1536]{1,0:T(8,128)S(1)}, bf16[192,1536]{1,0:T(8,128)(2,1)S(1)}, bf16[1536,6144]{1,0:T(8,128)(2,1)}) custom-call(bf16[384,1536]{1,0:T(8,128)(2,1)S(1)} %pad_maximum_fusion.4.n_ref, bf16[384,1536]{1,0:T(8,128)(2,1)S(1)} %multiply_convert_fusion.df_ref, ...), custom_call_target="tpu_custom_call" | custom-call | flops 30000001024 | bytes 1048576 | tf_op jit(solution)/shard_map/feed_forward/pallas_call | solution.py:438
  299.5 3.0 multiply_convert_fusion.1
  304.7 4.5 d_out_project.1
  309.1 9.2 %all-to-all-start.3 = ((bf16[32,3,32,128]{3,2,1,0:T(8,128)(2,1)}), bf16[32,3,32,128]{3,2,1,0:T(8,128)(2,1)S(1)}, u32[]{:S(2)}, u32[]{:S(2)}) async-start(bf16[32,3,32,128]{3,2,1,0:T(8,128)(2,1)} %bitcast.20), calls=%async_computation.3 | async-start | bytes 1572864 | tf_op jit(solution)/shard_map/all_to_all | solution.py:69
  323.0 8.4 %all-to-all-done.3.do_ref = bf16[32,3,32,128]{3,2,1,0:T(8,128)(2,1)S(1)} async-done(((bf16[32,3,32,128]{3,2,1,0:T(8,128)(2,1)}), bf16[32,3,32,128]{3,2,1,0:T(8,128)(2,1)S(1)}, u32[]{:S(2)}, u32[]{:S(2)}) %all-to-all-start.3) | async-done | bytes 786464 | tf_op jit(solution)/shard_map/all_to_all | solution.py:69
  331.4 12.0 %all-to-all-start.4 = ((bf16[32,48,768]{2,1,0:T(8,128)(2,1)}), bf16[32,48,768]{2,1,0:T(8,128)(2,1)}, u32[]{:S(2)}, u32[]{:S(2)}) async-start(bf16[32,48,768]{2,1,0:T(8,128)(2,1)} %bitcast.73), calls=%async_computation.4 | async-start | bytes 4718592 | tf_op jit(solution)/shard_map/all_to_all | solution.py:69
  343.4 27.6 %attend_backward.1 = bf16[32,3,96,128]{3,2,1,0:T(8,128)(2,1)S(1)} custom-call(s32[2]{0:T(128)S(1)} %pad_add_fusion.unit_ref, s32[24]{0:T(128)S(1)} %and_select_fusion.first_ref, bf16[32,3,96,128]{3,2,1,0:T(8,128)(2,1)S(1)} %all-to-all-done.1.u_ref, s32[3,8,192,128]{3,2,1,0:T(8,128)} %broadcast_in_dim.61.start_ref, ...), custom_call_target="tpu_custom_call" | custom-call | flops 40000000000 | bytes 1048576 | tf_op jit(solution)/shard_map/attend_backward/pallas_call | solution.py:498
  372.4 7.0 %all-to-all-done.4 = bf16[32,48,768]{2,1,0:T(8,128)(2,1)} async-done(((bf16[32,48,768]{2,1,0:T(8,128)(2,1)}), bf16[32,48,768]{2,1,0:T(8,128)(2,1)}, u32[]{:S(2)}, u32[]{:S(2)}) %all-to-all-start.4) | async-done | bytes 2359328 | tf_op jit(solution)/shard_map/all_to_all | solution.py:69
  382.3 52.6 %all_to_all.36 = bf16[32,3,96,128]{3,2,1,0:T(8,128)(2,1)S(1)} all-to-all(bf16[32,3,96,128]{3,2,1,0:T(8,128)(2,1)S(1)} %copy-done.2), channel_id=1, replica_groups=mesh['xl'=2,'c'=2,'z'=4,'y'=4,'xh'=2] {'z','y','xh'}, dimensions={0} | all-to-all | bytes 4718592 | tf_op jit(solution)/shard_map/all_to_all | solution.py:69
  435.8 3.8 fusion
  439.7 3.3 collective-permute-start.10
  445.9 4.3 gradients.1
  450.2 9.8 %all-to-all-start.6 = ((bf16[32,48,1408]{2,1,0:T(8,128)(2,1)}), bf16[32,48,1408]{2,1,0:T(8,128)(2,1)}, u32[]{:S(2)}, u32[]{:S(2)}) async-start(bf16[32,48,1408]{2,1,0:T(8,128)(2,1)} %bitcast.74), calls=%async_computation.6 | async-start | bytes 8650752 | tf_op jit(solution)/shard_map/all_to_all | solution.py:69
  460.5 49.5 %collective-permute-done.14 = bf16[48,768]{1,0:T(8,128)(2,1)} collective-permute-done((bf16[48,768]{1,0:T(8,128)(2,1)}, bf16[48,768]{1,0:T(8,128)(2,1)}, u32[]{:S(2)}, u32[]{:S(2)}) %collective-permute-start.14) | collective-permute-done | bytes 73760 | tf_op jit(solution)/shard_map/ppermute | solution.py:529
  511.5 11.3 %reduce-scatter.2.cloned.1.call-done = bf16[96,6144]{1,0:T(8,128)(2,1)} async-done(((bf16[1536,6144]{1,0:T(8,128)(2,1)}), bf16[96,6144]{1,0:T(8,128)(2,1)}) %reduce-scatter.2.cloned.1.call-update) | async-done | bytes 1179664 | tf_op jit(solution)/shard_map/reduce_scatter | solution.py:695
  537.0 12.8 %collective-permute-start.20 = (bf16[168,768]{1,0:T(8,128)(2,1)S(1)}, bf16[168,768]{1,0:T(8,128)(2,1)S(1)}, u32[]{:S(2)}, u32[]{:S(2)}) collective-permute-start(bf16[168,768]{1,0:T(8,128)(2,1)S(1)} %pad_maximum_fusion.8), channel_id=1, source_target_pairs={{0,0},{2,1},{4,2},{6,3},{8,4},{10,5},{12,6},{14,7},{16,8},{18,9},{... | collective-permute-start | bytes 774152 | tf_op jit(solution)/shard_map/ppermute | solution.py:724
  550.0 3.7 collective-permute-done.13
  553.9 2.9 reduce_sum.95
  557.5 4.0 collective-permute-done.18
  (254 shorter events, 86.1 us)
Async XLA Ops:
  7.2 239.8 %all-gather.2.cloned.1.call-start = ((), (), s32[]{:S(2)}) async-start(), calls=%async_computation.8 | async-start | bytes 22560768 | tf_op jit(solution)/shard_map/all_gather | solution.py:617
  9.4 11.6 %collective-permute-start.3 = (bf16[48,4096]{1,0:T(8,128)(2,1)S(1)}, bf16[48,4096]{1,0:T(8,128)(2,1)S(1)}, u32[]{:S(2)}, u32[]{:S(2)}) collective-permute-start(bf16[48,4096]{1,0:T(8,128)(2,1)S(1)} %bitcast_dynamic-update-slice_fusion), channel_id=1, source_target_pairs={{0,1},{1,0},{2,3},{3,2},{4,5},{5,4},{6,7},{7,6},{8,9},{9,8},{10,11... | collective-permute-start | bytes 1179656 | tf_op jit(solution)/shard_map/ppermute | solution.py:529
  12.2 14.4 %collective-permute-start.2 = (bf16[168,1536]{1,0:T(8,128)(2,1)S(1)}, bf16[168,1536]{1,0:T(8,128)(2,1)S(1)}, u32[]{:S(2)}, u32[]{:S(2)}) collective-permute-start(bf16[168,1536]{1,0:T(8,128)(2,1)S(1)} %pad_maximum_fusion.5), channel_id=1, source_target_pairs={{0,0},{1,2},{2,4},{3,6},{4,8},{5,10},{6,12},{7,14},{8,16},{9,18},{... | collective-permute-start | bytes 1548296 | tf_op jit(solution)/shard_map/ppermute | solution.py:615
  32.0 77.2 %all-to-all-start = ((bf16[32,48,1408]{2,1,0:T(8,128)(2,1)}), bf16[32,48,1408]{2,1,0:T(8,128)(2,1)}, u32[]{:S(2)}, u32[]{:S(2)}) async-start(bf16[32,48,1408]{2,1,0:T(8,128)(2,1)} %broadcast_in_dim.55), calls=%async_computation | async-start | bytes 8650752 | tf_op jit(solution)/shard_map/all_to_all | solution.py:69
  43.7 2.7 collective-permute-start.1
  45.3 66.1 %copy-start.8 = (f32[4,64,128]{2,1,0:T(8,128)}, f32[4,64,128]{2,1,0:T(8,128)S(1)}, u32[]{:S(2)}) copy-start(f32[4,64,128]{2,1,0:T(8,128)S(1)} %pad_maximum_fusion.9.table_ref) | copy-start | bytes 393220
  46.7 64.7 %copy-start.36 = (f32[384]{0:T(512)}, f32[384]{0:T(512)S(1)}, u32[]{:S(2)}) copy-start(f32[384]{0:T(512)S(1)} %add_rsqrt_fusion) | copy-start | bytes 4612
  118.8 50.1 %all-to-all-start.1 = ((bf16[32,3,96,128]{3,2,1,0:T(8,128)(2,1)}), bf16[32,3,96,128]{3,2,1,0:T(8,128)(2,1)S(1)}, u32[]{:S(2)}, u32[]{:S(2)}) async-start(bf16[32,3,96,128]{3,2,1,0:T(8,128)(2,1)} %bitcast.67), calls=%async_computation.1 | async-start | bytes 4718592 | tf_op jit(solution)/shard_map/all_to_all | solution.py:69
  130.8 392.0 %reduce-scatter.2.cloned.1.call-start = ((), (), s32[]{:S(2)}) async-start(), calls=%async_computation.9 | async-start | bytes 20054016 | tf_op jit(solution)/shard_map/reduce_scatter | solution.py:695
  132.7 2.7 collective-permute-start
  252.4 3.3 collective-permute-start.4
  253.1 6.8 %collective-permute-start.6 = (bf16[192,1536]{1,0:T(8,128)(2,1)}, bf16[192,1536]{1,0:T(8,128)(2,1)}, u32[]{:S(2)}, u32[]{:S(2)}) collective-permute-start(bf16[192,1536]{1,0:T(8,128)(2,1)} %bitcast.18), channel_id=1, source_target_pairs={{0,32},{32,0},{1,33},{33,1},{2,34},{34,2},{3,35},{35,3},{4,36},{36... | collective-permute-start | bytes 1769480 | tf_op jit(solution)/shard_map/ppermute | solution.py:65
  259.5 2.1 collective-permute-start.5
  294.7 2.3 collective-permute-start.8
  295.1 4.4 collective-permute-start.7
  302.6 2.0 collective-permute-start.9
  309.1 22.3 %all-to-all-start.3 = ((bf16[32,3,32,128]{3,2,1,0:T(8,128)(2,1)}), bf16[32,3,32,128]{3,2,1,0:T(8,128)(2,1)S(1)}, u32[]{:S(2)}, u32[]{:S(2)}) async-start(bf16[32,3,32,128]{3,2,1,0:T(8,128)(2,1)} %bitcast.20), calls=%async_computation.3 | async-start | bytes 1572864 | tf_op jit(solution)/shard_map/all_to_all | solution.py:69
  331.4 48.1 %all-to-all-start.4 = ((bf16[32,48,768]{2,1,0:T(8,128)(2,1)}), bf16[32,48,768]{2,1,0:T(8,128)(2,1)}, u32[]{:S(2)}, u32[]{:S(2)}) async-start(bf16[32,48,768]{2,1,0:T(8,128)(2,1)} %bitcast.73), calls=%async_computation.4 | async-start | bytes 4718592 | tf_op jit(solution)/shard_map/all_to_all | solution.py:69
  439.7 4.9 collective-permute-start.10
  450.2 103.7 %all-to-all-start.6 = ((bf16[32,48,1408]{2,1,0:T(8,128)(2,1)}), bf16[32,48,1408]{2,1,0:T(8,128)(2,1)}, u32[]{:S(2)}, u32[]{:S(2)}) async-start(bf16[32,48,1408]{2,1,0:T(8,128)(2,1)} %bitcast.74), calls=%async_computation.6 | async-start | bytes 8650752 | tf_op jit(solution)/shard_map/all_to_all | solution.py:69
  460.1 49.9 %collective-permute-start.14 = (bf16[48,768]{1,0:T(8,128)(2,1)}, bf16[48,768]{1,0:T(8,128)(2,1)}, u32[]{:S(2)}, u32[]{:S(2)}) collective-permute-start(bf16[48,768]{1,0:T(8,128)(2,1)} %reduce_sum.91), channel_id=1, source_target_pairs={{0,64},{64,0},{1,65},{65,1},{2,66},{66,2},{3,67},{67,3},{4,68},{68... | collective-permute-start | bytes 221192 | tf_op jit(solution)/shard_map/ppermute | solution.py:529
  524.0 12.0 %collective-permute-start.16 = (bf16[120,768]{1,0:T(8,128)(2,1)S(1)}, bf16[120,768]{1,0:T(8,128)(2,1)S(1)}, u32[]{:S(2)}, u32[]{:S(2)}) collective-permute-start(bf16[120,768]{1,0:T(8,128)(2,1)S(1)} %get-tuple-element.65), channel_id=1, source_target_pairs={{0,1},{1,0},{2,3},{3,2},{4,5},{5,4},{6,7},{7,6},{8,9},{9,8},{10,11... | collective-permute-start | bytes 552968 | tf_op jit(solution)/shard_map/ppermute | solution.py:529
  525.5 11.4 %collective-permute-start.17 = (bf16[120,768]{1,0:T(8,128)(2,1)S(1)}, bf16[120,768]{1,0:T(8,128)(2,1)S(1)}, u32[]{:S(2)}, u32[]{:S(2)}) collective-permute-start(bf16[120,768]{1,0:T(8,128)(2,1)S(1)} %get-tuple-element.65), channel_id=1, source_target_pairs={{0,65},{1,64},{64,1},{65,0},{2,67},{3,66},{66,3},{67,2},{4,69},{5,... | collective-permute-start | bytes 552968 | tf_op jit(solution)/shard_map/ppermute | solution.py:575
  527.1 6.0 %collective-permute-start.15 = (bf16[120,768]{1,0:T(8,128)(2,1)S(1)}, bf16[120,768]{1,0:T(8,128)(2,1)S(1)}, u32[]{:S(2)}, u32[]{:S(2)}) collective-permute-start(bf16[120,768]{1,0:T(8,128)(2,1)S(1)} %get-tuple-element.64), channel_id=1, source_target_pairs={{0,64},{64,0},{1,65},{65,1},{2,66},{66,2},{3,67},{67,3},{4,68},{68... | collective-permute-start | bytes 552968 | tf_op jit(solution)/shard_map/ppermute | solution.py:529
  527.2 22.8 %collective-permute-start.12 = (bf16[48,4096]{1,0:T(8,128)(2,1)S(1)}, bf16[48,4096]{1,0:T(8,128)(2,1)S(1)}, u32[]{:S(2)}, u32[]{:S(2)}) collective-permute-start(bf16[48,4096]{1,0:T(8,128)(2,1)S(1)} %get-tuple-element.51), channel_id=1, source_target_pairs={{0,1},{1,0},{2,3},{3,2},{4,5},{5,4},{6,7},{7,6},{8,9},{9,8},{10,11... | collective-permute-start | bytes 1179656 | tf_op jit(solution)/shard_map/ppermute | solution.py:529
  529.5 24.2 %collective-permute-start.13 = (bf16[48,4096]{1,0:T(8,128)(2,1)S(1)}, bf16[48,4096]{1,0:T(8,128)(2,1)S(1)}, u32[]{:S(2)}, u32[]{:S(2)}) collective-permute-start(bf16[48,4096]{1,0:T(8,128)(2,1)S(1)} %get-tuple-element.51), channel_id=1, source_target_pairs={{0,65},{1,64},{64,1},{65,0},{2,67},{3,66},{66,3},{67,2},{4,69},{5,... | collective-permute-start | bytes 1179656 | tf_op jit(solution)/shard_map/ppermute | solution.py:575
  533.1 16.9 %collective-permute-start.11 = (bf16[48,4096]{1,0:T(8,128)(2,1)S(1)}, bf16[48,4096]{1,0:T(8,128)(2,1)S(1)}, u32[]{:S(2)}, u32[]{:S(2)}) collective-permute-start(bf16[48,4096]{1,0:T(8,128)(2,1)S(1)} %get-tuple-element.50), channel_id=1, source_target_pairs={{0,64},{64,0},{1,65},{65,1},{2,66},{66,2},{3,67},{67,3},{4,68},{68... | collective-permute-start | bytes 1179656 | tf_op jit(solution)/shard_map/ppermute | solution.py:529
  537.0 27.5 %collective-permute-start.20 = (bf16[168,768]{1,0:T(8,128)(2,1)S(1)}, bf16[168,768]{1,0:T(8,128)(2,1)S(1)}, u32[]{:S(2)}, u32[]{:S(2)}) collective-permute-start(bf16[168,768]{1,0:T(8,128)(2,1)S(1)} %pad_maximum_fusion.8), channel_id=1, source_target_pairs={{0,0},{2,1},{4,2},{6,3},{8,4},{10,5},{12,6},{14,7},{16,8},{18,9},{... | collective-permute-start | bytes 774152 | tf_op jit(solution)/shard_map/ppermute | solution.py:724
  556.8 4.6 collective-permute-start.18
  561.5 3.1 collective-permute-start.19
  563.1 6.6 %collective-permute-start.22 = (bf16[48,3840]{1,0:T(8,128)(2,1)S(1)}, bf16[48,3840]{1,0:T(8,128)(2,1)S(1)}, u32[]{:S(2)}, u32[]{:S(2)}) collective-permute-start(bf16[48,3840]{1,0:T(8,128)(2,1)S(1)} %pad_maximum_fusion.7), channel_id=1, source_target_pairs={{0,32},{32,0},{1,33},{33,1},{2,34},{34,2},{3,35},{35,3},{4,36},{36... | collective-permute-start | bytes 1105928 | tf_op jit(solution)/shard_map/ppermute | solution.py:65
  564.6 3.4 collective-permute-start.21
  (44 other events, 223.4 us)
Sparse Core Ops, SparseCore 0:
  28.3 218.6 all-gather.1
  294.8 228.0 reduce-scatter.1

commit v7 on v3

--- a/solution.py
+++ b/solution.py
@@ -203,6 +203,12 @@
                     put(4 + k, o, m, at, CHUNK, third, 0, p * CHUNK)
 
 
+def gradient_kernel(n_ref, d_ref, gains_ref, out_ref):
+    out_ref[:, :QKV] = product(n_ref[...].T, d_ref[...]).astype(jnp.bfloat16)
+    gains = jnp.concatenate([gains_ref[...], jnp.zeros((120, D), jnp.float32)], axis=0)
+    out_ref[:, QKV:] = gains.T.astype(jnp.bfloat16)
+
+
 def stack_heads(first, third, odd):
     last = jnp.where(odd == 1, third[:, HD:], third[:, :HD])
     return jnp.concatenate([first[:, :HD], first[:, HD:], last], axis=0)
@@ -476,6 +482,16 @@
     )
 
 
+def gradients(n1, d_qkv, gains):
+    return pl.pallas_call(
+        gradient_kernel,
+        out_shape=low_shape(D, QKV + 128),
+        compiler_params=PARAMS,
+        cost_estimate=cost(5),
+        name="gradients",
+    )(n1, d_qkv, gains)
+
+
 def attend_fwd(unit, first, units, starts):
     return pl.pallas_call(
         fwd_kernel,
@@ -562,24 +578,13 @@
     return values + shift(values, axis, 1) + shift(values, axis, 2) + shift(values, axis, 3)
 
 
-def reduce_x(values):
-    size = values.shape[0] // 2
+def reduce_x(values, dim):
+    size = values.shape[dim] // 2
     me = lax.axis_index("xh")
-    keep = lax.dynamic_slice_in_dim(values, me * size, size, axis=0)
-    send = lax.dynamic_slice_in_dim(values, (1 - me) * size, size, axis=0)
+    keep = lax.dynamic_slice_in_dim(values, me * size, size, axis=dim)
+    send = lax.dynamic_slice_in_dim(values, (1 - me) * size, size, axis=dim)
     cross = lax.ppermute(send, ("xl", "xh"), [(i, 3 - i) for i in range(4)])
     return wide_sum(keep, flip(keep, "xl"), flip(send, "xh"), cross)
-
-
-def return_rows(rows, a, b):
-    pairs = []
-    for xl in range(2):
-        for c in range(2):
-            for j in range(16):
-                for xh in range(2):
-                    source = ((xl * 2 + c) * 16 + j) * 2 + xh
-                    pairs.append((source, ((xl ^ b) * 2 + (xh ^ a)) * SHARDS + 16 * c + j))
-    return lax.ppermute(rows, ("xl", "c") + SHARD, pairs)
 
 
 def add_pair(values, axis):
@@ -711,8 +716,6 @@
     unit_d = attend_bwd(unit, first, units, starts, unit_do, lse)
     d_qkv = collect(exchange(unit_d), tables)
 
-    g_qkv = t_product(n1, d_qkv).astype(low)
-    s_qkv = scatter_sum(g_qkv.reshape(SHARDS, 48, HQ + 2 * HK))
     dn1_both = product_t(d_qkv, w_qkv)
     dn1 = dn1_both[:ROWS] + swap(dn1_both[ROWS:].astype(low)).astype(jnp.float32)
     z1 = x * r1
@@ -720,11 +723,9 @@
     g_gain_attn = jnp.sum(dn1 * z1, axis=0)
     grad_in = (dh + r1 * (e1 - z1 * jnp.mean(e1 * z1, axis=-1, keepdims=True))).astype(low)
 
-    gains = jnp.stack([g_gain_attn, g_gain_ffn])
-    gains = gains + swap(gains)
-    gains = total_axis(total_axis(total_axis(gains, "x"), "y"), "z")
-    gains = lax.dynamic_slice_in_dim(gains, shard * 48, 48, axis=1)
-    s_all = after(s_all, gains)
+    gains = jnp.concatenate([g_gain_attn[None], g_gain_ffn[None], jnp.zeros((6, D), jnp.float32)], axis=0)
+    received = exchange(gradients(n1, d_qkv, gains).reshape(SHARDS, 48, QKV + 128))
+    s_all = after(s_all, d_qkv)
     rows = jnp.concatenate(
         [
             unfold(s_all[None, :, OUT_AT:], 2)[0],
@@ -733,8 +734,11 @@
         ],
         axis=0,
     )
-    rows = sum(return_rows(rows, a, b).astype(jnp.float32) for a in range(2) for b in range(2))
-    s_gu = reduce_x(s_all[:, GATE_AT:OUT_AT])
+    rows_x = reduce_x(rows, 1)
+    rows = join_cores(lax.ppermute(rows_x, ("c",) + SHARD, [(b, a) for a, b in piece_perm()]))
+    s_gu = reduce_x(s_all[:, GATE_AT:OUT_AT], 0)
+    received = after(received, (s_gu, rows_x))
+    s_qkv = add_pair(jnp.sum(received.astype(jnp.float32), axis=0).astype(low), "xl")
     s_gu = jnp.concatenate([crop_units(s_gu[:, :PAD_FF]), crop_units(s_gu[:, PAD_FF:])], axis=1)
     other = swap(s_gu)
     lower = core == 0
@@ -742,9 +746,9 @@
         jnp.concatenate([jnp.where(lower, m, t), jnp.where(lower, t, m)], axis=1).astype(jnp.float32)
         for m, t in ((s_gu[:, :HF], other[:, :HF]), (s_gu[:, HF:], other[:, HF:]))
     ]
-    s_qkv = add_pair(s_qkv, "xl")
     other = swap(s_qkv)
     whole = [jnp.where(lower, s_qkv, other), jnp.where(lower, other, s_qkv)]
+    gains = s_qkv[:, QKV : QKV + 2].astype(jnp.float32) + other[:, QKV : QKV + 2].astype(jnp.float32)
 
     def heads_of(offset):
         return jnp.concatenate(
@@ -754,12 +758,12 @@
     return (
         result.reshape(1, MB, SPAN, D).astype(low),
         grad_in.reshape(1, MB, SPAN, D),
-        gains[0],
+        gains[:, 0],
         jnp.concatenate([from_groups(w[:, :HQ]) for w in whole], axis=1).astype(jnp.float32),
         heads_of(0),
         heads_of(HD),
         rows[:48],
-        gains[1],
+        gains[:, 1],
         g_g,
         g_u,
         rows[48:],

time: 640 us -> 583 us (0.911)
  waiting for transfers between devices: 278 us -> 247 us
  starting transfers between devices: 85.7 us -> 67.7 us
    ppermute x13 -> x1, waiting for transfers between devices: 106 us -> 1.81 us  [on_device(): lax.ppermute(rows_x, ('c',) + SHARD, [(b, a) for a, b in piece_perm()])]
    reduce_scatter x1, waiting for transfers between devices: 21.1 us -> 86.5 us  [on_device(): s_all = lax.psum_scatter(g_all, ('z', 'y'), scatter_dimension=0, tiled=True)]
    ppermute x13 -> x1, starting transfers between devices: 27.2 us -> 6.81 us  [on_device(): lax.ppermute(rows_x, ('c',) + SHARD, [(b, a) for a, b in piece_perm()])]
    ppermute x4 -> x7, waiting for transfers between devices: 13.7 us -> 22.8 us  [flip(): return lax.ppermute(values, axis, [(0, 1), (1, 0)])]
  transfers between devices with their start and end apart: 36 -> 27, of which waited for: 25 -> 18; matrix products, arithmetic and copies ran while one was open for 7% -> 6% of each run, Pallas kernels for 9% -> 10%
where the time goes in v7:
time: 583 us; the launch traced here: 572 us
  waiting for transfers between devices  247 us (42%)
  Pallas kernels  97.3 us (17%)
  blocking collectives  93.8 us (16%)
  starting transfers between devices  67.7 us (12%)
  other arithmetic  28 us (5%)
  local copies, waits for them, and re-layouts  19 us (3%)
  between operations  15.3 us (3%)
    all_to_all x3, blocking collectives, exchange(): return lax.all_to_all(values, SHARD, 0, 0, tiled=True)  93.8 us
    all_to_all x3, waiting for transfers between devices, exchange(): return lax.all_to_all(values, SHARD, 0, 0, tiled=True)  89.4 us
    reduce_scatter x1, waiting for transfers between devices, on_device(): s_all = lax.psum_scatter(g_all, ('z', 'y'), scatter_dimension=0, tiled=True)  86.5 us
    all_to_all x3, starting transfers between devices, exchange(): return lax.all_to_all(values, SHARD, 0, 0, tiled=True)  34 us
    all_gather x1, waiting for transfers between devices, on_device(): lax.all_gather(jnp.concatenate([rows_in[48:144], fold(jnp.pad(rows_in[144...  31.9 us
    pallas_call x1, Pallas kernels, feed_forward(): pl.pallas_call(ffn_kernel, grid=(FF_TILES,), in_specs=[whole_spec(BOTH, D...  30.3 us
    pallas_call x1, Pallas kernels, attend_bwd(): pl.pallas_call(bwd_kernel, grid=(MB,), in_specs=[SMEM, SMEM, UNIT_SPEC, C...  27.9 us
    ppermute x7, waiting for transfers between devices, flip(): return lax.ppermute(values, axis, [(0, 1), (1, 0)])  22.8 us
  transfers between devices with their start and end apart: 27, of which 18 were waited for; matrix products, arithmetic and copies ran while one was open for 6% of the time, Pallas kernels for 10%

profile of v7, /device:TPU:49, one launch (start us, length us, event | category | flops | bytes accessed | tf_op | source)
XLA Modules:
  0.0 572.4 jit_solution(9019517569376079067)
XLA Ops:
  9.4 2.8 collective-permute-start.3
  12.2 5.2 collective-permute-start.2
  17.4 3.5 collective-permute-done.3
  21.0 5.7 collective-permute-done.2
  29.6 2.3 broadcast_in_dim.55
  31.9 11.7 %all-to-all-start = ((bf16[32,48,1408]{2,1,0:T(8,128)(2,1)}), bf16[32,48,1408]{2,1,0:T(8,128)(2,1)}, u32[]{:S(2)}, u32[]{:S(2)}) async-start(bf16[32,48,1408]{2,1,0:T(8,128)(2,1)} %broadcast_in_dim.55), calls=%async_computation | async-start | bytes 8650752 | tf_op jit(solution)/shard_map/all_to_all | solution.py:69
  46.7 62.4 %all-to-all-done = bf16[32,48,1408]{2,1,0:T(8,128)(2,1)} async-done(((bf16[32,48,1408]{2,1,0:T(8,128)(2,1)}), bf16[32,48,1408]{2,1,0:T(8,128)(2,1)}, u32[]{:S(2)}, u32[]{:S(2)}) %all-to-all-start) | async-done | bytes 4325408 | tf_op jit(solution)/shard_map/all_to_all | solution.py:69
  111.3 6.0 %project.1 = bf16[4,2,4,3,96,128]{5,4,3,2,1,0:T(8,128)(2,1)S(1)} custom-call(bf16[384,1536]{1,0:T(8,128)(2,1)S(1)} %fusion.4.n_ref, bf16[1536,1408]{1,0:T(8,128)(2,1)} %bitcast.7.w_ref, f32[4,64,128]{2,1,0:T(8,128)S(1)} %pad_maximum_fusion.8.table_ref), custom_call_target="tpu_custom_call" | custom-call | flops 6000000000 | bytes 1048576 | tf_op jit(solution)/shard_map/project/pallas_call | solution.py:324
  118.8 12.0 %all-to-all-start.1 = ((bf16[32,3,96,128]{3,2,1,0:T(8,128)(2,1)}), bf16[32,3,96,128]{3,2,1,0:T(8,128)(2,1)S(1)}, u32[]{:S(2)}, u32[]{:S(2)}) async-start(bf16[32,3,96,128]{3,2,1,0:T(8,128)(2,1)} %bitcast.63), calls=%async_computation.1 | async-start | bytes 4718592 | tf_op jit(solution)/shard_map/all_to_all | solution.py:69
  135.5 5.8 %convert_reduce_fusion = s32[3,2048]{1,0:T(4,128)S(1)} fusion(f32[3,2048]{1,0:T(4,128)S(1)} %select_convert_fusion), kind=kLoop, calls=%fused_computation | loop fusion | flops 37742592 | bytes 49152 | tf_op jit(solution)/shard_map/reduce_sum | solution.py:667
  142.0 26.9 %all-to-all-done.1.u_ref = bf16[32,3,96,128]{3,2,1,0:T(8,128)(2,1)S(1)} async-done(((bf16[32,3,96,128]{3,2,1,0:T(8,128)(2,1)}), bf16[32,3,96,128]{3,2,1,0:T(8,128)(2,1)S(1)}, u32[]{:S(2)}, u32[]{:S(2)}) %all-to-all-start.1) | async-done | bytes 2359328 | tf_op jit(solution)/shard_map/all_to_all | solution.py:69
  171.2 19.6 %attend_forward.1 = (bf16[32,3,32,128]{3,2,1,0:T(8,128)(2,1)S(1)}, f32[3,8,192,128]{3,2,1,0:T(8,128)S(1)}) custom-call(s32[2]{0:T(128)S(1)} %pad_add_fusion.unit_ref, s32[24]{0:T(128)S(1)} %and_select_fusion.first_ref, bf16[32,3,96,128]{3,2,1,0:T(8,128)(2,1)S(1)} %all-to-all-done.1.u_ref, s32[3,8,192,128]{3,2,1,0:T(8,128)} %broadcast_in_dim.61.start_ref), custom_call_target="tpu_custom_call" | custom-call | flops 20000000000 | bytes 1048576 | tf_op jit(solution)/shard_map/attend_forward/pallas_call | solution.py:496
  192.2 22.9 %all_to_all.30 = bf16[32,3,32,128]{3,2,1,0:T(8,128)(2,1)S(1)} all-to-all(bf16[32,3,32,128]{3,2,1,0:T(8,128)(2,1)S(1)} %get-tuple-element.25), channel_id=1, replica_groups=mesh['xl'=2,'c'=2,'z'=4,'y'=4,'xh'=2] {'z','y','xh'}, dimensions={0} | all-to-all | bytes 1572864 | tf_op jit(solution)/shard_map/all_to_all | solution.py:69
  215.0 31.9 %all-gather.2.cloned.1.call-done.w_ref.main_ref.rest_ref.gate_ref.up_ref = bf16[1536,6912]{1,0:T(8,128)(2,1)} async-done(((bf16[96,6912]{1,0:T(8,128)(2,1)}), bf16[1536,6912]{1,0:T(8,128)(2,1)}) %all-gather.2.cloned.1.call-update) | async-done | bytes 21233680 | tf_op jit(solution)/shard_map/all_gather | solution.py:628
  246.9 3.6 out_project.1
  259.6 30.3 %feed_forward.1 = (f32[192,1536]{1,0:T(8,128)S(1)}, bf16[192,1536]{1,0:T(8,128)(2,1)S(1)}, f32[192,1536]{1,0:T(8,128)S(1)}, bf16[192,1536]{1,0:T(8,128)(2,1)S(1)}, bf16[1536,6912]{1,0:T(8,128)(2,1)}) custom-call(bf16[384,1536]{1,0:T(8,128)(2,1)S(1)} %pad_maximum_fusion.2.n_ref, bf16[384,1536]{1,0:T(8,128)(2,1)S(1)} %multiply_convert_fusion.df_ref, ...), custom_call_target="tpu_custom_call" | custom-call | flops 30000001024 | bytes 1048576 | tf_op jit(solution)/shard_map/feed_forward/pallas_call | solution.py:449
  292.8 3.0 multiply_convert_fusion.1
  297.9 4.9 d_out_project.1
  302.8 22.1 %all_to_all.31.do_ref = bf16[32,3,32,128]{3,2,1,0:T(8,128)(2,1)S(1)} all-to-all(bf16[32,3,32,128]{3,2,1,0:T(8,128)(2,1)S(1)} %bitcast.65), channel_id=1, replica_groups=mesh['xl'=2,'c'=2,'z'=4,'y'=4,'xh'=2] {'z','y','xh'}, dimensions={0} | all-to-all | bytes 1572864 | tf_op jit(solution)/shard_map/all_to_all | solution.py:69
  324.9 27.9 %attend_backward.1 = bf16[32,3,96,128]{3,2,1,0:T(8,128)(2,1)S(1)} custom-call(s32[2]{0:T(128)S(1)} %pad_add_fusion.unit_ref, s32[24]{0:T(128)S(1)} %and_select_fusion.first_ref, bf16[32,3,96,128]{3,2,1,0:T(8,128)(2,1)S(1)} %all-to-all-done.1.u_ref, s32[3,8,192,128]{3,2,1,0:T(8,128)} %broadcast_in_dim.61.start_ref, ...), custom_call_target="tpu_custom_call" | custom-call | flops 27000000512 | bytes 1048576 | tf_op jit(solution)/shard_map/attend_backward/pallas_call | solution.py:509
  352.7 48.8 %all_to_all.32 = bf16[32,3,96,128]{3,2,1,0:T(8,128)(2,1)S(1)} all-to-all(bf16[32,3,96,128]{3,2,1,0:T(8,128)(2,1)S(1)} %attend_backward.1), channel_id=1, replica_groups=mesh['xl'=2,'c'=2,'z'=4,'y'=4,'xh'=2] {'z','y','xh'}, dimensions={0} | all-to-all | bytes 4718592 | tf_op jit(solution)/shard_map/all_to_all | solution.py:69
  402.4 3.8 fusion
  406.3 3.8 collective-permute-start.10
  412.4 4.3 gradients.1
  416.7 10.2 %all-to-all-start.5 = ((bf16[32,48,1408]{2,1,0:T(8,128)(2,1)}), bf16[32,48,1408]{2,1,0:T(8,128)(2,1)}, u32[]{:S(2)}, u32[]{:S(2)}) async-start(bf16[32,48,1408]{2,1,0:T(8,128)(2,1)} %bitcast.70), calls=%async_computation.5 | async-start | bytes 8650752 | tf_op jit(solution)/shard_map/all_to_all | solution.py:69
  426.9 86.5 %reduce-scatter.2.cloned.1.call-done = bf16[96,6912]{1,0:T(8,128)(2,1)} async-done(((bf16[1536,6912]{1,0:T(8,128)(2,1)}), bf16[96,6912]{1,0:T(8,128)(2,1)}) %reduce-scatter.2.cloned.1.call-update) | async-done | bytes 1327120 | tf_op jit(solution)/shard_map/reduce_scatter | solution.py:714
  520.8 8.5 %collective-permute-done.14 = bf16[168,768]{1,0:T(8,128)(2,1)S(1)} collective-permute-done((bf16[168,768]{1,0:T(8,128)(2,1)S(1)}, bf16[168,768]{1,0:T(8,128)(2,1)S(1)}, u32[]{:S(2)}, u32[]{:S(2)}) %collective-permute-start.14) | collective-permute-done | bytes 258080 | tf_op jit(solution)/shard_map/ppermute | solution.py:540
  531.3 6.8 %collective-permute-start.19 = (bf16[168,768]{1,0:T(8,128)(2,1)S(1)}, bf16[168,768]{1,0:T(8,128)(2,1)S(1)}, u32[]{:S(2)}, u32[]{:S(2)}) collective-permute-start(bf16[168,768]{1,0:T(8,128)(2,1)S(1)} %add_convert_fusion.2), channel_id=1, source_target_pairs={{0,0},{2,1},{4,2},{6,3},{8,4},{10,5},{12,6},{14,7},{16,8},{18,9},{... | collective-permute-start | bytes 774152 | tf_op jit(solution)/shard_map/ppermute | solution.py:738
  538.1 8.1 %collective-permute-done.11 = bf16[48,4096]{1,0:T(8,128)(2,1)S(1)} collective-permute-done((bf16[48,4096]{1,0:T(8,128)(2,1)S(1)}, bf16[48,4096]{1,0:T(8,128)(2,1)S(1)}, u32[]{:S(2)}, u32[]{:S(2)}) %collective-permute-start.11) | collective-permute-done | bytes 393248 | tf_op jit(solution)/shard_map/ppermute | solution.py:540
  546.4 2.9 reduce_sum.82
  550.6 2.7 collective-permute-done.17
  553.3 2.8 collective-permute-start.18
  (205 shorter events, 57.3 us)
Async XLA Ops:
  7.2 239.7 %all-gather.2.cloned.1.call-start = ((), (), s32[]{:S(2)}) async-start(), calls=%async_computation.7 | async-start | bytes 22560768 | tf_op jit(solution)/shard_map/all_gather | solution.py:628
  9.4 11.6 %collective-permute-start.3 = (bf16[48,4096]{1,0:T(8,128)(2,1)S(1)}, bf16[48,4096]{1,0:T(8,128)(2,1)S(1)}, u32[]{:S(2)}, u32[]{:S(2)}) collective-permute-start(bf16[48,4096]{1,0:T(8,128)(2,1)S(1)} %bitcast_dynamic-update-slice_fusion), channel_id=1, source_target_pairs={{0,1},{1,0},{2,3},{3,2},{4,5},{5,4},{6,7},{7,6},{8,9},{9,8},{10,11... | collective-permute-start | bytes 1179656 | tf_op jit(solution)/shard_map/ppermute | solution.py:540
  12.2 14.4 %collective-permute-start.2 = (bf16[168,1536]{1,0:T(8,128)(2,1)S(1)}, bf16[168,1536]{1,0:T(8,128)(2,1)S(1)}, u32[]{:S(2)}, u32[]{:S(2)}) collective-permute-start(bf16[168,1536]{1,0:T(8,128)(2,1)S(1)} %pad_maximum_fusion.4), channel_id=1, source_target_pairs={{0,0},{1,2},{2,4},{3,6},{4,8},{5,10},{6,12},{7,14},{8,16},{9,18},{... | collective-permute-start | bytes 1548296 | tf_op jit(solution)/shard_map/ppermute | solution.py:626
  31.9 11.7 %copy-start.7 = (bf16[1,3,64,1536]{3,2,1,0:T(8,128)(2,1)S(1)}, bf16[1,3,64,1536]{3,2,1,0:T(8,128)(2,1)}, u32[]{:S(2)}) copy-start(bf16[1,3,64,1536]{3,2,1,0:T(8,128)(2,1)} %param.12) | copy-start | bytes 1769476
  31.9 77.2 %all-to-all-start = ((bf16[32,48,1408]{2,1,0:T(8,128)(2,1)}), bf16[32,48,1408]{2,1,0:T(8,128)(2,1)}, u32[]{:S(2)}, u32[]{:S(2)}) async-start(bf16[32,48,1408]{2,1,0:T(8,128)(2,1)} %broadcast_in_dim.55), calls=%async_computation | async-start | bytes 8650752 | tf_op jit(solution)/shard_map/all_to_all | solution.py:69
  43.7 2.7 collective-permute-start.1
  46.7 64.6 %copy-start.15 = (f32[384]{0:T(512)}, f32[384]{0:T(512)S(1)}, u32[]{:S(2)}) copy-start(f32[384]{0:T(512)S(1)} %add_rsqrt_fusion) | copy-start | bytes 4612
  111.3 6.0 %copy-start.2 = (bf16[384,1536]{1,0:T(8,128)(2,1)}, bf16[384,1536]{1,0:T(8,128)(2,1)S(1)}, u32[]{:S(2)}) copy-start(bf16[384,1536]{1,0:T(8,128)(2,1)S(1)} %fusion.4.n_ref) | copy-start | bytes 3538948
  118.8 50.1 %all-to-all-start.1 = ((bf16[32,3,96,128]{3,2,1,0:T(8,128)(2,1)}), bf16[32,3,96,128]{3,2,1,0:T(8,128)(2,1)S(1)}, u32[]{:S(2)}, u32[]{:S(2)}) async-start(bf16[32,3,96,128]{3,2,1,0:T(8,128)(2,1)} %bitcast.63), calls=%async_computation.1 | async-start | bytes 4718592 | tf_op jit(solution)/shard_map/all_to_all | solution.py:69
  130.8 382.7 %reduce-scatter.2.cloned.1.call-start = ((), (), s32[]{:S(2)}) async-start(), calls=%async_computation.8 | async-start | bytes 22560768 | tf_op jit(solution)/shard_map/reduce_scatter | solution.py:714
  132.7 2.7 collective-permute-start
  252.4 3.0 collective-permute-start.4
  253.1 4.8 collective-permute-start.6
  257.4 2.1 collective-permute-start.5
  289.9 2.1 collective-permute-start.8
  290.3 2.5 collective-permute-start.7
  295.8 2.0 collective-permute-start.9
  406.3 5.4 collective-permute-start.10
  416.7 129.8 %all-to-all-start.5 = ((bf16[32,48,1408]{2,1,0:T(8,128)(2,1)}), bf16[32,48,1408]{2,1,0:T(8,128)(2,1)}, u32[]{:S(2)}, u32[]{:S(2)}) async-start(bf16[32,48,1408]{2,1,0:T(8,128)(2,1)} %bitcast.70), calls=%async_computation.5 | async-start | bytes 8650752 | tf_op jit(solution)/shard_map/all_to_all | solution.py:69
  514.7 15.2 %copy-start.9 = (f32[192,1536]{1,0:T(8,128)S(1)}, f32[192,1536]{1,0:T(8,128)}, u32[]{:S(2)}) copy-start(f32[192,1536]{1,0:T(8,128)} %get-tuple-element.48) | copy-start | bytes 3538948
  514.8 15.1 %copy-start.18 = (f32[192]{0:T(256)S(1)}, f32[192]{0:T(256)}, u32[]{:S(2)}) copy-start(f32[192]{0:T(256)} %copy-done.17) | copy-start | bytes 2308
  514.8 16.3 %collective-permute-start.16 = (bf16[168,768]{1,0:T(8,128)(2,1)S(1)}, bf16[168,768]{1,0:T(8,128)(2,1)S(1)}, u32[]{:S(2)}, u32[]{:S(2)}) collective-permute-start(bf16[168,768]{1,0:T(8,128)(2,1)S(1)} %get-tuple-element.61), channel_id=1, source_target_pairs={{0,65},{1,64},{64,1},{65,0},{2,67},{3,66},{66,3},{67,2},{4,69},{5,... | collective-permute-start | bytes 774152 | tf_op jit(solution)/shard_map/ppermute | solution.py:586
  516.9 14.3 %collective-permute-start.15 = (bf16[168,768]{1,0:T(8,128)(2,1)S(1)}, bf16[168,768]{1,0:T(8,128)(2,1)S(1)}, u32[]{:S(2)}, u32[]{:S(2)}) collective-permute-start(bf16[168,768]{1,0:T(8,128)(2,1)S(1)} %get-tuple-element.61), channel_id=1, source_target_pairs={{0,1},{1,0},{2,3},{3,2},{4,5},{5,4},{6,7},{7,6},{8,9},{9,8},{10,11... | collective-permute-start | bytes 774152 | tf_op jit(solution)/shard_map/ppermute | solution.py:540
  517.5 11.9 %collective-permute-start.14 = (bf16[168,768]{1,0:T(8,128)(2,1)S(1)}, bf16[168,768]{1,0:T(8,128)(2,1)S(1)}, u32[]{:S(2)}, u32[]{:S(2)}) collective-permute-start(bf16[168,768]{1,0:T(8,128)(2,1)S(1)} %get-tuple-element.60), channel_id=1, source_target_pairs={{0,64},{64,0},{1,65},{65,1},{2,66},{66,2},{3,67},{67,3},{4,68},{68... | collective-permute-start | bytes 774152 | tf_op jit(solution)/shard_map/ppermute | solution.py:540
  518.2 28.0 %collective-permute-start.13 = (bf16[48,4096]{1,0:T(8,128)(2,1)S(1)}, bf16[48,4096]{1,0:T(8,128)(2,1)S(1)}, u32[]{:S(2)}, u32[]{:S(2)}) collective-permute-start(bf16[48,4096]{1,0:T(8,128)(2,1)S(1)} %get-tuple-element.51), channel_id=1, source_target_pairs={{0,65},{1,64},{64,1},{65,0},{2,67},{3,66},{66,3},{67,2},{4,69},{5,... | collective-permute-start | bytes 1179656 | tf_op jit(solution)/shard_map/ppermute | solution.py:586
  520.3 26.0 %collective-permute-start.12 = (bf16[48,4096]{1,0:T(8,128)(2,1)S(1)}, bf16[48,4096]{1,0:T(8,128)(2,1)S(1)}, u32[]{:S(2)}, u32[]{:S(2)}) collective-permute-start(bf16[48,4096]{1,0:T(8,128)(2,1)S(1)} %get-tuple-element.51), channel_id=1, source_target_pairs={{0,1},{1,0},{2,3},{3,2},{4,5},{5,4},{6,7},{7,6},{8,9},{9,8},{10,11... | collective-permute-start | bytes 1179656 | tf_op jit(solution)/shard_map/ppermute | solution.py:540
  529.3 16.9 %collective-permute-start.11 = (bf16[48,4096]{1,0:T(8,128)(2,1)S(1)}, bf16[48,4096]{1,0:T(8,128)(2,1)S(1)}, u32[]{:S(2)}, u32[]{:S(2)}) collective-permute-start(bf16[48,4096]{1,0:T(8,128)(2,1)S(1)} %get-tuple-element.50), channel_id=1, source_target_pairs={{0,64},{64,0},{1,65},{65,1},{2,66},{66,2},{3,67},{67,3},{4,68},{68... | collective-permute-start | bytes 1179656 | tf_op jit(solution)/shard_map/ppermute | solution.py:540
  531.3 26.8 %collective-permute-start.19 = (bf16[168,768]{1,0:T(8,128)(2,1)S(1)}, bf16[168,768]{1,0:T(8,128)(2,1)S(1)}, u32[]{:S(2)}, u32[]{:S(2)}) collective-permute-start(bf16[168,768]{1,0:T(8,128)(2,1)S(1)} %add_convert_fusion.2), channel_id=1, source_target_pairs={{0,0},{2,1},{4,2},{6,3},{8,4},{10,5},{12,6},{14,7},{16,8},{18,9},{... | collective-permute-start | bytes 774152 | tf_op jit(solution)/shard_map/ppermute | solution.py:738
  549.4 3.9 collective-permute-start.17
  553.3 4.8 collective-permute-start.18
  556.2 5.3 collective-permute-start.21
  558.1 5.3 collective-permute-start.20
  (21 other events, 40.9 us)
Sparse Core Ops, SparseCore 0:
  28.2 218.6 all-gather.1
  302.9 210.5 reduce-scatter.1

commit v8 on v7

--- a/solution.py
+++ b/solution.py
@@ -724,8 +724,9 @@
     grad_in = (dh + r1 * (e1 - z1 * jnp.mean(e1 * z1, axis=-1, keepdims=True))).astype(low)
 
     gains = jnp.concatenate([g_gain_attn[None], g_gain_ffn[None], jnp.zeros((6, D), jnp.float32)], axis=0)
-    received = exchange(gradients(n1, d_qkv, gains).reshape(SHARDS, 48, QKV + 128))
-    s_all = after(s_all, d_qkv)
+    s_qkv = add_pair(scatter_sum(gradients(n1, d_qkv, gains).reshape(SHARDS, 48, QKV + 128)), "xl")
+    other_qkv = swap(s_qkv)
+    s_all = after(s_all, other_qkv)
     rows = jnp.concatenate(
         [
             unfold(s_all[None, :, OUT_AT:], 2)[0],
@@ -737,18 +738,16 @@
     rows_x = reduce_x(rows, 1)
     rows = join_cores(lax.ppermute(rows_x, ("c",) + SHARD, [(b, a) for a, b in piece_perm()]))
     s_gu = reduce_x(s_all[:, GATE_AT:OUT_AT], 0)
-    received = after(received, (s_gu, rows_x))
-    s_qkv = add_pair(jnp.sum(received.astype(jnp.float32), axis=0).astype(low), "xl")
-    s_gu = jnp.concatenate([crop_units(s_gu[:, :PAD_FF]), crop_units(s_gu[:, PAD_FF:])], axis=1)
     other = swap(s_gu)
     lower = core == 0
+    s_gu, other = [
+        [crop_units(v[:, :PAD_FF]), crop_units(v[:, PAD_FF:])] for v in (s_gu.astype(jnp.float32), other.astype(jnp.float32))
+    ]
     g_g, g_u = [
-        jnp.concatenate([jnp.where(lower, m, t), jnp.where(lower, t, m)], axis=1).astype(jnp.float32)
-        for m, t in ((s_gu[:, :HF], other[:, :HF]), (s_gu[:, HF:], other[:, HF:]))
+        jnp.concatenate([jnp.where(lower, m, t), jnp.where(lower, t, m)], axis=1) for m, t in zip(s_gu, other)
     ]
-    other = swap(s_qkv)
-    whole = [jnp.where(lower, s_qkv, other), jnp.where(lower, other, s_qkv)]
-    gains = s_qkv[:, QKV : QKV + 2].astype(jnp.float32) + other[:, QKV : QKV + 2].astype(jnp.float32)
+    whole = [jnp.where(lower, s_qkv, other_qkv), jnp.where(lower, other_qkv, s_qkv)]
+    gains = s_qkv[:, QKV : QKV + 2].astype(jnp.float32) + other_qkv[:, QKV : QKV + 2].astype(jnp.float32)
 
     def heads_of(offset):
         return jnp.concatenate(

time: 583 us -> 579 us (level)
    reduce_scatter x1, waiting for transfers between devices: 86.5 us -> 13 us  [on_device(): s_all = lax.psum_scatter(g_all, ('z', 'y'), scatter_dimension=0, tiled=True)]
    all_to_all x3, waiting for transfers between devices: 89.4 us -> 150 us  [exchange(): return lax.all_to_all(values, SHARD, 0, 0, tiled=True)]
    ppermute x1, waiting for transfers between devices: 1.81 us -> 19.6 us  [on_device(): lax.ppermute(rows_x, ('c',) + SHARD, [(b, a) for a, b in piece_perm()])]
    ppermute x7, waiting for transfers between devices: 22.8 us -> 16.2 us  [flip(): return lax.ppermute(values, axis, [(0, 1), (1, 0)])]
  transfers between devices with their start and end apart: 27 -> 27, of which waited for: 18 -> 19; matrix products, arithmetic and copies ran while one was open for 6% -> 6% of each run, Pallas kernels for 10% -> 10%
where the time goes in v8:
time: 579 us; the launch traced here: 572 us
  waiting for transfers between devices  246 us (42%)
  Pallas kernels  95.9 us (17%)
  blocking collectives  94.8 us (16%)
  starting transfers between devices  67.1 us (12%)
  other arithmetic  29.5 us (5%)
  local copies, waits for them, and re-layouts  19.7 us (3%)
  between operations  15.3 us (3%)
    all_to_all x3, waiting for transfers between devices, exchange(): return lax.all_to_all(values, SHARD, 0, 0, tiled=True)  150 us
    all_to_all x3, blocking collectives, exchange(): return lax.all_to_all(values, SHARD, 0, 0, tiled=True)  94.8 us
    all_to_all x3, starting transfers between devices, exchange(): return lax.all_to_all(values, SHARD, 0, 0, tiled=True)  33.3 us
    all_gather x1, waiting for transfers between devices, on_device(): lax.all_gather(jnp.concatenate([rows_in[48:144], fold(jnp.pad(rows_in[144...  31.6 us
    pallas_call x1, Pallas kernels, feed_forward(): pl.pallas_call(ffn_kernel, grid=(FF_TILES,), in_specs=[whole_spec(BOTH, D...  30.3 us
    pallas_call x1, Pallas kernels, attend_bwd(): pl.pallas_call(bwd_kernel, grid=(MB,), in_specs=[SMEM, SMEM, UNIT_SPEC, C...  27 us
    ppermute x1, waiting for transfers between devices, on_device(): lax.ppermute(rows_x, ('c',) + SHARD, [(b, a) for a, b in piece_perm()])  19.6 us
    pallas_call x1, Pallas kernels, attend_fwd(): pl.pallas_call(fwd_kernel, grid=(MB,), in_specs=[SMEM, SMEM, UNIT_SPEC, C...  19 us
  transfers between devices with their start and end apart: 27, of which 19 were waited for; matrix products, arithmetic and copies ran while one was open for 6% of the time, Pallas kernels for 10%

profile of v8, /device:TPU:49, one launch (start us, length us, event | category | flops | bytes accessed | tf_op | source)
XLA Modules:
  0.0 571.8 jit_solution(11619263076534810777)
XLA Ops:
  9.4 2.8 collective-permute-start.3
  12.2 5.2 collective-permute-start.2
  17.4 3.5 collective-permute-done.3
  21.0 5.7 collective-permute-done.2
  31.9 11.7 %all-to-all-start = ((bf16[32,48,1408]{2,1,0:T(8,128)(2,1)}), bf16[32,48,1408]{2,1,0:T(8,128)(2,1)}, u32[]{:S(2)}, u32[]{:S(2)}) async-start(bf16[32,48,1408]{2,1,0:T(8,128)(2,1)} %broadcast_in_dim.55), calls=%async_computation | async-start | bytes 8650752 | tf_op jit(solution)/shard_map/all_to_all | solution.py:69
  46.7 62.5 %all-to-all-done = bf16[32,48,1408]{2,1,0:T(8,128)(2,1)} async-done(((bf16[32,48,1408]{2,1,0:T(8,128)(2,1)}), bf16[32,48,1408]{2,1,0:T(8,128)(2,1)}, u32[]{:S(2)}, u32[]{:S(2)}) %all-to-all-start) | async-done | bytes 4325408 | tf_op jit(solution)/shard_map/all_to_all | solution.py:69
  111.3 6.0 %project.1 = bf16[4,2,4,3,96,128]{5,4,3,2,1,0:T(8,128)(2,1)S(1)} custom-call(bf16[384,1536]{1,0:T(8,128)(2,1)S(1)} %fusion.4.n_ref, bf16[1536,1408]{1,0:T(8,128)(2,1)} %bitcast.7.w_ref, f32[4,64,128]{2,1,0:T(8,128)S(1)} %pad_maximum_fusion.9.table_ref), custom_call_target="tpu_custom_call" | custom-call | flops 6000000000 | bytes 1048576 | tf_op jit(solution)/shard_map/project/pallas_call | solution.py:324
  118.8 12.0 %all-to-all-start.1 = ((bf16[32,3,96,128]{3,2,1,0:T(8,128)(2,1)}), bf16[32,3,96,128]{3,2,1,0:T(8,128)(2,1)S(1)}, u32[]{:S(2)}, u32[]{:S(2)}) async-start(bf16[32,3,96,128]{3,2,1,0:T(8,128)(2,1)} %bitcast.67), calls=%async_computation.1 | async-start | bytes 4718592 | tf_op jit(solution)/shard_map/all_to_all | solution.py:69
  135.4 5.8 %convert_reduce_fusion = s32[3,2048]{1,0:T(4,128)S(1)} fusion(f32[3,2048]{1,0:T(4,128)S(1)} %select_convert_fusion), kind=kLoop, calls=%fused_computation | loop fusion | flops 37742592 | bytes 49152 | tf_op jit(solution)/shard_map/reduce_sum | solution.py:667
  142.0 26.9 %all-to-all-done.1.u_ref = bf16[32,3,96,128]{3,2,1,0:T(8,128)(2,1)S(1)} async-done(((bf16[32,3,96,128]{3,2,1,0:T(8,128)(2,1)}), bf16[32,3,96,128]{3,2,1,0:T(8,128)(2,1)S(1)}, u32[]{:S(2)}, u32[]{:S(2)}) %all-to-all-start.1) | async-done | bytes 2359328 | tf_op jit(solution)/shard_map/all_to_all | solution.py:69
  171.2 19.0 %attend_forward.1 = (bf16[32,3,32,128]{3,2,1,0:T(8,128)(2,1)S(1)}, f32[3,8,192,128]{3,2,1,0:T(8,128)S(1)}) custom-call(s32[2]{0:T(128)S(1)} %pad_add_fusion.unit_ref, s32[24]{0:T(128)S(1)} %and_select_fusion.first_ref, bf16[32,3,96,128]{3,2,1,0:T(8,128)(2,1)S(1)} %all-to-all-done.1.u_ref, s32[3,8,192,128]{3,2,1,0:T(8,128)} %broadcast_in_dim.61.start_ref), custom_call_target="tpu_custom_call" | custom-call | flops 20000000000 | bytes 1048576 | tf_op jit(solution)/shard_map/attend_forward/pallas_call | solution.py:496
  191.6 23.7 %all_to_all.30 = bf16[32,3,32,128]{3,2,1,0:T(8,128)(2,1)S(1)} all-to-all(bf16[32,3,32,128]{3,2,1,0:T(8,128)(2,1)S(1)} %get-tuple-element.24), channel_id=1, replica_groups=mesh['xl'=2,'c'=2,'z'=4,'y'=4,'xh'=2] {'z','y','xh'}, dimensions={0} | all-to-all | bytes 1572864 | tf_op jit(solution)/shard_map/all_to_all | solution.py:69
  215.3 31.6 %all-gather.2.cloned.1.call-done.w_ref.main_ref.rest_ref.gate_ref.up_ref = bf16[1536,6912]{1,0:T(8,128)(2,1)} async-done(((bf16[96,6912]{1,0:T(8,128)(2,1)}), bf16[1536,6912]{1,0:T(8,128)(2,1)}) %all-gather.2.cloned.1.call-update) | async-done | bytes 21233680 | tf_op jit(solution)/shard_map/all_gather | solution.py:628
  246.9 3.6 out_project.1
  259.6 30.3 %feed_forward.1 = (f32[192,1536]{1,0:T(8,128)S(1)}, bf16[192,1536]{1,0:T(8,128)(2,1)S(1)}, f32[192,1536]{1,0:T(8,128)S(1)}, bf16[192,1536]{1,0:T(8,128)(2,1)S(1)}, bf16[1536,6912]{1,0:T(8,128)(2,1)}) custom-call(bf16[384,1536]{1,0:T(8,128)(2,1)S(1)} %pad_maximum_fusion.2.n_ref, bf16[384,1536]{1,0:T(8,128)(2,1)S(1)} %multiply_convert_fusion.df_ref, ...), custom_call_target="tpu_custom_call" | custom-call | flops 30000001024 | bytes 1048576 | tf_op jit(solution)/shard_map/feed_forward/pallas_call | solution.py:449
  292.8 3.0 multiply_convert_fusion.1
  297.9 4.9 d_out_project.1
  302.8 22.1 %all_to_all.31.do_ref = bf16[32,3,32,128]{3,2,1,0:T(8,128)(2,1)S(1)} all-to-all(bf16[32,3,32,128]{3,2,1,0:T(8,128)(2,1)S(1)} %bitcast.69), channel_id=1, replica_groups=mesh['xl'=2,'c'=2,'z'=4,'y'=4,'xh'=2] {'z','y','xh'}, dimensions={0} | all-to-all | bytes 1572864 | tf_op jit(solution)/shard_map/all_to_all | solution.py:69
  324.9 27.0 %attend_backward.1 = bf16[32,3,96,128]{3,2,1,0:T(8,128)(2,1)S(1)} custom-call(s32[2]{0:T(128)S(1)} %pad_add_fusion.unit_ref, s32[24]{0:T(128)S(1)} %and_select_fusion.first_ref, bf16[32,3,96,128]{3,2,1,0:T(8,128)(2,1)S(1)} %all-to-all-done.1.u_ref, s32[3,8,192,128]{3,2,1,0:T(8,128)} %broadcast_in_dim.61.start_ref, ...), custom_call_target="tpu_custom_call" | custom-call | flops 27000000512 | bytes 1048576 | tf_op jit(solution)/shard_map/attend_backward/pallas_call | solution.py:509
  351.9 49.1 %all_to_all.32 = bf16[32,3,96,128]{3,2,1,0:T(8,128)(2,1)S(1)} all-to-all(bf16[32,3,96,128]{3,2,1,0:T(8,128)(2,1)S(1)} %attend_backward.1), channel_id=1, replica_groups=mesh['xl'=2,'c'=2,'z'=4,'y'=4,'xh'=2] {'z','y','xh'}, dimensions={0} | all-to-all | bytes 4718592 | tf_op jit(solution)/shard_map/all_to_all | solution.py:69
  401.8 3.9 fusion
  405.8 3.6 collective-permute-start.10
  411.8 4.3 gradients.1
  416.1 9.5 %all-to-all-start.5 = ((bf16[32,48,1408]{2,1,0:T(8,128)(2,1)}), bf16[32,48,1408]{2,1,0:T(8,128)(2,1)}, u32[]{:S(2)}, u32[]{:S(2)}) async-start(bf16[32,48,1408]{2,1,0:T(8,128)(2,1)} %bitcast.74), calls=%async_computation.5 | async-start | bytes 8650752 | tf_op jit(solution)/shard_map/all_to_all | solution.py:69
  425.6 60.8 %all-to-all-done.5 = bf16[32,48,1408]{2,1,0:T(8,128)(2,1)} async-done(((bf16[32,48,1408]{2,1,0:T(8,128)(2,1)}), bf16[32,48,1408]{2,1,0:T(8,128)(2,1)}, u32[]{:S(2)}, u32[]{:S(2)}) %all-to-all-start.5) | async-done | bytes 4325408 | tf_op jit(solution)/shard_map/all_to_all | solution.py:69
  486.5 3.0 reduce_sum.82
  489.6 4.2 collective-permute-done.11
  496.0 2.5 fusion.12
  501.2 13.0 %reduce-scatter.2.cloned.1.call-done = bf16[96,6912]{1,0:T(8,128)(2,1)} async-done(((bf16[1536,6912]{1,0:T(8,128)(2,1)}), bf16[96,6912]{1,0:T(8,128)(2,1)}) %reduce-scatter.2.cloned.1.call-update) | async-done | bytes 1327120 | tf_op jit(solution)/shard_map/reduce_scatter | solution.py:714
  521.9 7.9 %collective-permute-done.13 = bf16[168,768]{1,0:T(8,128)(2,1)S(1)} collective-permute-done((bf16[168,768]{1,0:T(8,128)(2,1)S(1)}, bf16[168,768]{1,0:T(8,128)(2,1)S(1)}, u32[]{:S(2)}, u32[]{:S(2)}) %collective-permute-start.13) | collective-permute-done | bytes 258080 | tf_op jit(solution)/shard_map/ppermute | solution.py:540
  531.1 6.8 %collective-permute-start.16 = (bf16[168,768]{1,0:T(8,128)(2,1)S(1)}, bf16[168,768]{1,0:T(8,128)(2,1)S(1)}, u32[]{:S(2)}, u32[]{:S(2)}) collective-permute-start(bf16[168,768]{1,0:T(8,128)(2,1)S(1)} %add_convert_fusion.2), channel_id=1, source_target_pairs={{0,0},{2,1},{4,2},{6,3},{8,4},{10,5},{12,6},{14,7},{16,8},{18,9},{... | collective-permute-start | bytes 774152 | tf_op jit(solution)/shard_map/ppermute | solution.py:739
  538.6 19.6 %collective-permute-done.16 = bf16[168,768]{1,0:T(8,128)(2,1)S(1)} collective-permute-done((bf16[168,768]{1,0:T(8,128)(2,1)S(1)}, bf16[168,768]{1,0:T(8,128)(2,1)S(1)}, u32[]{:S(2)}, u32[]{:S(2)}) %collective-permute-start.16) | collective-permute-done | bytes 258080 | tf_op jit(solution)/shard_map/ppermute | solution.py:739
  (205 shorter events, 60.9 us)
Async XLA Ops:
  7.2 239.7 %all-gather.2.cloned.1.call-start = ((), (), s32[]{:S(2)}) async-start(), calls=%async_computation.7 | async-start | bytes 22560768 | tf_op jit(solution)/shard_map/all_gather | solution.py:628
  9.4 11.6 %collective-permute-start.3 = (bf16[48,4096]{1,0:T(8,128)(2,1)S(1)}, bf16[48,4096]{1,0:T(8,128)(2,1)S(1)}, u32[]{:S(2)}, u32[]{:S(2)}) collective-permute-start(bf16[48,4096]{1,0:T(8,128)(2,1)S(1)} %bitcast_dynamic-update-slice_fusion), channel_id=1, source_target_pairs={{0,1},{1,0},{2,3},{3,2},{4,5},{5,4},{6,7},{7,6},{8,9},{9,8},{10,11... | collective-permute-start | bytes 1179656 | tf_op jit(solution)/shard_map/ppermute | solution.py:540
  12.2 14.4 %collective-permute-start.2 = (bf16[168,1536]{1,0:T(8,128)(2,1)S(1)}, bf16[168,1536]{1,0:T(8,128)(2,1)S(1)}, u32[]{:S(2)}, u32[]{:S(2)}) collective-permute-start(bf16[168,1536]{1,0:T(8,128)(2,1)S(1)} %pad_maximum_fusion.6), channel_id=1, source_target_pairs={{0,0},{1,2},{2,4},{3,6},{4,8},{5,10},{6,12},{7,14},{8,16},{9,18},{... | collective-permute-start | bytes 1548296 | tf_op jit(solution)/shard_map/ppermute | solution.py:626
  31.9 11.7 %copy-start.7 = (bf16[1,3,64,1536]{3,2,1,0:T(8,128)(2,1)S(1)}, bf16[1,3,64,1536]{3,2,1,0:T(8,128)(2,1)}, u32[]{:S(2)}) copy-start(bf16[1,3,64,1536]{3,2,1,0:T(8,128)(2,1)} %param.12) | copy-start | bytes 1769476
  31.9 77.2 %all-to-all-start = ((bf16[32,48,1408]{2,1,0:T(8,128)(2,1)}), bf16[32,48,1408]{2,1,0:T(8,128)(2,1)}, u32[]{:S(2)}, u32[]{:S(2)}) async-start(bf16[32,48,1408]{2,1,0:T(8,128)(2,1)} %broadcast_in_dim.55), calls=%async_computation | async-start | bytes 8650752 | tf_op jit(solution)/shard_map/all_to_all | solution.py:69
  43.7 2.7 collective-permute-start.1
  111.3 6.0 %copy-start.2 = (bf16[384,1536]{1,0:T(8,128)(2,1)}, bf16[384,1536]{1,0:T(8,128)(2,1)S(1)}, u32[]{:S(2)}) copy-start(bf16[384,1536]{1,0:T(8,128)(2,1)S(1)} %fusion.4.n_ref) | copy-start | bytes 3538948
  118.8 50.1 %all-to-all-start.1 = ((bf16[32,3,96,128]{3,2,1,0:T(8,128)(2,1)}), bf16[32,3,96,128]{3,2,1,0:T(8,128)(2,1)S(1)}, u32[]{:S(2)}, u32[]{:S(2)}) async-start(bf16[32,3,96,128]{3,2,1,0:T(8,128)(2,1)} %bitcast.67), calls=%async_computation.1 | async-start | bytes 4718592 | tf_op jit(solution)/shard_map/all_to_all | solution.py:69
  130.8 383.3 %reduce-scatter.2.cloned.1.call-start = ((), (), s32[]{:S(2)}) async-start(), calls=%async_computation.8 | async-start | bytes 22560768 | tf_op jit(solution)/shard_map/reduce_scatter | solution.py:714
  132.7 2.7 collective-permute-start
  252.4 3.0 collective-permute-start.4
  253.1 4.8 collective-permute-start.6
  257.4 2.1 collective-permute-start.5
  289.8 2.1 collective-permute-start.8
  290.3 2.5 collective-permute-start.7
  295.8 2.0 collective-permute-start.9
  405.7 6.0 %copy-start.10 = (f32[384,1536]{1,0:T(8,128)}, f32[384,1536]{1,0:T(8,128)S(1)}, u32[]{:S(2)}) copy-start(f32[384,1536]{1,0:T(8,128)S(1)} %fusion) | copy-start | bytes 7077892
  405.7 5.3 copy-start.8
  405.8 5.3 collective-permute-start.10
  416.1 70.4 %all-to-all-start.5 = ((bf16[32,48,1408]{2,1,0:T(8,128)(2,1)}), bf16[32,48,1408]{2,1,0:T(8,128)(2,1)}, u32[]{:S(2)}, u32[]{:S(2)}) async-start(bf16[32,48,1408]{2,1,0:T(8,128)(2,1)} %bitcast.74), calls=%async_computation.5 | async-start | bytes 8650752 | tf_op jit(solution)/shard_map/all_to_all | solution.py:69
  486.5 9.5 %copy-start.9 = (f32[192,1536]{1,0:T(8,128)S(1)}, f32[192,1536]{1,0:T(8,128)}, u32[]{:S(2)}) copy-start(f32[192,1536]{1,0:T(8,128)} %get-tuple-element.48) | copy-start | bytes 3538948
  489.5 4.3 collective-permute-start.11
  493.8 4.7 collective-permute-start.12
  515.5 15.5 %collective-permute-start.15 = (bf16[168,768]{1,0:T(8,128)(2,1)S(1)}, bf16[168,768]{1,0:T(8,128)(2,1)S(1)}, u32[]{:S(2)}, u32[]{:S(2)}) collective-permute-start(bf16[168,768]{1,0:T(8,128)(2,1)S(1)} %get-tuple-element.65), channel_id=1, source_target_pairs={{0,65},{1,64},{64,1},{65,0},{2,67},{3,66},{66,3},{67,2},{4,69},{5,... | collective-permute-start | bytes 774152 | tf_op jit(solution)/shard_map/ppermute | solution.py:586
  518.0 13.0 %collective-permute-start.14 = (bf16[168,768]{1,0:T(8,128)(2,1)S(1)}, bf16[168,768]{1,0:T(8,128)(2,1)S(1)}, u32[]{:S(2)}, u32[]{:S(2)}) collective-permute-start(bf16[168,768]{1,0:T(8,128)(2,1)S(1)} %get-tuple-element.65), channel_id=1, source_target_pairs={{0,1},{1,0},{2,3},{3,2},{4,5},{5,4},{6,7},{7,6},{8,9},{9,8},{10,11... | collective-permute-start | bytes 774152 | tf_op jit(solution)/shard_map/ppermute | solution.py:540
  518.5 11.3 %collective-permute-start.13 = (bf16[168,768]{1,0:T(8,128)(2,1)S(1)}, bf16[168,768]{1,0:T(8,128)(2,1)S(1)}, u32[]{:S(2)}, u32[]{:S(2)}) collective-permute-start(bf16[168,768]{1,0:T(8,128)(2,1)S(1)} %get-tuple-element.64), channel_id=1, source_target_pairs={{0,64},{64,0},{1,65},{65,1},{2,66},{66,2},{3,67},{67,3},{4,68},{68... | collective-permute-start | bytes 774152 | tf_op jit(solution)/shard_map/ppermute | solution.py:540
  518.9 39.4 %collective-permute-start.20 = (bf16[48,4096]{1,0:T(8,128)(2,1)S(1)}, bf16[48,4096]{1,0:T(8,128)(2,1)S(1)}, u32[]{:S(2)}, u32[]{:S(2)}) collective-permute-start(bf16[48,4096]{1,0:T(8,128)(2,1)S(1)} %get-tuple-element.59), channel_id=1, source_target_pairs={{0,65},{1,64},{64,1},{65,0},{2,67},{3,66},{66,3},{67,2},{4,69},{5,... | collective-permute-start | bytes 1179656 | tf_op jit(solution)/shard_map/ppermute | solution.py:586
  521.3 36.9 %collective-permute-start.19 = (bf16[48,4096]{1,0:T(8,128)(2,1)S(1)}, bf16[48,4096]{1,0:T(8,128)(2,1)S(1)}, u32[]{:S(2)}, u32[]{:S(2)}) collective-permute-start(bf16[48,4096]{1,0:T(8,128)(2,1)S(1)} %get-tuple-element.59), channel_id=1, source_target_pairs={{0,1},{1,0},{2,3},{3,2},{4,5},{5,4},{6,7},{7,6},{8,9},{9,8},{10,11... | collective-permute-start | bytes 1179656 | tf_op jit(solution)/shard_map/ppermute | solution.py:540
  529.8 28.4 %collective-permute-start.18 = (bf16[48,4096]{1,0:T(8,128)(2,1)S(1)}, bf16[48,4096]{1,0:T(8,128)(2,1)S(1)}, u32[]{:S(2)}, u32[]{:S(2)}) collective-permute-start(bf16[48,4096]{1,0:T(8,128)(2,1)S(1)} %get-tuple-element.58), channel_id=1, source_target_pairs={{0,64},{64,0},{1,65},{65,1},{2,66},{66,2},{3,67},{67,3},{4,68},{68... | collective-permute-start | bytes 1179656 | tf_op jit(solution)/shard_map/ppermute | solution.py:540
  531.1 27.1 %collective-permute-start.16 = (bf16[168,768]{1,0:T(8,128)(2,1)S(1)}, bf16[168,768]{1,0:T(8,128)(2,1)S(1)}, u32[]{:S(2)}, u32[]{:S(2)}) collective-permute-start(bf16[168,768]{1,0:T(8,128)(2,1)S(1)} %add_convert_fusion.2), channel_id=1, source_target_pairs={{0,0},{2,1},{4,2},{6,3},{8,4},{10,5},{12,6},{14,7},{16,8},{18,9},{... | collective-permute-start | bytes 774152 | tf_op jit(solution)/shard_map/ppermute | solution.py:739
  558.2 1.5 collective-permute-start.17
  558.7 2.8 collective-permute-start.21
  (18 other events, 29.3 us)
Sparse Core Ops, SparseCore 0:
  28.2 218.6 all-gather.1
  302.9 211.1 reduce-scatter.1

commit v9 on v8

--- a/solution.py
+++ b/solution.py
@@ -33,7 +33,7 @@
 GATE_AT = D + D // 3
 UP_AT = GATE_AT + PAD_FF
 OUT_AT = UP_AT + PAD_FF
-FF_TILE = 256
+FF_TILE = 512
 FF_TILES = PAD_FF // FF_TILE
 FF_ROWS = 96 * FF_TILE // UNIT_FF
 CHUNK = SPAN // PARTS

time: 579 us -> 579 us (level)
  no operation moved by 1% of the time
where the time goes in v9:
time: 579 us; the launch traced here: 572 us
  waiting for transfers between devices  246 us (42%)
  Pallas kernels  95.5 us (16%)
  blocking collectives  94.6 us (16%)
  starting transfers between devices  67.1 us (12%)
  other arithmetic  29.5 us (5%)
  local copies, waits for them, and re-layouts  19.7 us (3%)
  between operations  15.3 us (3%)
    all_to_all x3, waiting for transfers between devices, exchange(): return lax.all_to_all(values, SHARD, 0, 0, tiled=True)  150 us
    all_to_all x3, blocking collectives, exchange(): return lax.all_to_all(values, SHARD, 0, 0, tiled=True)  94.6 us
    all_to_all x3, starting transfers between devices, exchange(): return lax.all_to_all(values, SHARD, 0, 0, tiled=True)  33.3 us
    all_gather x1, waiting for transfers between devices, on_device(): lax.all_gather(jnp.concatenate([rows_in[48:144], fold(jnp.pad(rows_in[144...  32.1 us
    pallas_call x1, Pallas kernels, feed_forward(): pl.pallas_call(ffn_kernel, grid=(FF_TILES,), in_specs=[whole_spec(BOTH, D...  30.2 us
    pallas_call x1, Pallas kernels, attend_bwd(): pl.pallas_call(bwd_kernel, grid=(MB,), in_specs=[SMEM, SMEM, UNIT_SPEC, C...  26.8 us
    ppermute x1, waiting for transfers between devices, on_device(): lax.ppermute(rows_x, ('c',) + SHARD, [(b, a) for a, b in piece_perm()])  19.6 us
    pallas_call x1, Pallas kernels, attend_fwd(): pl.pallas_call(fwd_kernel, grid=(MB,), in_specs=[SMEM, SMEM, UNIT_SPEC, C...  18.9 us
  transfers between devices with their start and end apart: 27, of which 19 were waited for; matrix products, arithmetic and copies ran while one was open for 6% of the time, Pallas kernels for 10%

profile of v9, /device:TPU:49, one launch (start us, length us, event | category | flops | bytes accessed | tf_op | source)
XLA Modules:
  0.0 571.6 jit_solution(11895250929197508964)
XLA Ops:
  9.4 2.8 collective-permute-start.3
  12.2 5.2 collective-permute-start.2
  17.4 3.5 collective-permute-done.3
  21.0 5.7 collective-permute-done.2
  31.9 11.7 %all-to-all-start = ((bf16[32,48,1408]{2,1,0:T(8,128)(2,1)}), bf16[32,48,1408]{2,1,0:T(8,128)(2,1)}, u32[]{:S(2)}, u32[]{:S(2)}) async-start(bf16[32,48,1408]{2,1,0:T(8,128)(2,1)} %broadcast_in_dim.55), calls=%async_computation | async-start | bytes 8650752 | tf_op jit(solution)/shard_map/all_to_all | solution.py:69
  46.7 62.5 %all-to-all-done = bf16[32,48,1408]{2,1,0:T(8,128)(2,1)} async-done(((bf16[32,48,1408]{2,1,0:T(8,128)(2,1)}), bf16[32,48,1408]{2,1,0:T(8,128)(2,1)}, u32[]{:S(2)}, u32[]{:S(2)}) %all-to-all-start) | async-done | bytes 4325408 | tf_op jit(solution)/shard_map/all_to_all | solution.py:69
  111.3 6.0 %project.1 = bf16[4,2,4,3,96,128]{5,4,3,2,1,0:T(8,128)(2,1)S(1)} custom-call(bf16[384,1536]{1,0:T(8,128)(2,1)S(1)} %fusion.4.n_ref, bf16[1536,1408]{1,0:T(8,128)(2,1)} %bitcast.7.w_ref, f32[4,64,128]{2,1,0:T(8,128)S(1)} %pad_maximum_fusion.9.table_ref), custom_call_target="tpu_custom_call" | custom-call | flops 6000000000 | bytes 1048576 | tf_op jit(solution)/shard_map/project/pallas_call | solution.py:324
  118.8 12.0 %all-to-all-start.1 = ((bf16[32,3,96,128]{3,2,1,0:T(8,128)(2,1)}), bf16[32,3,96,128]{3,2,1,0:T(8,128)(2,1)S(1)}, u32[]{:S(2)}, u32[]{:S(2)}) async-start(bf16[32,3,96,128]{3,2,1,0:T(8,128)(2,1)} %bitcast.67), calls=%async_computation.1 | async-start | bytes 4718592 | tf_op jit(solution)/shard_map/all_to_all | solution.py:69
  135.4 5.8 %convert_reduce_fusion = s32[3,2048]{1,0:T(4,128)S(1)} fusion(f32[3,2048]{1,0:T(4,128)S(1)} %select_convert_fusion), kind=kLoop, calls=%fused_computation | loop fusion | flops 37742592 | bytes 49152 | tf_op jit(solution)/shard_map/reduce_sum | solution.py:667
  142.0 26.9 %all-to-all-done.1.u_ref = bf16[32,3,96,128]{3,2,1,0:T(8,128)(2,1)S(1)} async-done(((bf16[32,3,96,128]{3,2,1,0:T(8,128)(2,1)}), bf16[32,3,96,128]{3,2,1,0:T(8,128)(2,1)S(1)}, u32[]{:S(2)}, u32[]{:S(2)}) %all-to-all-start.1) | async-done | bytes 2359328 | tf_op jit(solution)/shard_map/all_to_all | solution.py:69
  171.2 18.9 %attend_forward.1 = (bf16[32,3,32,128]{3,2,1,0:T(8,128)(2,1)S(1)}, f32[3,8,192,128]{3,2,1,0:T(8,128)S(1)}) custom-call(s32[2]{0:T(128)S(1)} %pad_add_fusion.unit_ref, s32[24]{0:T(128)S(1)} %and_select_fusion.first_ref, bf16[32,3,96,128]{3,2,1,0:T(8,128)(2,1)S(1)} %all-to-all-done.1.u_ref, s32[3,8,192,128]{3,2,1,0:T(8,128)} %broadcast_in_dim.61.start_ref), custom_call_target="tpu_custom_call" | custom-call | flops 20000000000 | bytes 1048576 | tf_op jit(solution)/shard_map/attend_forward/pallas_call | solution.py:496
  191.5 23.3 %all_to_all.30 = bf16[32,3,32,128]{3,2,1,0:T(8,128)(2,1)S(1)} all-to-all(bf16[32,3,32,128]{3,2,1,0:T(8,128)(2,1)S(1)} %get-tuple-element.24), channel_id=1, replica_groups=mesh['xl'=2,'c'=2,'z'=4,'y'=4,'xh'=2] {'z','y','xh'}, dimensions={0} | all-to-all | bytes 1572864 | tf_op jit(solution)/shard_map/all_to_all | solution.py:69
  214.8 32.1 %all-gather.2.cloned.1.call-done.w_ref.main_ref.rest_ref.gate_ref.up_ref = bf16[1536,6912]{1,0:T(8,128)(2,1)} async-done(((bf16[96,6912]{1,0:T(8,128)(2,1)}), bf16[1536,6912]{1,0:T(8,128)(2,1)}) %all-gather.2.cloned.1.call-update) | async-done | bytes 21233680 | tf_op jit(solution)/shard_map/all_gather | solution.py:628
  246.9 3.6 out_project.1
  259.6 30.2 %feed_forward.1 = (f32[192,1536]{1,0:T(8,128)S(1)}, bf16[192,1536]{1,0:T(8,128)(2,1)S(1)}, f32[192,1536]{1,0:T(8,128)S(1)}, bf16[192,1536]{1,0:T(8,128)(2,1)S(1)}, bf16[1536,6912]{1,0:T(8,128)(2,1)}) custom-call(bf16[384,1536]{1,0:T(8,128)(2,1)S(1)} %pad_maximum_fusion.2.n_ref, bf16[384,1536]{1,0:T(8,128)(2,1)S(1)} %multiply_convert_fusion.df_ref, ...), custom_call_target="tpu_custom_call" | custom-call | flops 30000001024 | bytes 1048576 | tf_op jit(solution)/shard_map/feed_forward/pallas_call | solution.py:449
  292.7 3.0 multiply_convert_fusion.1
  298.0 4.9 d_out_project.1
  302.9 21.7 %all_to_all.31.do_ref = bf16[32,3,32,128]{3,2,1,0:T(8,128)(2,1)S(1)} all-to-all(bf16[32,3,32,128]{3,2,1,0:T(8,128)(2,1)S(1)} %bitcast.69), channel_id=1, replica_groups=mesh['xl'=2,'c'=2,'z'=4,'y'=4,'xh'=2] {'z','y','xh'}, dimensions={0} | all-to-all | bytes 1572864 | tf_op jit(solution)/shard_map/all_to_all | solution.py:69
  324.6 26.8 %attend_backward.1 = bf16[32,3,96,128]{3,2,1,0:T(8,128)(2,1)S(1)} custom-call(s32[2]{0:T(128)S(1)} %pad_add_fusion.unit_ref, s32[24]{0:T(128)S(1)} %and_select_fusion.first_ref, bf16[32,3,96,128]{3,2,1,0:T(8,128)(2,1)S(1)} %all-to-all-done.1.u_ref, s32[3,8,192,128]{3,2,1,0:T(8,128)} %broadcast_in_dim.61.start_ref, ...), custom_call_target="tpu_custom_call" | custom-call | flops 27000000512 | bytes 1048576 | tf_op jit(solution)/shard_map/attend_backward/pallas_call | solution.py:509
  351.4 49.6 %all_to_all.32 = bf16[32,3,96,128]{3,2,1,0:T(8,128)(2,1)S(1)} all-to-all(bf16[32,3,96,128]{3,2,1,0:T(8,128)(2,1)S(1)} %attend_backward.1), channel_id=1, replica_groups=mesh['xl'=2,'c'=2,'z'=4,'y'=4,'xh'=2] {'z','y','xh'}, dimensions={0} | all-to-all | bytes 4718592 | tf_op jit(solution)/shard_map/all_to_all | solution.py:69
  401.8 3.9 fusion
  405.9 3.3 collective-permute-start.10
  411.6 4.3 gradients.1
  415.8 9.6 %all-to-all-start.5 = ((bf16[32,48,1408]{2,1,0:T(8,128)(2,1)}), bf16[32,48,1408]{2,1,0:T(8,128)(2,1)}, u32[]{:S(2)}, u32[]{:S(2)}) async-start(bf16[32,48,1408]{2,1,0:T(8,128)(2,1)} %bitcast.74), calls=%async_computation.5 | async-start | bytes 8650752 | tf_op jit(solution)/shard_map/all_to_all | solution.py:69
  425.4 60.8 %all-to-all-done.5 = bf16[32,48,1408]{2,1,0:T(8,128)(2,1)} async-done(((bf16[32,48,1408]{2,1,0:T(8,128)(2,1)}), bf16[32,48,1408]{2,1,0:T(8,128)(2,1)}, u32[]{:S(2)}, u32[]{:S(2)}) %all-to-all-start.5) | async-done | bytes 4325408 | tf_op jit(solution)/shard_map/all_to_all | solution.py:69
  486.2 3.0 reduce_sum.82
  489.4 4.2 collective-permute-done.11
  495.8 2.5 fusion.12
  501.0 13.0 %reduce-scatter.2.cloned.1.call-done = bf16[96,6912]{1,0:T(8,128)(2,1)} async-done(((bf16[1536,6912]{1,0:T(8,128)(2,1)}), bf16[96,6912]{1,0:T(8,128)(2,1)}) %reduce-scatter.2.cloned.1.call-update) | async-done | bytes 1327120 | tf_op jit(solution)/shard_map/reduce_scatter | solution.py:714
  521.7 7.9 %collective-permute-done.13 = bf16[168,768]{1,0:T(8,128)(2,1)S(1)} collective-permute-done((bf16[168,768]{1,0:T(8,128)(2,1)S(1)}, bf16[168,768]{1,0:T(8,128)(2,1)S(1)}, u32[]{:S(2)}, u32[]{:S(2)}) %collective-permute-start.13) | collective-permute-done | bytes 258080 | tf_op jit(solution)/shard_map/ppermute | solution.py:540
  530.9 6.8 %collective-permute-start.16 = (bf16[168,768]{1,0:T(8,128)(2,1)S(1)}, bf16[168,768]{1,0:T(8,128)(2,1)S(1)}, u32[]{:S(2)}, u32[]{:S(2)}) collective-permute-start(bf16[168,768]{1,0:T(8,128)(2,1)S(1)} %add_convert_fusion.2), channel_id=1, source_target_pairs={{0,0},{2,1},{4,2},{6,3},{8,4},{10,5},{12,6},{14,7},{16,8},{18,9},{... | collective-permute-start | bytes 774152 | tf_op jit(solution)/shard_map/ppermute | solution.py:739
  538.4 19.6 %collective-permute-done.16 = bf16[168,768]{1,0:T(8,128)(2,1)S(1)} collective-permute-done((bf16[168,768]{1,0:T(8,128)(2,1)S(1)}, bf16[168,768]{1,0:T(8,128)(2,1)S(1)}, u32[]{:S(2)}, u32[]{:S(2)}) %collective-permute-start.16) | collective-permute-done | bytes 258080 | tf_op jit(solution)/shard_map/ppermute | solution.py:739
  (205 shorter events, 61.1 us)
Async XLA Ops:
  7.2 239.7 %all-gather.2.cloned.1.call-start = ((), (), s32[]{:S(2)}) async-start(), calls=%async_computation.7 | async-start | bytes 22560768 | tf_op jit(solution)/shard_map/all_gather | solution.py:628
  9.4 11.6 %collective-permute-start.3 = (bf16[48,4096]{1,0:T(8,128)(2,1)S(1)}, bf16[48,4096]{1,0:T(8,128)(2,1)S(1)}, u32[]{:S(2)}, u32[]{:S(2)}) collective-permute-start(bf16[48,4096]{1,0:T(8,128)(2,1)S(1)} %bitcast_dynamic-update-slice_fusion), channel_id=1, source_target_pairs={{0,1},{1,0},{2,3},{3,2},{4,5},{5,4},{6,7},{7,6},{8,9},{9,8},{10,11... | collective-permute-start | bytes 1179656 | tf_op jit(solution)/shard_map/ppermute | solution.py:540
  12.2 14.4 %collective-permute-start.2 = (bf16[168,1536]{1,0:T(8,128)(2,1)S(1)}, bf16[168,1536]{1,0:T(8,128)(2,1)S(1)}, u32[]{:S(2)}, u32[]{:S(2)}) collective-permute-start(bf16[168,1536]{1,0:T(8,128)(2,1)S(1)} %pad_maximum_fusion.6), channel_id=1, source_target_pairs={{0,0},{1,2},{2,4},{3,6},{4,8},{5,10},{6,12},{7,14},{8,16},{9,18},{... | collective-permute-start | bytes 1548296 | tf_op jit(solution)/shard_map/ppermute | solution.py:626
  31.9 11.7 %copy-start.7 = (bf16[1,3,64,1536]{3,2,1,0:T(8,128)(2,1)S(1)}, bf16[1,3,64,1536]{3,2,1,0:T(8,128)(2,1)}, u32[]{:S(2)}) copy-start(bf16[1,3,64,1536]{3,2,1,0:T(8,128)(2,1)} %param.12) | copy-start | bytes 1769476
  31.9 77.2 %all-to-all-start = ((bf16[32,48,1408]{2,1,0:T(8,128)(2,1)}), bf16[32,48,1408]{2,1,0:T(8,128)(2,1)}, u32[]{:S(2)}, u32[]{:S(2)}) async-start(bf16[32,48,1408]{2,1,0:T(8,128)(2,1)} %broadcast_in_dim.55), calls=%async_computation | async-start | bytes 8650752 | tf_op jit(solution)/shard_map/all_to_all | solution.py:69
  43.7 2.7 collective-permute-start.1
  111.3 6.0 %copy-start.2 = (bf16[384,1536]{1,0:T(8,128)(2,1)}, bf16[384,1536]{1,0:T(8,128)(2,1)S(1)}, u32[]{:S(2)}) copy-start(bf16[384,1536]{1,0:T(8,128)(2,1)S(1)} %fusion.4.n_ref) | copy-start | bytes 3538948
  118.8 50.1 %all-to-all-start.1 = ((bf16[32,3,96,128]{3,2,1,0:T(8,128)(2,1)}), bf16[32,3,96,128]{3,2,1,0:T(8,128)(2,1)S(1)}, u32[]{:S(2)}, u32[]{:S(2)}) async-start(bf16[32,3,96,128]{3,2,1,0:T(8,128)(2,1)} %bitcast.67), calls=%async_computation.1 | async-start | bytes 4718592 | tf_op jit(solution)/shard_map/all_to_all | solution.py:69
  130.8 383.1 %reduce-scatter.2.cloned.1.call-start = ((), (), s32[]{:S(2)}) async-start(), calls=%async_computation.8 | async-start | bytes 22560768 | tf_op jit(solution)/shard_map/reduce_scatter | solution.py:714
  132.7 2.7 collective-permute-start
  252.4 3.0 collective-permute-start.4
  253.1 4.8 collective-permute-start.6
  257.4 2.1 collective-permute-start.5
  289.8 2.1 collective-permute-start.8
  290.2 2.5 collective-permute-start.7
  295.7 2.2 collective-permute-start.9
  405.8 5.7 copy-start.10
  405.8 5.0 copy-start.8
  405.9 5.0 collective-permute-start.10
  415.8 70.4 %all-to-all-start.5 = ((bf16[32,48,1408]{2,1,0:T(8,128)(2,1)}), bf16[32,48,1408]{2,1,0:T(8,128)(2,1)}, u32[]{:S(2)}, u32[]{:S(2)}) async-start(bf16[32,48,1408]{2,1,0:T(8,128)(2,1)} %bitcast.74), calls=%async_computation.5 | async-start | bytes 8650752 | tf_op jit(solution)/shard_map/all_to_all | solution.py:69
  486.2 9.5 %copy-start.9 = (f32[192,1536]{1,0:T(8,128)S(1)}, f32[192,1536]{1,0:T(8,128)}, u32[]{:S(2)}) copy-start(f32[192,1536]{1,0:T(8,128)} %get-tuple-element.48) | copy-start | bytes 3538948
  489.2 4.3 collective-permute-start.11
  493.6 4.7 collective-permute-start.12
  515.2 15.5 %collective-permute-start.15 = (bf16[168,768]{1,0:T(8,128)(2,1)S(1)}, bf16[168,768]{1,0:T(8,128)(2,1)S(1)}, u32[]{:S(2)}, u32[]{:S(2)}) collective-permute-start(bf16[168,768]{1,0:T(8,128)(2,1)S(1)} %get-tuple-element.65), channel_id=1, source_target_pairs={{0,65},{1,64},{64,1},{65,0},{2,67},{3,66},{66,3},{67,2},{4,69},{5,... | collective-permute-start | bytes 774152 | tf_op jit(solution)/shard_map/ppermute | solution.py:586
  517.7 13.0 %collective-permute-start.14 = (bf16[168,768]{1,0:T(8,128)(2,1)S(1)}, bf16[168,768]{1,0:T(8,128)(2,1)S(1)}, u32[]{:S(2)}, u32[]{:S(2)}) collective-permute-start(bf16[168,768]{1,0:T(8,128)(2,1)S(1)} %get-tuple-element.65), channel_id=1, source_target_pairs={{0,1},{1,0},{2,3},{3,2},{4,5},{5,4},{6,7},{7,6},{8,9},{9,8},{10,11... | collective-permute-start | bytes 774152 | tf_op jit(solution)/shard_map/ppermute | solution.py:540
  518.3 11.3 %collective-permute-start.13 = (bf16[168,768]{1,0:T(8,128)(2,1)S(1)}, bf16[168,768]{1,0:T(8,128)(2,1)S(1)}, u32[]{:S(2)}, u32[]{:S(2)}) collective-permute-start(bf16[168,768]{1,0:T(8,128)(2,1)S(1)} %get-tuple-element.64), channel_id=1, source_target_pairs={{0,64},{64,0},{1,65},{65,1},{2,66},{66,2},{3,67},{67,3},{4,68},{68... | collective-permute-start | bytes 774152 | tf_op jit(solution)/shard_map/ppermute | solution.py:540
  518.6 39.4 %collective-permute-start.20 = (bf16[48,4096]{1,0:T(8,128)(2,1)S(1)}, bf16[48,4096]{1,0:T(8,128)(2,1)S(1)}, u32[]{:S(2)}, u32[]{:S(2)}) collective-permute-start(bf16[48,4096]{1,0:T(8,128)(2,1)S(1)} %get-tuple-element.59), channel_id=1, source_target_pairs={{0,65},{1,64},{64,1},{65,0},{2,67},{3,66},{66,3},{67,2},{4,69},{5,... | collective-permute-start | bytes 1179656 | tf_op jit(solution)/shard_map/ppermute | solution.py:586
  521.1 36.9 %collective-permute-start.19 = (bf16[48,4096]{1,0:T(8,128)(2,1)S(1)}, bf16[48,4096]{1,0:T(8,128)(2,1)S(1)}, u32[]{:S(2)}, u32[]{:S(2)}) collective-permute-start(bf16[48,4096]{1,0:T(8,128)(2,1)S(1)} %get-tuple-element.59), channel_id=1, source_target_pairs={{0,1},{1,0},{2,3},{3,2},{4,5},{5,4},{6,7},{7,6},{8,9},{9,8},{10,11... | collective-permute-start | bytes 1179656 | tf_op jit(solution)/shard_map/ppermute | solution.py:540
  529.5 28.5 %collective-permute-start.18 = (bf16[48,4096]{1,0:T(8,128)(2,1)S(1)}, bf16[48,4096]{1,0:T(8,128)(2,1)S(1)}, u32[]{:S(2)}, u32[]{:S(2)}) collective-permute-start(bf16[48,4096]{1,0:T(8,128)(2,1)S(1)} %get-tuple-element.58), channel_id=1, source_target_pairs={{0,64},{64,0},{1,65},{65,1},{2,66},{66,2},{3,67},{67,3},{4,68},{68... | collective-permute-start | bytes 1179656 | tf_op jit(solution)/shard_map/ppermute | solution.py:540
  530.9 27.1 %collective-permute-start.16 = (bf16[168,768]{1,0:T(8,128)(2,1)S(1)}, bf16[168,768]{1,0:T(8,128)(2,1)S(1)}, u32[]{:S(2)}, u32[]{:S(2)}) collective-permute-start(bf16[168,768]{1,0:T(8,128)(2,1)S(1)} %add_convert_fusion.2), channel_id=1, source_target_pairs={{0,0},{2,1},{4,2},{6,3},{8,4},{10,5},{12,6},{14,7},{16,8},{18,9},{... | collective-permute-start | bytes 774152 | tf_op jit(solution)/shard_map/ppermute | solution.py:739
  558.0 1.5 collective-permute-start.17
  558.5 2.8 collective-permute-start.21
  (18 other events, 29.5 us)
Sparse Core Ops, SparseCore 0:
  28.2 218.6 all-gather.1
  303.0 210.8 reduce-scatter.1
